TPU v7x, 32 devices: a whole 2x2x4 slice. The times are simulated.
32 devices in a mesh: prow: 4 (over z), pcol: 8 (over y, x, core).
Axes of the slice: x: 2, y: 2, z: 4, core: 2. Of those that a mesh axis runs over, the one named last changes fastest.
Arguments:
- slab: float32 [256, 50176], P('pcol', 'prow'), may hold values from -6 to 6
- reflectors: float32 [2, 128, 50176], P(None, 'pcol', 'prow'), may hold values from -6 to 6
- factors: float32 [2, 128, 128], P(None, 'pcol'), as said below
Outputs:
- result: float32 [256, 50176], P('pcol', 'prow')
Inputs may be any that keep to these rules, and one draw needn't show every extreme that they name: factors[p] is upper triangular with a positive diagonal.
All inputs are finite; a program needn't handle non-finite values.
Results may differ from a plain program's by a relative error of at most 0.00013.
Values sent between devices are 32-bit elements; how exact they have to be, the bound alone decides.
No kernel may reach another device: no remote copies, remote signals or barrier semaphores. Data moves between devices by JAX's collectives and lax.ppermute only.
A program may use at most 128 MiB of HBM per device.

v0:
```python
import functools

import jax
import jax.numpy as jnp
from jax import lax
from jax.experimental import pallas as pl
from jax.experimental.pallas import tpu as pltpu
from jax.sharding import PartitionSpec as P


UNIT_LIMIT = 2048
TILE_LIMIT = 8192
VMEM_LIMIT = 32 * 1024 * 1024
SMALL_LIMIT = 8 * 1024 * 1024
COST = pl.CostEstimate(flops=1, bytes_accessed=1, transcendentals=0)
PANELS = 2
ROWS = (((1,), (1,)), ((), ()))
PLAIN = (((1,), (0,)), ((), ()))


def divisor(width, limit):
    for unit in (128, 1):
        fits = [t for t in range(unit, min(limit, width) + 1, unit) if width % t == 0]
        if fits:
            return max(fits)
    return width


def split(value):
    high = value.astype(jnp.bfloat16)
    return high, (value - high.astype(jnp.float32)).astype(jnp.bfloat16)


def dot(left, right, dims):
    return lax.dot_general(left, right, dims, preferred_element_type=jnp.float32)


def exact(left, right, dims):
    return lax.dot_general(left, right, dims, precision=lax.Precision.HIGHEST, preferred_element_type=jnp.float32)


def column_tiles(width, limit):
    tile = divisor(width, limit)
    return [pl.ds(begin, tile) for begin in range(0, width, tile)]


def panel_rows(refs, panel, columns):
    return jnp.concatenate([ref[panel, :, columns] for ref in refs], axis=0)


def near_kernel(kept, slab_ref, *refs):
    vector_refs, out_ref, kept_refs = refs[: -1 - kept], refs[-1 - kept], refs[len(refs) - kept :]
    for ref, kept_ref in zip(vector_refs[1:], kept_refs):
        kept_ref[...] = ref[...]
    (rows, width), nb = slab_ref.shape, out_ref.shape[1]
    group = nb // 4
    total = 0
    for columns in column_tiles(width, TILE_LIMIT):
        (fh, fl), (sh, sl) = (split(panel_rows(vector_refs, p, columns)) for p in range(PANELS))
        ch, cl = split(slab_ref[:, columns])
        first = dot(jnp.concatenate([ch, cl], axis=0), fh, ROWS)
        first = first[:rows] + first[rows:] + dot(ch, fl, ROWS)
        high = jnp.concatenate([ch, fh[: 2 * group]], axis=0)
        low = jnp.concatenate([cl, fl[: 2 * group]], axis=0)
        second = dot(jnp.concatenate([high, low], axis=0), sh, ROWS)
        second = second[: high.shape[0]] + second[high.shape[0] :] + dot(high, sl, ROWS)
        total += jnp.concatenate([first, second], axis=0)
    inner, own, via = total[: 2 * rows], total[2 * rows : 2 * rows + group], total[2 * rows + group :]
    inner = jnp.concatenate([inner, jnp.zeros((2 * rows, group), jnp.float32)], axis=1)
    share = jnp.concatenate([own, via[:, 2 * group :]], axis=1)
    out_ref[...] = jnp.concatenate([inner, share], axis=0)


def corner_kernel(slab_ref, *refs):
    vector_refs, out_ref = refs[:-1], refs[-1]
    (rows, width), (part, nb) = slab_ref.shape, out_ref.shape
    total = 0
    for columns in column_tiles(width, TILE_LIMIT):
        vh, vl = split(jnp.concatenate([ref[:, columns] for ref in vector_refs], axis=0))
        ch, cl = split(slab_ref[:, columns])
        found = dot(jnp.concatenate([ch, cl], axis=0), vh, ROWS)
        total += found[:rows] + found[rows:] + dot(ch, vl, ROWS)
    total = jnp.concatenate([total[:, : nb // 4], total[:, nb // 4 :]], axis=0)
    out_ref[...] = jnp.concatenate([total[k * part : (k + 1) * part] for k in range(4)], axis=1)


def turn_kernel(size, *refs):
    factor_refs, out_ref = refs[:-1], refs[-1]
    nb, low = out_ref.shape[1], size // 4
    block = nb // size
    me = lax.axis_index("pcol")
    column = lax.broadcasted_iota(jnp.int32, (nb, nb), 1)
    place = column // block
    role = place // low
    swapped = ((role == 1) | (role == 2)) & (opposite(size) * (me % 2) == 1)
    bits = jnp.where(swapped, 3 - role, role) * low + place % low
    order = lax.broadcasted_iota(jnp.int32, (nb, nb), 0) == (bits ^ me) * block + column % block
    rows = [ref[p] for p in range(PANELS) for ref in factor_refs]
    out_ref[...] = exact(jnp.concatenate(rows, axis=0), order.astype(jnp.float32), PLAIN)


def share_kernel(terms, *refs):
    term_refs, turned_ref, inner_ref, share_ref = refs[:terms], *refs[terms:]
    group = share_ref.shape[0] // (1 + PANELS)
    total = term_refs[0][...]
    for ref in term_refs[1:]:
        total += ref[...]
    inner_ref[...] = total[:-group]
    share_ref[:group] = total[-group:]
    share_ref[group:] = turned_ref[...]


def from_place(value, q, block, lane):
    width = value.shape[1]
    bit = 1
    while bit * block < width:
        if q & bit:
            shift = bit * block
            ahead, behind = pltpu.roll(value, width - shift, 1), pltpu.roll(value, shift, 1)
            value = jnp.where((lane // shift) % 2 == 0, ahead, behind)
        bit *= 2
    return value


def matrices_kernel(*refs):
    share_refs, between_ref, triangle_refs = refs[:4], refs[4], refs[5:]
    nb = between_ref.shape[0]
    group = nb // 4
    lane = lax.broadcasted_iota(jnp.int32, (1, nb), 1)
    triangles = [[] for _ in range(PANELS)]
    for side in range(4):
        held = from_place(share_refs[side][...], side, group, lane)
        other = from_place(share_refs[side ^ 1][:group], side, group, lane)
        far = ((lane // group) ^ side) == 3
        between_ref[side * group : (side + 1) * group] = jnp.where(far, other, held[:group])
        for p in range(PANELS):
            triangles[p].append(held[(1 + p) * group : (2 + p) * group])
    for p in range(PANELS):
        triangle_refs[p][...] = jnp.concatenate(triangles[p], axis=0).T


def update_kernel(pieces, terms, *refs):
    near_ref, term_refs, (between_ref, first_ref, second_ref) = refs[0], refs[1 : 1 + terms], refs[1 + terms : 4 + terms]
    slab_ref, *vector_refs = refs[4 + terms : -3]
    out_ref, after, sems = refs[-3:]
    (rows, width), nb = slab_ref.shape, near_ref.shape[1]
    group = nb // 4

    total = term_refs[0][...]
    for ref in term_refs[1:]:
        total += ref[...]
    total = jnp.concatenate([total[:, k * group : (k + 1) * group] for k in range(4)], axis=0)
    total = near_ref[...] + jnp.concatenate([jnp.zeros((PANELS * rows, nb - group), jnp.float32), total], axis=1)
    scaled = exact(total[:rows], first_ref[...], PLAIN)
    inner = total[rows:] - exact(scaled, between_ref[...], PLAIN)
    later = exact(inner, second_ref[...], PLAIN)
    both = jnp.concatenate(split(jnp.concatenate([scaled, later], axis=1)), axis=0)

    copies = []
    for at, columns in enumerate(column_tiles(width, UNIT_LIMIT)):
        blocks = [vector_refs[ref][:, columns] if p is None else vector_refs[ref][p, :, columns] for ref, p in pieces]
        high, low = split(jnp.concatenate(blocks, axis=0))
        main = dot(both, high, PLAIN)
        rest = dot(both[:rows], low, PLAIN)
        after[:, columns] = slab_ref[:, columns] - (main[:rows] + main[rows:] + rest)
        copies.append(pltpu.make_async_copy(after.at[:, columns], out_ref.at[:, columns], sems.at[at]))
        copies[-1].start()
    for copy in copies:
        copy.wait()


def products(kernel, arrays, *shapes):
    return pl.pallas_call(
        kernel,
        in_specs=[pl.BlockSpec(memory_space=pltpu.VMEM)] * len(arrays),
        out_specs=[pl.BlockSpec(memory_space=pltpu.VMEM)] * len(shapes),
        out_shape=[jax.ShapeDtypeStruct(shape, jnp.float32) for shape in shapes],
        compiler_params=pltpu.CompilerParams(vmem_limit_bytes=VMEM_LIMIT),
        cost_estimate=COST,
    )(*arrays)


def small(kernel, shapes, *arrays):
    return pl.pallas_call(
        kernel,
        out_shape=[jax.ShapeDtypeStruct(shape, jnp.float32) for shape in shapes],
        compiler_params=pltpu.CompilerParams(vmem_limit_bytes=SMALL_LIMIT),
        cost_estimate=COST,
    )(*arrays)


def update(near, terms, matrices, slab, arrays, pieces):
    width = slab.shape[1]
    whole = [near, *terms, *matrices, slab, *arrays]
    return pl.pallas_call(
        functools.partial(update_kernel, pieces, len(terms)),
        in_specs=[pl.BlockSpec(memory_space=pltpu.VMEM)] * len(whole),
        out_specs=pl.BlockSpec(memory_space=pl.ANY),
        out_shape=jax.ShapeDtypeStruct(slab.shape, jnp.float32),
        scratch_shapes=[
            pltpu.VMEM(slab.shape, jnp.float32),
            pltpu.SemaphoreType.DMA((len(column_tiles(width, UNIT_LIMIT)),)),
        ],
        compiler_params=pltpu.CompilerParams(vmem_limit_bytes=VMEM_LIMIT),
        cost_estimate=COST,
    )(*whole)


def opposite(size):
    return int(size > 4)


def exchange(array, partner, size, axis):
    return lax.ppermute(array, axis, [(i, i ^ partner(i)) for i in range(size)])


def summed_terms(value, depth, step):
    terms, reach = [value], 1
    while reach < depth:
        value = sum(terms[1:], terms[0])
        span = min(step, depth // reach)
        terms = [value] + [exchange(value, lambda i, k=k: k * reach, depth, "prow") for k in range(1, span)]
        reach *= span
    return terms


def over_rest(held, low, across):
    bit = 1
    while bit < low:
        for q, array in list(held.items()):
            turned = q // low in (1, 2) and bit == 1
            held[(q ^ (3 * low) if turned else q) | bit] = across(array, lambda i, bit=bit: bit)
        bit *= 2
    return held


def body(sizes, slab, reflectors, factors):
    size, depth = sizes["pcol"], sizes["prow"]
    rows = slab.shape[0]
    block, nb = factors.shape[1:]
    high, low = size // 2, size // 4
    across = functools.partial(exchange, size=size, axis="pcol")
    first = lambda i: high if opposite(size) * (i % 2) else low
    second = lambda i: low if opposite(size) * (i % 2) else high
    both = lambda i: high | low

    by_first, by_second = across(reflectors, first), across(reflectors, second)
    corner = [across(by_second[0], first), across(by_first[1], second)]
    near = over_rest({0: reflectors, low: by_first, high: by_second}, low, across)
    near = [near[q] for q in sorted(near)]
    group = over_rest({0: factors}, low, across)
    (turned,) = small(functools.partial(turn_kernel, size), [(PANELS * nb // 4, nb)], *[group[q] for q in sorted(group)])
    near, turned = lax.optimization_barrier((near, turned))
    (total,) = products(functools.partial(near_kernel, 0), [slab, *near], (2 * rows + nb // 4, nb))
    terms = summed_terms(total, depth, 4)
    terms, corner = lax.optimization_barrier((terms, corner))
    inner, share = small(
        functools.partial(share_kernel, len(terms)), [(2 * rows, nb), ((1 + PANELS) * nb // 4, nb)], *terms, turned
    )
    shares = [share, *(across(share, way) for way in (first, second, both))]
    far = [over_rest({high | low: array}, low, across) for array in corner]
    far = [held[q] for held in far for q in sorted(held)]
    matrices = small(matrices_kernel, [(nb, nb)] * (1 + PANELS), *shares)
    (found,) = products(corner_kernel, [slab, *far], (2 * rows // 4, nb))
    count, part = len(near), len(far) // PANELS
    pieces = [piece for p in range(PANELS) for piece in (*((at, p) for at in range(count)), *((count + p * part + at, None) for at in range(part)))]
    return update(inner, summed_terms(found, depth, 4), matrices, slab, [*near, *far], pieces)


def solution(mesh):
    in_specs = (P("pcol", "prow"), P(None, "pcol", "prow"), P(None, "pcol", None))
    out_specs = P("pcol", "prow")
    return jax.shard_map(functools.partial(body, dict(mesh.shape)), mesh=mesh, in_specs=in_specs, out_specs=out_specs, check_vma=False)
```

profile of v0, /device:TPU:0, one launch (start us, length us, event | category | flops | bytes accessed | tf_op | source)
XLA Modules:
  0.0 77.4 jit_solution(9707702093750224912)
XLA Ops:
  0.0 0.0 copy-start.1
  0.0 0.0 copy-start.2
  0.0 0.0 copy-start
  0.0 3.0 %collective-permute-start.1 = (f32[2,16,12544]{2,1,0:T(8,128)}, f32[2,16,12544]{2,1,0:T(8,128)S(1)}, u32[]{:S(2)}, u32[]{:S(2)}) collective-permute-start(f32[2,16,12544]{2,1,0:T(8,128)} %refs_9_), channel_id=1, source_target_pairs={{0,2},{1,5},{2,0},{3,7},{4,6},{5,1},{6,4},{7,3},{8,10},{9,13},{10,... | collective-permute-start | bytes 4816904 | tf_op jit(solution)/shard_map/ppermute | solution.py:214
  3.0 0.0 collective-permute-start
  3.0 1.5 %collective-permute-start.2 = (f32[2,16,12544]{2,1,0:T(8,128)}, f32[2,16,12544]{2,1,0:T(8,128)S(1)}, u32[]{:S(2)}, u32[]{:S(2)}) collective-permute-start(f32[2,16,12544]{2,1,0:T(8,128)} %refs_9_), channel_id=1, source_target_pairs={{0,4},{1,3},{2,6},{3,1},{4,0},{5,7},{6,2},{7,5},{8,12},{9,11},{10,... | collective-permute-start | bytes 4816904 | tf_op jit(solution)/shard_map/ppermute | solution.py:214
  4.5 0.0 collective-permute-start.5
  4.5 34.2 %collective-permute-done.1.refs_2_.refs_11_ = f32[2,16,12544]{2,1,0:T(8,128)S(1)} collective-permute-done((f32[2,16,12544]{2,1,0:T(8,128)}, f32[2,16,12544]{2,1,0:T(8,128)S(1)}, u32[]{:S(2)}, u32[]{:S(2)}) %collective-permute-start.1) | collective-permute-done | bytes 1605664 | tf_op jit(solution)/shard_map/ppermute | solution.py:214
  38.7 0.1 slice_bitcast_fusion
  38.8 1.6 %collective-permute-start.10 = (f32[16,12544]{1,0:T(8,128)S(1)}, f32[16,12544]{1,0:T(8,128)S(1)}, u32[]{:S(2)}, u32[]{:S(2)}) collective-permute-start(f32[16,12544]{1,0:T(8,128)S(1)} %slice_bitcast_fusion), channel_id=1, source_target_pairs={{0,4},{1,3},{2,6},{3,1},{4,0},{5,7},{6,2},{7,5},{8,12},{9,11},{10,... | collective-permute-start | bytes 2408456 | tf_op jit(solution)/shard_map/ppermute | solution.py:214
  40.4 0.0 collective-permute-start.4
  40.4 0.0 collective-permute-done.2.refs_4_.refs_13_
  40.4 0.5 collective-permute-start.3
  40.9 0.1 slice_bitcast_fusion.1
  41.0 0.0 collective-permute-done.5.refs_1_
  41.0 2.4 %collective-permute-start.9 = (f32[16,12544]{1,0:T(8,128)S(1)}, f32[16,12544]{1,0:T(8,128)S(1)}, u32[]{:S(2)}, u32[]{:S(2)}) collective-permute-start(f32[16,12544]{1,0:T(8,128)S(1)} %slice_bitcast_fusion.1), channel_id=1, source_target_pairs={{0,2},{1,5},{2,0},{3,7},{4,6},{5,1},{6,4},{7,3},{8,10},{9,13},{10,... | collective-permute-start | bytes 2408456 | tf_op jit(solution)/shard_map/ppermute | solution.py:214
  43.4 0.0 copy-done.2
  43.4 0.2 shard_map.37.refs_4_
  43.6 0.0 collective-permute-done.refs_1_.refs_10_
  43.6 0.2 collective-permute-done.4.refs_5_.refs_14_
  43.8 2.3 %collective-permute-done.3.refs_3_.refs_12_ = f32[2,16,12544]{2,1,0:T(8,128)S(1)} collective-permute-done((f32[2,16,12544]{2,1,0:T(8,128)S(1)}, f32[2,16,12544]{2,1,0:T(8,128)S(1)}, u32[]{:S(2)}, u32[]{:S(2)}) %collective-permute-start.3) | collective-permute-done | bytes 1605664 | tf_op jit(solution)/shard_map/ppermute | solution.py:214
  46.1 0.0 copy-done.1
  46.1 0.0 copy-done
  46.1 3.6 %shard_map.38.refs_0_ = f32[96,128]{1,0:T(8,128)S(1)} custom-call(f32[32,12544]{1,0:T(8,128)S(1)} %copy-done, f32[2,16,12544]{2,1,0:T(8,128)S(1)} %copy-done.1, f32[2,16,12544]{2,1,0:T(8,128)S(1)} %collective-permute-done.refs_1_.refs_10_, f32[2,16,12544]{2,1,0:T(8,128)S(1)} %collective-permute-done.1.refs_2_.refs_11_, ...), custom_call_target="tpu_custom_call" | custom-call | flops 1 | bytes 1 | tf_op jit(solution)/shard_map/pallas_call | solution.py:173
  49.7 3.6 %collective-permute-start.8 = (f32[96,128]{1,0:T(8,128)S(1)}, f32[96,128]{1,0:T(8,128)S(1)}, u32[]{:S(2)}, u32[]{:S(2)}) collective-permute-start(f32[96,128]{1,0:T(8,128)S(1)} %shard_map.38.refs_0_), channel_id=1, source_target_pairs={{0,24},{8,16},{16,8},{24,0},{1,25},{9,17},{17,9},{25,1},{2,26},{10... | collective-permute-start | bytes 147464 | tf_op jit(solution)/shard_map/ppermute | solution.py:214
  53.3 0.0 collective-permute-start.7
  53.4 0.8 %collective-permute-start.6 = (f32[96,128]{1,0:T(8,128)S(1)}, f32[96,128]{1,0:T(8,128)S(1)}, u32[]{:S(2)}, u32[]{:S(2)}) collective-permute-start(f32[96,128]{1,0:T(8,128)S(1)} %shard_map.38.refs_0_), channel_id=1, source_target_pairs={{0,8},{8,0},{16,24},{24,16},{1,9},{9,1},{17,25},{25,17},{2,10},{10... | collective-permute-start | bytes 147464 | tf_op jit(solution)/shard_map/ppermute | solution.py:214
  54.1 4.4 %collective-permute-done.10.refs_2_.refs_17_ = f32[16,12544]{1,0:T(8,128)S(1)} collective-permute-done((f32[16,12544]{1,0:T(8,128)S(1)}, f32[16,12544]{1,0:T(8,128)S(1)}, u32[]{:S(2)}, u32[]{:S(2)}) %collective-permute-start.10) | collective-permute-done | bytes 802848 | tf_op jit(solution)/shard_map/ppermute | solution.py:214
  58.5 0.0 collective-permute-done.9.refs_0_.refs_15_
  58.5 0.0 collective-permute-done.8.refs_3_
  58.5 0.0 collective-permute-done.7.refs_2_
  58.5 0.0 collective-permute-done.6.refs_1_
  58.5 1.0 %collective-permute-start.11 = (f32[16,12544]{1,0:T(8,128)S(1)}, f32[16,12544]{1,0:T(8,128)S(1)}, u32[]{:S(2)}, u32[]{:S(2)}) collective-permute-start(f32[16,12544]{1,0:T(8,128)S(1)} %collective-permute-done.9.refs_0_.refs_15_), channel_id=1, source_target_pairs={{0,1},{1,0},{2,3},{3,2},{4,5},{5,4},{6,7},{7,6},{8,9},{9,8},{10,11... | collective-permute-start | bytes 2408456 | tf_op jit(solution)/shard_map/ppermute | solution.py:214
  59.5 0.1 collective-permute-start.12
  59.6 3.9 %collective-permute-start.18 = (f32[96,128]{1,0:T(8,128)S(1)}, f32[96,128]{1,0:T(8,128)S(1)}, u32[]{:S(2)}, u32[]{:S(2)}) collective-permute-start(f32[96,128]{1,0:T(8,128)S(1)} %get-tuple-element.37.refs_0_), channel_id=1, source_target_pairs={{0,6},{1,7},{2,4},{3,5},{4,2},{5,3},{6,0},{7,1},{8,14},{9,15},{10,... | collective-permute-start | bytes 147464 | tf_op jit(solution)/shard_map/ppermute | solution.py:214
  63.5 0.0 collective-permute-start.17
  63.5 0.6 collective-permute-start.16
  64.1 0.0 collective-permute-done.11.refs_1_.refs_16_
  64.1 0.0 collective-permute-done.12.refs_3_.refs_18_
  64.1 1.1 %shard_map.40.refs_1_ = f32[16,128]{1,0:T(8,128)S(1)} custom-call(f32[32,12544]{1,0:T(8,128)S(1)} %copy-done, f32[16,12544]{1,0:T(8,128)S(1)} %collective-permute-done.9.refs_0_.refs_15_, f32[16,12544]{1,0:T(8,128)S(1)} %collective-permute-done.11.refs_1_.refs_16_, f32[16,12544]{1,0:T(8,128)S(1)} %collective-permute-done.10.refs_2_.refs_17_, ...), custom_call_target="tpu_custom_call" | custom-call | flops 1 | bytes 1 | tf_op jit(solution)/shard_map/pallas_call | solution.py:173
  65.3 3.6 %collective-permute-start.15 = (f32[16,128]{1,0:T(8,128)S(1)}, f32[16,128]{1,0:T(8,128)S(1)}, u32[]{:S(2)}, u32[]{:S(2)}) collective-permute-start(f32[16,128]{1,0:T(8,128)S(1)} %shard_map.40.refs_1_), channel_id=1, source_target_pairs={{0,24},{8,16},{16,8},{24,0},{1,25},{9,17},{17,9},{25,1},{2,26},{10... | collective-permute-start | bytes 24584 | tf_op jit(solution)/shard_map/ppermute | solution.py:214
  68.9 0.0 collective-permute-start.14
  68.9 0.0 collective-permute-done.18.refs_3_
  68.9 0.8 %collective-permute-start.13 = (f32[16,128]{1,0:T(8,128)S(1)}, f32[16,128]{1,0:T(8,128)S(1)}, u32[]{:S(2)}, u32[]{:S(2)}) collective-permute-start(f32[16,128]{1,0:T(8,128)S(1)} %shard_map.40.refs_1_), channel_id=1, source_target_pairs={{0,8},{8,0},{16,24},{24,16},{1,9},{9,1},{17,25},{25,17},{2,10},{10... | collective-permute-start | bytes 24584 | tf_op jit(solution)/shard_map/ppermute | solution.py:214
  69.7 0.0 collective-permute-done.17.refs_2_
  69.7 0.0 collective-permute-done.16.refs_1_
  69.7 0.3 shard_map.41
  70.0 0.9 %collective-permute-done.15.refs_4_ = f32[16,128]{1,0:T(8,128)S(1)} collective-permute-done((f32[16,128]{1,0:T(8,128)S(1)}, f32[16,128]{1,0:T(8,128)S(1)}, u32[]{:S(2)}, u32[]{:S(2)}) %collective-permute-start.15) | collective-permute-done | bytes 8224 | tf_op jit(solution)/shard_map/ppermute | solution.py:214
  70.9 2.6 %collective-permute-done.14.refs_3_ = f32[16,128]{1,0:T(8,128)S(1)} collective-permute-done((f32[16,128]{1,0:T(8,128)S(1)}, f32[16,128]{1,0:T(8,128)S(1)}, u32[]{:S(2)}, u32[]{:S(2)}) %collective-permute-start.14) | collective-permute-done | bytes 8224 | tf_op jit(solution)/shard_map/ppermute | solution.py:214
  73.4 0.0 collective-permute-done.13.refs_2_
  73.4 3.9 %shard_map.42 = f32[32,12544]{1,0:T(8,128)} custom-call(f32[64,128]{1,0:T(8,128)S(1)} %get-tuple-element.34.refs_0_, f32[16,128]{1,0:T(8,128)S(1)} %shard_map.40.refs_1_, f32[16,128]{1,0:T(8,128)S(1)} %collective-permute-done.13.refs_2_, f32[16,128]{1,0:T(8,128)S(1)} %collective-permute-done.14.refs_3_, f32[16,128]{1,0:T(8,128)S(1)} %collective-permute-done.15.refs_4_, ...), custom_call_target="tpu_custom_call" | custom-call | flops 1 | bytes 1 | tf_op jit(solution)/shard_map/pallas_call | solution.py:195
  (1 shorter events, 0.0 us)
Async XLA Ops:
  0.0 46.1 %copy-start.1 = (f32[2,16,12544]{2,1,0:T(8,128)S(1)}, f32[2,16,12544]{2,1,0:T(8,128)}, u32[]{:S(2)}) copy-start(f32[2,16,12544]{2,1,0:T(8,128)} %refs_9_) | copy-start | bytes 4816900
  0.0 43.4 %copy-start.2 = (f32[2,16,128]{2,1,0:T(8,128)S(1)}, f32[2,16,128]{2,1,0:T(8,128)}, u32[]{:S(2)}) copy-start(f32[2,16,128]{2,1,0:T(8,128)} %refs_0_.1) | copy-start | bytes 49156
  0.0 46.1 %copy-start = (f32[32,12544]{1,0:T(8,128)S(1)}, f32[32,12544]{1,0:T(8,128)}, u32[]{:S(2)}) copy-start(f32[32,12544]{1,0:T(8,128)} %refs_8_.1) | copy-start | bytes 4816900
  0.0 38.7 %collective-permute-start.1 = (f32[2,16,12544]{2,1,0:T(8,128)}, f32[2,16,12544]{2,1,0:T(8,128)S(1)}, u32[]{:S(2)}, u32[]{:S(2)}) collective-permute-start(f32[2,16,12544]{2,1,0:T(8,128)} %refs_9_), channel_id=1, source_target_pairs={{0,2},{1,5},{2,0},{3,7},{4,6},{5,1},{6,4},{7,3},{8,10},{9,13},{10,... | collective-permute-start | bytes 4816904 | tf_op jit(solution)/shard_map/ppermute | solution.py:214
  3.0 40.6 %collective-permute-start = (f32[2,16,12544]{2,1,0:T(8,128)}, f32[2,16,12544]{2,1,0:T(8,128)S(1)}, u32[]{:S(2)}, u32[]{:S(2)}) collective-permute-start(f32[2,16,12544]{2,1,0:T(8,128)} %refs_9_), channel_id=1, source_target_pairs={{0,1},{1,0},{2,3},{3,2},{4,5},{5,4},{6,7},{7,6},{8,9},{9,8},{10,11... | collective-permute-start | bytes 4816904 | tf_op jit(solution)/shard_map/ppermute | solution.py:214
  3.0 37.4 %collective-permute-start.2 = (f32[2,16,12544]{2,1,0:T(8,128)}, f32[2,16,12544]{2,1,0:T(8,128)S(1)}, u32[]{:S(2)}, u32[]{:S(2)}) collective-permute-start(f32[2,16,12544]{2,1,0:T(8,128)} %refs_9_), channel_id=1, source_target_pairs={{0,4},{1,3},{2,6},{3,1},{4,0},{5,7},{6,2},{7,5},{8,12},{9,11},{10,... | collective-permute-start | bytes 4816904 | tf_op jit(solution)/shard_map/ppermute | solution.py:214
  4.5 36.4 %collective-permute-start.5 = (f32[2,16,128]{2,1,0:T(8,128)}, f32[2,16,128]{2,1,0:T(8,128)S(1)}, u32[]{:S(2)}, u32[]{:S(2)}) collective-permute-start(f32[2,16,128]{2,1,0:T(8,128)} %refs_0_.1), channel_id=1, source_target_pairs={{0,1},{1,0},{2,3},{3,2},{4,5},{5,4},{6,7},{7,6},{8,9},{9,8},{10,11... | collective-permute-start | bytes 49160 | tf_op jit(solution)/shard_map/ppermute | solution.py:214
  38.8 19.7 %collective-permute-start.10 = (f32[16,12544]{1,0:T(8,128)S(1)}, f32[16,12544]{1,0:T(8,128)S(1)}, u32[]{:S(2)}, u32[]{:S(2)}) collective-permute-start(f32[16,12544]{1,0:T(8,128)S(1)} %slice_bitcast_fusion), channel_id=1, source_target_pairs={{0,4},{1,3},{2,6},{3,1},{4,0},{5,7},{6,2},{7,5},{8,12},{9,11},{10,... | collective-permute-start | bytes 2408456 | tf_op jit(solution)/shard_map/ppermute | solution.py:214
  40.4 3.5 %collective-permute-start.4 = (f32[2,16,12544]{2,1,0:T(8,128)S(1)}, f32[2,16,12544]{2,1,0:T(8,128)S(1)}, u32[]{:S(2)}, u32[]{:S(2)}) collective-permute-start(f32[2,16,12544]{2,1,0:T(8,128)S(1)} %collective-permute-done.1.refs_2_.refs_11_), channel_id=1, source_target_pairs={{0,1},{1,0},{2,3},{3,2},{4,5},{5,4},{6,7},{7,6},{8,9},{9,8},{10,11... | collective-permute-start | bytes 4816904 | tf_op jit(solution)/shard_map/ppermute | solution.py:214
  40.4 5.7 %collective-permute-start.3 = (f32[2,16,12544]{2,1,0:T(8,128)S(1)}, f32[2,16,12544]{2,1,0:T(8,128)S(1)}, u32[]{:S(2)}, u32[]{:S(2)}) collective-permute-start(f32[2,16,12544]{2,1,0:T(8,128)S(1)} %collective-permute-done.2.refs_4_.refs_13_), channel_id=1, source_target_pairs={{0,1},{1,0},{2,3},{3,2},{4,5},{5,4},{6,7},{7,6},{8,9},{9,8},{10,11... | collective-permute-start | bytes 4816904 | tf_op jit(solution)/shard_map/ppermute | solution.py:214
  41.0 17.5 %collective-permute-start.9 = (f32[16,12544]{1,0:T(8,128)S(1)}, f32[16,12544]{1,0:T(8,128)S(1)}, u32[]{:S(2)}, u32[]{:S(2)}) collective-permute-start(f32[16,12544]{1,0:T(8,128)S(1)} %slice_bitcast_fusion.1), channel_id=1, source_target_pairs={{0,2},{1,5},{2,0},{3,7},{4,6},{5,1},{6,4},{7,3},{8,10},{9,13},{10,... | collective-permute-start | bytes 2408456 | tf_op jit(solution)/shard_map/ppermute | solution.py:214
  49.7 8.8 %collective-permute-start.8 = (f32[96,128]{1,0:T(8,128)S(1)}, f32[96,128]{1,0:T(8,128)S(1)}, u32[]{:S(2)}, u32[]{:S(2)}) collective-permute-start(f32[96,128]{1,0:T(8,128)S(1)} %shard_map.38.refs_0_), channel_id=1, source_target_pairs={{0,24},{8,16},{16,8},{24,0},{1,25},{9,17},{17,9},{25,1},{2,26},{10... | collective-permute-start | bytes 147464 | tf_op jit(solution)/shard_map/ppermute | solution.py:214
  53.3 5.2 %collective-permute-start.7 = (f32[96,128]{1,0:T(8,128)S(1)}, f32[96,128]{1,0:T(8,128)S(1)}, u32[]{:S(2)}, u32[]{:S(2)}) collective-permute-start(f32[96,128]{1,0:T(8,128)S(1)} %shard_map.38.refs_0_), channel_id=1, source_target_pairs={{0,16},{8,24},{16,0},{24,8},{1,17},{9,25},{17,1},{25,9},{2,18},{10... | collective-permute-start | bytes 147464 | tf_op jit(solution)/shard_map/ppermute | solution.py:214
  53.4 5.2 %collective-permute-start.6 = (f32[96,128]{1,0:T(8,128)S(1)}, f32[96,128]{1,0:T(8,128)S(1)}, u32[]{:S(2)}, u32[]{:S(2)}) collective-permute-start(f32[96,128]{1,0:T(8,128)S(1)} %shard_map.38.refs_0_), channel_id=1, source_target_pairs={{0,8},{8,0},{16,24},{24,16},{1,9},{9,1},{17,25},{25,17},{2,10},{10... | collective-permute-start | bytes 147464 | tf_op jit(solution)/shard_map/ppermute | solution.py:214
  58.5 5.6 %collective-permute-start.11 = (f32[16,12544]{1,0:T(8,128)S(1)}, f32[16,12544]{1,0:T(8,128)S(1)}, u32[]{:S(2)}, u32[]{:S(2)}) collective-permute-start(f32[16,12544]{1,0:T(8,128)S(1)} %collective-permute-done.9.refs_0_.refs_15_), channel_id=1, source_target_pairs={{0,1},{1,0},{2,3},{3,2},{4,5},{5,4},{6,7},{7,6},{8,9},{9,8},{10,11... | collective-permute-start | bytes 2408456 | tf_op jit(solution)/shard_map/ppermute | solution.py:214
  59.5 4.6 %collective-permute-start.12 = (f32[16,12544]{1,0:T(8,128)S(1)}, f32[16,12544]{1,0:T(8,128)S(1)}, u32[]{:S(2)}, u32[]{:S(2)}) collective-permute-start(f32[16,12544]{1,0:T(8,128)S(1)} %collective-permute-done.10.refs_2_.refs_17_), channel_id=1, source_target_pairs={{0,1},{1,0},{2,3},{3,2},{4,5},{5,4},{6,7},{7,6},{8,9},{9,8},{10,11... | collective-permute-start | bytes 2408456 | tf_op jit(solution)/shard_map/ppermute | solution.py:214
  59.6 9.3 %collective-permute-start.18 = (f32[96,128]{1,0:T(8,128)S(1)}, f32[96,128]{1,0:T(8,128)S(1)}, u32[]{:S(2)}, u32[]{:S(2)}) collective-permute-start(f32[96,128]{1,0:T(8,128)S(1)} %get-tuple-element.37.refs_0_), channel_id=1, source_target_pairs={{0,6},{1,7},{2,4},{3,5},{4,2},{5,3},{6,0},{7,1},{8,14},{9,15},{10,... | collective-permute-start | bytes 147464 | tf_op jit(solution)/shard_map/ppermute | solution.py:214
  63.5 6.2 %collective-permute-start.17 = (f32[96,128]{1,0:T(8,128)S(1)}, f32[96,128]{1,0:T(8,128)S(1)}, u32[]{:S(2)}, u32[]{:S(2)}) collective-permute-start(f32[96,128]{1,0:T(8,128)S(1)} %get-tuple-element.37.refs_0_), channel_id=1, source_target_pairs={{0,4},{1,3},{2,6},{3,1},{4,0},{5,7},{6,2},{7,5},{8,12},{9,11},{10,... | collective-permute-start | bytes 147464 | tf_op jit(solution)/shard_map/ppermute | solution.py:214
  63.5 6.2 %collective-permute-start.16 = (f32[96,128]{1,0:T(8,128)S(1)}, f32[96,128]{1,0:T(8,128)S(1)}, u32[]{:S(2)}, u32[]{:S(2)}) collective-permute-start(f32[96,128]{1,0:T(8,128)S(1)} %get-tuple-element.37.refs_0_), channel_id=1, source_target_pairs={{0,2},{1,5},{2,0},{3,7},{4,6},{5,1},{6,4},{7,3},{8,10},{9,13},{10,... | collective-permute-start | bytes 147464 | tf_op jit(solution)/shard_map/ppermute | solution.py:214
  65.3 5.6 %collective-permute-start.15 = (f32[16,128]{1,0:T(8,128)S(1)}, f32[16,128]{1,0:T(8,128)S(1)}, u32[]{:S(2)}, u32[]{:S(2)}) collective-permute-start(f32[16,128]{1,0:T(8,128)S(1)} %shard_map.40.refs_1_), channel_id=1, source_target_pairs={{0,24},{8,16},{16,8},{24,0},{1,25},{9,17},{17,9},{25,1},{2,26},{10... | collective-permute-start | bytes 24584 | tf_op jit(solution)/shard_map/ppermute | solution.py:214
  68.9 4.5 %collective-permute-start.14 = (f32[16,128]{1,0:T(8,128)S(1)}, f32[16,128]{1,0:T(8,128)S(1)}, u32[]{:S(2)}, u32[]{:S(2)}) collective-permute-start(f32[16,128]{1,0:T(8,128)S(1)} %shard_map.40.refs_1_), channel_id=1, source_target_pairs={{0,16},{8,24},{16,0},{24,8},{1,17},{9,25},{17,1},{25,9},{2,18},{10... | collective-permute-start | bytes 24584 | tf_op jit(solution)/shard_map/ppermute | solution.py:214
  68.9 4.5 %collective-permute-start.13 = (f32[16,128]{1,0:T(8,128)S(1)}, f32[16,128]{1,0:T(8,128)S(1)}, u32[]{:S(2)}, u32[]{:S(2)}) collective-permute-start(f32[16,128]{1,0:T(8,128)S(1)} %shard_map.40.refs_1_), channel_id=1, source_target_pairs={{0,8},{8,0},{16,24},{24,16},{1,9},{9,1},{17,25},{25,17},{2,10},{10... | collective-permute-start | bytes 24584 | tf_op jit(solution)/shard_map/ppermute | solution.py:214
where the time goes:
time: 77.5 us; the launch traced here: 77.4 us
  waiting for transfers between devices  44.5 us (57%)
  starting transfers between devices  23.5 us (30%)
  Pallas kernels  9.17 us (12%)
    ppermute x19, waiting for transfers between devices, exchange(): return lax.ppermute(array, axis, [(i, i ^ partner(i)) for i in range(size)])  44.5 us
    ppermute x19, starting transfers between devices, exchange(): return lax.ppermute(array, axis, [(i, i ^ partner(i)) for i in range(size)])  23.5 us
    pallas_call x2, Pallas kernels, products(): pl.pallas_call(kernel, in_specs=[pl.BlockSpec(memory_space=pltpu.VMEM)] *...  4.71 us
    pallas_call x1, Pallas kernels, update(): pl.pallas_call(functools.partial(update_kernel, pieces, len(terms)), in_s...  3.94 us
  transfers between devices with their start and end apart: 19, of which 6 were waited for; matrix products, arithmetic and copies ran while one was open for 0% of the time, Pallas kernels for 7%

commit v1 on v0

--- a/solution.py
+++ b/solution.py
@@ -75,7 +75,7 @@
     vector_refs, out_ref = refs[:-1], refs[-1]
     (rows, width), (part, nb) = slab_ref.shape, out_ref.shape
     total = 0
-    for columns in column_tiles(width, TILE_LIMIT):
+    for columns in column_tiles(width, width):
         vh, vl = split(jnp.concatenate([ref[:, columns] for ref in vector_refs], axis=0))
         ch, cl = split(slab_ref[:, columns])
         found = dot(jnp.concatenate([ch, cl], axis=0), vh, ROWS)
@@ -124,19 +124,27 @@
 
 def matrices_kernel(*refs):
     share_refs, between_ref, triangle_refs = refs[:4], refs[4], refs[5:]
-    nb = between_ref.shape[0]
+    nb = between_ref.shape[1]
     group = nb // 4
     lane = lax.broadcasted_iota(jnp.int32, (1, nb), 1)
-    triangles = [[] for _ in range(PANELS)]
+    between, triangles = [], [[] for _ in range(PANELS)]
     for side in range(4):
         held = from_place(share_refs[side][...], side, group, lane)
         other = from_place(share_refs[side ^ 1][:group], side, group, lane)
         far = ((lane // group) ^ side) == 3
-        between_ref[side * group : (side + 1) * group] = jnp.where(far, other, held[:group])
+        between.append(jnp.where(far, other, held[:group]))
         for p in range(PANELS):
             triangles[p].append(held[(1 + p) * group : (2 + p) * group])
+    between_ref[...] = jnp.concatenate(split(jnp.concatenate(between, axis=0)), axis=0)
     for p in range(PANELS):
-        triangle_refs[p][...] = jnp.concatenate(triangles[p], axis=0).T
+        triangle_refs[p][...] = jnp.concatenate(split(jnp.concatenate(triangles[p], axis=0).T), axis=0)
+
+
+def times(left, parts):
+    rows, depth = left.shape
+    high, low = split(left)
+    main = dot(jnp.concatenate([high, low], axis=0), parts[:depth], PLAIN)
+    return main[:rows] + (main[rows:] + dot(high, parts[depth:], PLAIN))
 
 
 def update_kernel(pieces, terms, *refs):
@@ -151,9 +159,9 @@
         total += ref[...]
     total = jnp.concatenate([total[:, k * group : (k + 1) * group] for k in range(4)], axis=0)
     total = near_ref[...] + jnp.concatenate([jnp.zeros((PANELS * rows, nb - group), jnp.float32), total], axis=1)
-    scaled = exact(total[:rows], first_ref[...], PLAIN)
-    inner = total[rows:] - exact(scaled, between_ref[...], PLAIN)
-    later = exact(inner, second_ref[...], PLAIN)
+    scaled = times(total[:rows], first_ref[...])
+    inner = total[rows:] - times(scaled, between_ref[...])
+    later = times(inner, second_ref[...])
     both = jnp.concatenate(split(jnp.concatenate([scaled, later], axis=1)), axis=0)
 
     copies = []
@@ -180,10 +188,10 @@
     )(*arrays)
 
 
-def small(kernel, shapes, *arrays):
+def small(kernel, shapes, *arrays, kind=jnp.float32):
     return pl.pallas_call(
         kernel,
-        out_shape=[jax.ShapeDtypeStruct(shape, jnp.float32) for shape in shapes],
+        out_shape=[jax.ShapeDtypeStruct(shape, kind) for shape in shapes],
         compiler_params=pltpu.CompilerParams(vmem_limit_bytes=SMALL_LIMIT),
         cost_estimate=COST,
     )(*arrays)
@@ -260,7 +268,7 @@
     shares = [share, *(across(share, way) for way in (first, second, both))]
     far = [over_rest({high | low: array}, low, across) for array in corner]
     far = [held[q] for held in far for q in sorted(held)]
-    matrices = small(matrices_kernel, [(nb, nb)] * (1 + PANELS), *shares)
+    matrices = small(matrices_kernel, [(2 * nb, nb)] * (1 + PANELS), *shares, kind=jnp.bfloat16)
     (found,) = products(corner_kernel, [slab, *far], (2 * rows // 4, nb))
     count, part = len(near), len(far) // PANELS
     pieces = [piece for p in range(PANELS) for piece in (*((at, p) for at in range(count)), *((count + p * part + at, None) for at in range(part)))]

time: 77.5 us -> 77.5 us (level)
  no operation moved by 1% of the time
where the time goes in v1:
time: 77.5 us; the launch traced here: 77.3 us
  waiting for transfers between devices  44.5 us (57%)
  starting transfers between devices  23.5 us (30%)
  Pallas kernels  9.13 us (12%)
    ppermute x19, waiting for transfers between devices, exchange(): return lax.ppermute(array, axis, [(i, i ^ partner(i)) for i in range(size)])  44.5 us
    ppermute x19, starting transfers between devices, exchange(): return lax.ppermute(array, axis, [(i, i ^ partner(i)) for i in range(size)])  23.5 us
    pallas_call x2, Pallas kernels, products(): pl.pallas_call(kernel, in_specs=[pl.BlockSpec(memory_space=pltpu.VMEM)] *...  4.69 us
    pallas_call x1, Pallas kernels, update(): pl.pallas_call(functools.partial(update_kernel, pieces, len(terms)), in_s...  3.92 us
  transfers between devices with their start and end apart: 19, of which 6 were waited for; matrix products, arithmetic and copies ran while one was open for 0% of the time, Pallas kernels for 7%

profile of v1, /device:TPU:0, one launch (start us, length us, event | category | flops | bytes accessed | tf_op | source)
XLA Modules:
  0.0 77.3 jit_solution(9680699202809125588)
XLA Ops:
  0.0 0.0 copy-start.1
  0.0 0.0 copy-start.2
  0.0 0.0 copy-start
  0.0 3.0 %collective-permute-start.1 = (f32[2,16,12544]{2,1,0:T(8,128)}, f32[2,16,12544]{2,1,0:T(8,128)S(1)}, u32[]{:S(2)}, u32[]{:S(2)}) collective-permute-start(f32[2,16,12544]{2,1,0:T(8,128)} %refs_9_), channel_id=1, source_target_pairs={{0,2},{1,5},{2,0},{3,7},{4,6},{5,1},{6,4},{7,3},{8,10},{9,13},{10,... | collective-permute-start | bytes 4816904 | tf_op jit(solution)/shard_map/ppermute | solution.py:222
  3.0 0.0 collective-permute-start
  3.0 1.5 %collective-permute-start.2 = (f32[2,16,12544]{2,1,0:T(8,128)}, f32[2,16,12544]{2,1,0:T(8,128)S(1)}, u32[]{:S(2)}, u32[]{:S(2)}) collective-permute-start(f32[2,16,12544]{2,1,0:T(8,128)} %refs_9_), channel_id=1, source_target_pairs={{0,4},{1,3},{2,6},{3,1},{4,0},{5,7},{6,2},{7,5},{8,12},{9,11},{10,... | collective-permute-start | bytes 4816904 | tf_op jit(solution)/shard_map/ppermute | solution.py:222
  4.5 0.0 collective-permute-start.5
  4.5 34.2 %collective-permute-done.1.refs_2_.refs_11_ = f32[2,16,12544]{2,1,0:T(8,128)S(1)} collective-permute-done((f32[2,16,12544]{2,1,0:T(8,128)}, f32[2,16,12544]{2,1,0:T(8,128)S(1)}, u32[]{:S(2)}, u32[]{:S(2)}) %collective-permute-start.1) | collective-permute-done | bytes 1605664 | tf_op jit(solution)/shard_map/ppermute | solution.py:222
  38.7 0.1 slice_bitcast_fusion
  38.8 1.6 %collective-permute-start.10 = (f32[16,12544]{1,0:T(8,128)S(1)}, f32[16,12544]{1,0:T(8,128)S(1)}, u32[]{:S(2)}, u32[]{:S(2)}) collective-permute-start(f32[16,12544]{1,0:T(8,128)S(1)} %slice_bitcast_fusion), channel_id=1, source_target_pairs={{0,4},{1,3},{2,6},{3,1},{4,0},{5,7},{6,2},{7,5},{8,12},{9,11},{10,... | collective-permute-start | bytes 2408456 | tf_op jit(solution)/shard_map/ppermute | solution.py:222
  40.4 0.0 collective-permute-start.4
  40.4 0.0 collective-permute-done.2.refs_4_.refs_13_
  40.4 0.5 collective-permute-start.3
  40.9 0.1 slice_bitcast_fusion.1
  41.0 0.0 collective-permute-done.5.refs_1_
  41.0 2.4 %collective-permute-start.9 = (f32[16,12544]{1,0:T(8,128)S(1)}, f32[16,12544]{1,0:T(8,128)S(1)}, u32[]{:S(2)}, u32[]{:S(2)}) collective-permute-start(f32[16,12544]{1,0:T(8,128)S(1)} %slice_bitcast_fusion.1), channel_id=1, source_target_pairs={{0,2},{1,5},{2,0},{3,7},{4,6},{5,1},{6,4},{7,3},{8,10},{9,13},{10,... | collective-permute-start | bytes 2408456 | tf_op jit(solution)/shard_map/ppermute | solution.py:222
  43.4 0.0 copy-done.2
  43.4 0.2 shard_map.37.refs_4_
  43.6 0.0 collective-permute-done.refs_1_.refs_10_
  43.6 0.2 collective-permute-done.4.refs_5_.refs_14_
  43.8 2.3 %collective-permute-done.3.refs_3_.refs_12_ = f32[2,16,12544]{2,1,0:T(8,128)S(1)} collective-permute-done((f32[2,16,12544]{2,1,0:T(8,128)S(1)}, f32[2,16,12544]{2,1,0:T(8,128)S(1)}, u32[]{:S(2)}, u32[]{:S(2)}) %collective-permute-start.3) | collective-permute-done | bytes 1605664 | tf_op jit(solution)/shard_map/ppermute | solution.py:222
  46.1 0.0 copy-done.1
  46.1 0.0 copy-done
  46.1 3.6 %shard_map.38.refs_0_ = f32[96,128]{1,0:T(8,128)S(1)} custom-call(f32[32,12544]{1,0:T(8,128)S(1)} %copy-done, f32[2,16,12544]{2,1,0:T(8,128)S(1)} %copy-done.1, f32[2,16,12544]{2,1,0:T(8,128)S(1)} %collective-permute-done.refs_1_.refs_10_, f32[2,16,12544]{2,1,0:T(8,128)S(1)} %collective-permute-done.1.refs_2_.refs_11_, ...), custom_call_target="tpu_custom_call" | custom-call | flops 1 | bytes 1 | tf_op jit(solution)/shard_map/pallas_call | solution.py:181
  49.7 3.6 %collective-permute-start.8 = (f32[96,128]{1,0:T(8,128)S(1)}, f32[96,128]{1,0:T(8,128)S(1)}, u32[]{:S(2)}, u32[]{:S(2)}) collective-permute-start(f32[96,128]{1,0:T(8,128)S(1)} %shard_map.38.refs_0_), channel_id=1, source_target_pairs={{0,24},{8,16},{16,8},{24,0},{1,25},{9,17},{17,9},{25,1},{2,26},{10... | collective-permute-start | bytes 147464 | tf_op jit(solution)/shard_map/ppermute | solution.py:222
  53.3 0.0 collective-permute-start.7
  53.4 0.8 %collective-permute-start.6 = (f32[96,128]{1,0:T(8,128)S(1)}, f32[96,128]{1,0:T(8,128)S(1)}, u32[]{:S(2)}, u32[]{:S(2)}) collective-permute-start(f32[96,128]{1,0:T(8,128)S(1)} %shard_map.38.refs_0_), channel_id=1, source_target_pairs={{0,8},{8,0},{16,24},{24,16},{1,9},{9,1},{17,25},{25,17},{2,10},{10... | collective-permute-start | bytes 147464 | tf_op jit(solution)/shard_map/ppermute | solution.py:222
  54.1 4.4 %collective-permute-done.10.refs_2_.refs_17_ = f32[16,12544]{1,0:T(8,128)S(1)} collective-permute-done((f32[16,12544]{1,0:T(8,128)S(1)}, f32[16,12544]{1,0:T(8,128)S(1)}, u32[]{:S(2)}, u32[]{:S(2)}) %collective-permute-start.10) | collective-permute-done | bytes 802848 | tf_op jit(solution)/shard_map/ppermute | solution.py:222
  58.5 0.0 collective-permute-done.9.refs_0_.refs_15_
  58.5 0.0 collective-permute-done.8.refs_3_
  58.5 0.0 collective-permute-done.7.refs_2_
  58.5 0.0 collective-permute-done.6.refs_1_
  58.5 1.0 %collective-permute-start.11 = (f32[16,12544]{1,0:T(8,128)S(1)}, f32[16,12544]{1,0:T(8,128)S(1)}, u32[]{:S(2)}, u32[]{:S(2)}) collective-permute-start(f32[16,12544]{1,0:T(8,128)S(1)} %collective-permute-done.9.refs_0_.refs_15_), channel_id=1, source_target_pairs={{0,1},{1,0},{2,3},{3,2},{4,5},{5,4},{6,7},{7,6},{8,9},{9,8},{10,11... | collective-permute-start | bytes 2408456 | tf_op jit(solution)/shard_map/ppermute | solution.py:222
  59.5 0.1 collective-permute-start.12
  59.6 3.9 %collective-permute-start.18 = (f32[96,128]{1,0:T(8,128)S(1)}, f32[96,128]{1,0:T(8,128)S(1)}, u32[]{:S(2)}, u32[]{:S(2)}) collective-permute-start(f32[96,128]{1,0:T(8,128)S(1)} %get-tuple-element.37.refs_0_), channel_id=1, source_target_pairs={{0,6},{1,7},{2,4},{3,5},{4,2},{5,3},{6,0},{7,1},{8,14},{9,15},{10,... | collective-permute-start | bytes 147464 | tf_op jit(solution)/shard_map/ppermute | solution.py:222
  63.5 0.0 collective-permute-start.17
  63.5 0.6 collective-permute-start.16
  64.1 0.0 collective-permute-done.11.refs_1_.refs_16_
  64.1 0.0 collective-permute-done.12.refs_3_.refs_18_
  64.1 1.1 %shard_map.40.refs_1_ = f32[16,128]{1,0:T(8,128)S(1)} custom-call(f32[32,12544]{1,0:T(8,128)S(1)} %copy-done, f32[16,12544]{1,0:T(8,128)S(1)} %collective-permute-done.9.refs_0_.refs_15_, f32[16,12544]{1,0:T(8,128)S(1)} %collective-permute-done.11.refs_1_.refs_16_, f32[16,12544]{1,0:T(8,128)S(1)} %collective-permute-done.10.refs_2_.refs_17_, ...), custom_call_target="tpu_custom_call" | custom-call | flops 1 | bytes 1 | tf_op jit(solution)/shard_map/pallas_call | solution.py:181
  65.2 3.6 %collective-permute-start.15 = (f32[16,128]{1,0:T(8,128)S(1)}, f32[16,128]{1,0:T(8,128)S(1)}, u32[]{:S(2)}, u32[]{:S(2)}) collective-permute-start(f32[16,128]{1,0:T(8,128)S(1)} %shard_map.40.refs_1_), channel_id=1, source_target_pairs={{0,24},{8,16},{16,8},{24,0},{1,25},{9,17},{17,9},{25,1},{2,26},{10... | collective-permute-start | bytes 24584 | tf_op jit(solution)/shard_map/ppermute | solution.py:222
  68.9 0.0 collective-permute-start.14
  68.9 0.0 collective-permute-done.18.refs_3_
  68.9 0.8 %collective-permute-start.13 = (f32[16,128]{1,0:T(8,128)S(1)}, f32[16,128]{1,0:T(8,128)S(1)}, u32[]{:S(2)}, u32[]{:S(2)}) collective-permute-start(f32[16,128]{1,0:T(8,128)S(1)} %shard_map.40.refs_1_), channel_id=1, source_target_pairs={{0,8},{8,0},{16,24},{24,16},{1,9},{9,1},{17,25},{25,17},{2,10},{10... | collective-permute-start | bytes 24584 | tf_op jit(solution)/shard_map/ppermute | solution.py:222
  69.6 0.0 collective-permute-done.17.refs_2_
  69.6 0.0 collective-permute-done.16.refs_1_
  69.6 0.3 shard_map.41
  70.0 0.9 %collective-permute-done.15.refs_4_ = f32[16,128]{1,0:T(8,128)S(1)} collective-permute-done((f32[16,128]{1,0:T(8,128)S(1)}, f32[16,128]{1,0:T(8,128)S(1)}, u32[]{:S(2)}, u32[]{:S(2)}) %collective-permute-start.15) | collective-permute-done | bytes 8224 | tf_op jit(solution)/shard_map/ppermute | solution.py:222
  70.8 2.6 %collective-permute-done.14.refs_3_ = f32[16,128]{1,0:T(8,128)S(1)} collective-permute-done((f32[16,128]{1,0:T(8,128)S(1)}, f32[16,128]{1,0:T(8,128)S(1)}, u32[]{:S(2)}, u32[]{:S(2)}) %collective-permute-start.14) | collective-permute-done | bytes 8224 | tf_op jit(solution)/shard_map/ppermute | solution.py:222
  73.4 0.0 collective-permute-done.13.refs_2_
  73.4 3.9 %shard_map.42 = f32[32,12544]{1,0:T(8,128)} custom-call(f32[64,128]{1,0:T(8,128)S(1)} %get-tuple-element.34.refs_0_, f32[16,128]{1,0:T(8,128)S(1)} %shard_map.40.refs_1_, f32[16,128]{1,0:T(8,128)S(1)} %collective-permute-done.13.refs_2_, f32[16,128]{1,0:T(8,128)S(1)} %collective-permute-done.14.refs_3_, f32[16,128]{1,0:T(8,128)S(1)} %collective-permute-done.15.refs_4_, ...), custom_call_target="tpu_custom_call" | custom-call | flops 1 | bytes 1 | tf_op jit(solution)/shard_map/pallas_call | solution.py:203
  (1 shorter events, 0.0 us)
Async XLA Ops:
  0.0 46.1 %copy-start.1 = (f32[2,16,12544]{2,1,0:T(8,128)S(1)}, f32[2,16,12544]{2,1,0:T(8,128)}, u32[]{:S(2)}) copy-start(f32[2,16,12544]{2,1,0:T(8,128)} %refs_9_) | copy-start | bytes 4816900
  0.0 43.4 %copy-start.2 = (f32[2,16,128]{2,1,0:T(8,128)S(1)}, f32[2,16,128]{2,1,0:T(8,128)}, u32[]{:S(2)}) copy-start(f32[2,16,128]{2,1,0:T(8,128)} %refs_0_.1) | copy-start | bytes 49156
  0.0 46.1 %copy-start = (f32[32,12544]{1,0:T(8,128)S(1)}, f32[32,12544]{1,0:T(8,128)}, u32[]{:S(2)}) copy-start(f32[32,12544]{1,0:T(8,128)} %refs_8_.1) | copy-start | bytes 4816900
  0.0 38.7 %collective-permute-start.1 = (f32[2,16,12544]{2,1,0:T(8,128)}, f32[2,16,12544]{2,1,0:T(8,128)S(1)}, u32[]{:S(2)}, u32[]{:S(2)}) collective-permute-start(f32[2,16,12544]{2,1,0:T(8,128)} %refs_9_), channel_id=1, source_target_pairs={{0,2},{1,5},{2,0},{3,7},{4,6},{5,1},{6,4},{7,3},{8,10},{9,13},{10,... | collective-permute-start | bytes 4816904 | tf_op jit(solution)/shard_map/ppermute | solution.py:222
  3.0 40.6 %collective-permute-start = (f32[2,16,12544]{2,1,0:T(8,128)}, f32[2,16,12544]{2,1,0:T(8,128)S(1)}, u32[]{:S(2)}, u32[]{:S(2)}) collective-permute-start(f32[2,16,12544]{2,1,0:T(8,128)} %refs_9_), channel_id=1, source_target_pairs={{0,1},{1,0},{2,3},{3,2},{4,5},{5,4},{6,7},{7,6},{8,9},{9,8},{10,11... | collective-permute-start | bytes 4816904 | tf_op jit(solution)/shard_map/ppermute | solution.py:222
  3.0 37.4 %collective-permute-start.2 = (f32[2,16,12544]{2,1,0:T(8,128)}, f32[2,16,12544]{2,1,0:T(8,128)S(1)}, u32[]{:S(2)}, u32[]{:S(2)}) collective-permute-start(f32[2,16,12544]{2,1,0:T(8,128)} %refs_9_), channel_id=1, source_target_pairs={{0,4},{1,3},{2,6},{3,1},{4,0},{5,7},{6,2},{7,5},{8,12},{9,11},{10,... | collective-permute-start | bytes 4816904 | tf_op jit(solution)/shard_map/ppermute | solution.py:222
  4.5 36.4 %collective-permute-start.5 = (f32[2,16,128]{2,1,0:T(8,128)}, f32[2,16,128]{2,1,0:T(8,128)S(1)}, u32[]{:S(2)}, u32[]{:S(2)}) collective-permute-start(f32[2,16,128]{2,1,0:T(8,128)} %refs_0_.1), channel_id=1, source_target_pairs={{0,1},{1,0},{2,3},{3,2},{4,5},{5,4},{6,7},{7,6},{8,9},{9,8},{10,11... | collective-permute-start | bytes 49160 | tf_op jit(solution)/shard_map/ppermute | solution.py:222
  38.8 19.7 %collective-permute-start.10 = (f32[16,12544]{1,0:T(8,128)S(1)}, f32[16,12544]{1,0:T(8,128)S(1)}, u32[]{:S(2)}, u32[]{:S(2)}) collective-permute-start(f32[16,12544]{1,0:T(8,128)S(1)} %slice_bitcast_fusion), channel_id=1, source_target_pairs={{0,4},{1,3},{2,6},{3,1},{4,0},{5,7},{6,2},{7,5},{8,12},{9,11},{10,... | collective-permute-start | bytes 2408456 | tf_op jit(solution)/shard_map/ppermute | solution.py:222
  40.4 3.5 %collective-permute-start.4 = (f32[2,16,12544]{2,1,0:T(8,128)S(1)}, f32[2,16,12544]{2,1,0:T(8,128)S(1)}, u32[]{:S(2)}, u32[]{:S(2)}) collective-permute-start(f32[2,16,12544]{2,1,0:T(8,128)S(1)} %collective-permute-done.1.refs_2_.refs_11_), channel_id=1, source_target_pairs={{0,1},{1,0},{2,3},{3,2},{4,5},{5,4},{6,7},{7,6},{8,9},{9,8},{10,11... | collective-permute-start | bytes 4816904 | tf_op jit(solution)/shard_map/ppermute | solution.py:222
  40.4 5.7 %collective-permute-start.3 = (f32[2,16,12544]{2,1,0:T(8,128)S(1)}, f32[2,16,12544]{2,1,0:T(8,128)S(1)}, u32[]{:S(2)}, u32[]{:S(2)}) collective-permute-start(f32[2,16,12544]{2,1,0:T(8,128)S(1)} %collective-permute-done.2.refs_4_.refs_13_), channel_id=1, source_target_pairs={{0,1},{1,0},{2,3},{3,2},{4,5},{5,4},{6,7},{7,6},{8,9},{9,8},{10,11... | collective-permute-start | bytes 4816904 | tf_op jit(solution)/shard_map/ppermute | solution.py:222
  41.0 17.5 %collective-permute-start.9 = (f32[16,12544]{1,0:T(8,128)S(1)}, f32[16,12544]{1,0:T(8,128)S(1)}, u32[]{:S(2)}, u32[]{:S(2)}) collective-permute-start(f32[16,12544]{1,0:T(8,128)S(1)} %slice_bitcast_fusion.1), channel_id=1, source_target_pairs={{0,2},{1,5},{2,0},{3,7},{4,6},{5,1},{6,4},{7,3},{8,10},{9,13},{10,... | collective-permute-start | bytes 2408456 | tf_op jit(solution)/shard_map/ppermute | solution.py:222
  49.7 8.8 %collective-permute-start.8 = (f32[96,128]{1,0:T(8,128)S(1)}, f32[96,128]{1,0:T(8,128)S(1)}, u32[]{:S(2)}, u32[]{:S(2)}) collective-permute-start(f32[96,128]{1,0:T(8,128)S(1)} %shard_map.38.refs_0_), channel_id=1, source_target_pairs={{0,24},{8,16},{16,8},{24,0},{1,25},{9,17},{17,9},{25,1},{2,26},{10... | collective-permute-start | bytes 147464 | tf_op jit(solution)/shard_map/ppermute | solution.py:222
  53.3 5.2 %collective-permute-start.7 = (f32[96,128]{1,0:T(8,128)S(1)}, f32[96,128]{1,0:T(8,128)S(1)}, u32[]{:S(2)}, u32[]{:S(2)}) collective-permute-start(f32[96,128]{1,0:T(8,128)S(1)} %shard_map.38.refs_0_), channel_id=1, source_target_pairs={{0,16},{8,24},{16,0},{24,8},{1,17},{9,25},{17,1},{25,9},{2,18},{10... | collective-permute-start | bytes 147464 | tf_op jit(solution)/shard_map/ppermute | solution.py:222
  53.4 5.2 %collective-permute-start.6 = (f32[96,128]{1,0:T(8,128)S(1)}, f32[96,128]{1,0:T(8,128)S(1)}, u32[]{:S(2)}, u32[]{:S(2)}) collective-permute-start(f32[96,128]{1,0:T(8,128)S(1)} %shard_map.38.refs_0_), channel_id=1, source_target_pairs={{0,8},{8,0},{16,24},{24,16},{1,9},{9,1},{17,25},{25,17},{2,10},{10... | collective-permute-start | bytes 147464 | tf_op jit(solution)/shard_map/ppermute | solution.py:222
  58.5 5.6 %collective-permute-start.11 = (f32[16,12544]{1,0:T(8,128)S(1)}, f32[16,12544]{1,0:T(8,128)S(1)}, u32[]{:S(2)}, u32[]{:S(2)}) collective-permute-start(f32[16,12544]{1,0:T(8,128)S(1)} %collective-permute-done.9.refs_0_.refs_15_), channel_id=1, source_target_pairs={{0,1},{1,0},{2,3},{3,2},{4,5},{5,4},{6,7},{7,6},{8,9},{9,8},{10,11... | collective-permute-start | bytes 2408456 | tf_op jit(solution)/shard_map/ppermute | solution.py:222
  59.5 4.6 %collective-permute-start.12 = (f32[16,12544]{1,0:T(8,128)S(1)}, f32[16,12544]{1,0:T(8,128)S(1)}, u32[]{:S(2)}, u32[]{:S(2)}) collective-permute-start(f32[16,12544]{1,0:T(8,128)S(1)} %collective-permute-done.10.refs_2_.refs_17_), channel_id=1, source_target_pairs={{0,1},{1,0},{2,3},{3,2},{4,5},{5,4},{6,7},{7,6},{8,9},{9,8},{10,11... | collective-permute-start | bytes 2408456 | tf_op jit(solution)/shard_map/ppermute | solution.py:222
  59.6 9.3 %collective-permute-start.18 = (f32[96,128]{1,0:T(8,128)S(1)}, f32[96,128]{1,0:T(8,128)S(1)}, u32[]{:S(2)}, u32[]{:S(2)}) collective-permute-start(f32[96,128]{1,0:T(8,128)S(1)} %get-tuple-element.37.refs_0_), channel_id=1, source_target_pairs={{0,6},{1,7},{2,4},{3,5},{4,2},{5,3},{6,0},{7,1},{8,14},{9,15},{10,... | collective-permute-start | bytes 147464 | tf_op jit(solution)/shard_map/ppermute | solution.py:222
  63.5 6.2 %collective-permute-start.17 = (f32[96,128]{1,0:T(8,128)S(1)}, f32[96,128]{1,0:T(8,128)S(1)}, u32[]{:S(2)}, u32[]{:S(2)}) collective-permute-start(f32[96,128]{1,0:T(8,128)S(1)} %get-tuple-element.37.refs_0_), channel_id=1, source_target_pairs={{0,4},{1,3},{2,6},{3,1},{4,0},{5,7},{6,2},{7,5},{8,12},{9,11},{10,... | collective-permute-start | bytes 147464 | tf_op jit(solution)/shard_map/ppermute | solution.py:222
  63.5 6.2 %collective-permute-start.16 = (f32[96,128]{1,0:T(8,128)S(1)}, f32[96,128]{1,0:T(8,128)S(1)}, u32[]{:S(2)}, u32[]{:S(2)}) collective-permute-start(f32[96,128]{1,0:T(8,128)S(1)} %get-tuple-element.37.refs_0_), channel_id=1, source_target_pairs={{0,2},{1,5},{2,0},{3,7},{4,6},{5,1},{6,4},{7,3},{8,10},{9,13},{10,... | collective-permute-start | bytes 147464 | tf_op jit(solution)/shard_map/ppermute | solution.py:222
  65.2 5.6 %collective-permute-start.15 = (f32[16,128]{1,0:T(8,128)S(1)}, f32[16,128]{1,0:T(8,128)S(1)}, u32[]{:S(2)}, u32[]{:S(2)}) collective-permute-start(f32[16,128]{1,0:T(8,128)S(1)} %shard_map.40.refs_1_), channel_id=1, source_target_pairs={{0,24},{8,16},{16,8},{24,0},{1,25},{9,17},{17,9},{25,1},{2,26},{10... | collective-permute-start | bytes 24584 | tf_op jit(solution)/shard_map/ppermute | solution.py:222
  68.9 4.5 %collective-permute-start.14 = (f32[16,128]{1,0:T(8,128)S(1)}, f32[16,128]{1,0:T(8,128)S(1)}, u32[]{:S(2)}, u32[]{:S(2)}) collective-permute-start(f32[16,128]{1,0:T(8,128)S(1)} %shard_map.40.refs_1_), channel_id=1, source_target_pairs={{0,16},{8,24},{16,0},{24,8},{1,17},{9,25},{17,1},{25,9},{2,18},{10... | collective-permute-start | bytes 24584 | tf_op jit(solution)/shard_map/ppermute | solution.py:222
  68.9 4.5 %collective-permute-start.13 = (f32[16,128]{1,0:T(8,128)S(1)}, f32[16,128]{1,0:T(8,128)S(1)}, u32[]{:S(2)}, u32[]{:S(2)}) collective-permute-start(f32[16,128]{1,0:T(8,128)S(1)} %shard_map.40.refs_1_), channel_id=1, source_target_pairs={{0,8},{8,0},{16,24},{24,16},{1,9},{9,1},{17,25},{25,17},{2,10},{10... | collective-permute-start | bytes 24584 | tf_op jit(solution)/shard_map/ppermute | solution.py:222

commit v2 on v0

--- a/solution.py
+++ b/solution.py
@@ -8,7 +8,6 @@
 from jax.sharding import PartitionSpec as P
 
 
-UNIT_LIMIT = 2048
 TILE_LIMIT = 8192
 VMEM_LIMIT = 32 * 1024 * 1024
 SMALL_LIMIT = 8 * 1024 * 1024
@@ -157,7 +156,7 @@
     both = jnp.concatenate(split(jnp.concatenate([scaled, later], axis=1)), axis=0)
 
     copies = []
-    for at, columns in enumerate(column_tiles(width, UNIT_LIMIT)):
+    for at, columns in enumerate(column_tiles(width, TILE_LIMIT)):
         blocks = [vector_refs[ref][:, columns] if p is None else vector_refs[ref][p, :, columns] for ref, p in pieces]
         high, low = split(jnp.concatenate(blocks, axis=0))
         main = dot(both, high, PLAIN)
@@ -199,7 +198,7 @@
         out_shape=jax.ShapeDtypeStruct(slab.shape, jnp.float32),
         scratch_shapes=[
             pltpu.VMEM(slab.shape, jnp.float32),
-            pltpu.SemaphoreType.DMA((len(column_tiles(width, UNIT_LIMIT)),)),
+            pltpu.SemaphoreType.DMA((len(column_tiles(width, TILE_LIMIT)),)),
         ],
         compiler_params=pltpu.CompilerParams(vmem_limit_bytes=VMEM_LIMIT),
         cost_estimate=COST,

time: 77.5 us -> 77.8 us (level)
  no operation moved by 1% of the time
where the time goes in v2:
time: 77.8 us; the launch traced here: 77.7 us
  waiting for transfers between devices  44.5 us (57%)
  starting transfers between devices  23.5 us (30%)
  Pallas kernels  9.48 us (12%)
    ppermute x19, waiting for transfers between devices, exchange(): return lax.ppermute(array, axis, [(i, i ^ partner(i)) for i in range(size)])  44.5 us
    ppermute x19, starting transfers between devices, exchange(): return lax.ppermute(array, axis, [(i, i ^ partner(i)) for i in range(size)])  23.5 us
    pallas_call x2, Pallas kernels, products(): pl.pallas_call(kernel, in_specs=[pl.BlockSpec(memory_space=pltpu.VMEM)] *...  4.71 us
    pallas_call x1, Pallas kernels, update(): pl.pallas_call(functools.partial(update_kernel, pieces, len(terms)), in_s...  4.26 us
  transfers between devices with their start and end apart: 19, of which 6 were waited for; matrix products, arithmetic and copies ran while one was open for 0% of the time, Pallas kernels for 7%

profile of v2, /device:TPU:0, one launch (start us, length us, event | category | flops | bytes accessed | tf_op | source)
XLA Modules:
  0.0 77.7 jit_solution(6323508379167465645)
XLA Ops:
  0.0 0.0 copy-start.1
  0.0 0.0 copy-start.2
  0.0 0.0 copy-start
  0.0 3.0 %collective-permute-start.1 = (f32[2,16,12544]{2,1,0:T(8,128)}, f32[2,16,12544]{2,1,0:T(8,128)S(1)}, u32[]{:S(2)}, u32[]{:S(2)}) collective-permute-start(f32[2,16,12544]{2,1,0:T(8,128)} %refs_9_), channel_id=1, source_target_pairs={{0,2},{1,5},{2,0},{3,7},{4,6},{5,1},{6,4},{7,3},{8,10},{9,13},{10,... | collective-permute-start | bytes 4816904 | tf_op jit(solution)/shard_map/ppermute | solution.py:213
  3.0 0.0 collective-permute-start
  3.0 1.5 %collective-permute-start.2 = (f32[2,16,12544]{2,1,0:T(8,128)}, f32[2,16,12544]{2,1,0:T(8,128)S(1)}, u32[]{:S(2)}, u32[]{:S(2)}) collective-permute-start(f32[2,16,12544]{2,1,0:T(8,128)} %refs_9_), channel_id=1, source_target_pairs={{0,4},{1,3},{2,6},{3,1},{4,0},{5,7},{6,2},{7,5},{8,12},{9,11},{10,... | collective-permute-start | bytes 4816904 | tf_op jit(solution)/shard_map/ppermute | solution.py:213
  4.5 0.0 collective-permute-start.5
  4.5 34.2 %collective-permute-done.1.refs_2_.refs_11_ = f32[2,16,12544]{2,1,0:T(8,128)S(1)} collective-permute-done((f32[2,16,12544]{2,1,0:T(8,128)}, f32[2,16,12544]{2,1,0:T(8,128)S(1)}, u32[]{:S(2)}, u32[]{:S(2)}) %collective-permute-start.1) | collective-permute-done | bytes 1605664 | tf_op jit(solution)/shard_map/ppermute | solution.py:213
  38.7 0.1 slice_bitcast_fusion
  38.8 1.6 %collective-permute-start.10 = (f32[16,12544]{1,0:T(8,128)S(1)}, f32[16,12544]{1,0:T(8,128)S(1)}, u32[]{:S(2)}, u32[]{:S(2)}) collective-permute-start(f32[16,12544]{1,0:T(8,128)S(1)} %slice_bitcast_fusion), channel_id=1, source_target_pairs={{0,4},{1,3},{2,6},{3,1},{4,0},{5,7},{6,2},{7,5},{8,12},{9,11},{10,... | collective-permute-start | bytes 2408456 | tf_op jit(solution)/shard_map/ppermute | solution.py:213
  40.4 0.0 collective-permute-start.4
  40.4 0.0 collective-permute-done.2.refs_4_.refs_13_
  40.4 0.5 collective-permute-start.3
  40.9 0.1 slice_bitcast_fusion.1
  41.0 0.0 collective-permute-done.5.refs_1_
  41.0 2.4 %collective-permute-start.9 = (f32[16,12544]{1,0:T(8,128)S(1)}, f32[16,12544]{1,0:T(8,128)S(1)}, u32[]{:S(2)}, u32[]{:S(2)}) collective-permute-start(f32[16,12544]{1,0:T(8,128)S(1)} %slice_bitcast_fusion.1), channel_id=1, source_target_pairs={{0,2},{1,5},{2,0},{3,7},{4,6},{5,1},{6,4},{7,3},{8,10},{9,13},{10,... | collective-permute-start | bytes 2408456 | tf_op jit(solution)/shard_map/ppermute | solution.py:213
  43.4 0.0 copy-done.2
  43.4 0.2 shard_map.37.refs_4_
  43.6 0.0 collective-permute-done.refs_1_.refs_10_
  43.6 0.2 collective-permute-done.4.refs_5_.refs_14_
  43.8 2.3 %collective-permute-done.3.refs_3_.refs_12_ = f32[2,16,12544]{2,1,0:T(8,128)S(1)} collective-permute-done((f32[2,16,12544]{2,1,0:T(8,128)S(1)}, f32[2,16,12544]{2,1,0:T(8,128)S(1)}, u32[]{:S(2)}, u32[]{:S(2)}) %collective-permute-start.3) | collective-permute-done | bytes 1605664 | tf_op jit(solution)/shard_map/ppermute | solution.py:213
  46.1 0.0 copy-done.1
  46.1 0.0 copy-done
  46.1 3.6 %shard_map.38.refs_0_ = f32[96,128]{1,0:T(8,128)S(1)} custom-call(f32[32,12544]{1,0:T(8,128)S(1)} %copy-done, f32[2,16,12544]{2,1,0:T(8,128)S(1)} %copy-done.1, f32[2,16,12544]{2,1,0:T(8,128)S(1)} %collective-permute-done.refs_1_.refs_10_, f32[2,16,12544]{2,1,0:T(8,128)S(1)} %collective-permute-done.1.refs_2_.refs_11_, ...), custom_call_target="tpu_custom_call" | custom-call | flops 1 | bytes 1 | tf_op jit(solution)/shard_map/pallas_call | solution.py:172
  49.7 3.6 %collective-permute-start.8 = (f32[96,128]{1,0:T(8,128)S(1)}, f32[96,128]{1,0:T(8,128)S(1)}, u32[]{:S(2)}, u32[]{:S(2)}) collective-permute-start(f32[96,128]{1,0:T(8,128)S(1)} %shard_map.38.refs_0_), channel_id=1, source_target_pairs={{0,24},{8,16},{16,8},{24,0},{1,25},{9,17},{17,9},{25,1},{2,26},{10... | collective-permute-start | bytes 147464 | tf_op jit(solution)/shard_map/ppermute | solution.py:213
  53.3 0.0 collective-permute-start.7
  53.4 0.8 %collective-permute-start.6 = (f32[96,128]{1,0:T(8,128)S(1)}, f32[96,128]{1,0:T(8,128)S(1)}, u32[]{:S(2)}, u32[]{:S(2)}) collective-permute-start(f32[96,128]{1,0:T(8,128)S(1)} %shard_map.38.refs_0_), channel_id=1, source_target_pairs={{0,8},{8,0},{16,24},{24,16},{1,9},{9,1},{17,25},{25,17},{2,10},{10... | collective-permute-start | bytes 147464 | tf_op jit(solution)/shard_map/ppermute | solution.py:213
  54.1 4.4 %collective-permute-done.10.refs_2_.refs_17_ = f32[16,12544]{1,0:T(8,128)S(1)} collective-permute-done((f32[16,12544]{1,0:T(8,128)S(1)}, f32[16,12544]{1,0:T(8,128)S(1)}, u32[]{:S(2)}, u32[]{:S(2)}) %collective-permute-start.10) | collective-permute-done | bytes 802848 | tf_op jit(solution)/shard_map/ppermute | solution.py:213
  58.5 0.0 collective-permute-done.9.refs_0_.refs_15_
  58.5 0.0 collective-permute-done.8.refs_3_
  58.5 0.0 collective-permute-done.7.refs_2_
  58.5 0.0 collective-permute-done.6.refs_1_
  58.5 1.0 %collective-permute-start.11 = (f32[16,12544]{1,0:T(8,128)S(1)}, f32[16,12544]{1,0:T(8,128)S(1)}, u32[]{:S(2)}, u32[]{:S(2)}) collective-permute-start(f32[16,12544]{1,0:T(8,128)S(1)} %collective-permute-done.9.refs_0_.refs_15_), channel_id=1, source_target_pairs={{0,1},{1,0},{2,3},{3,2},{4,5},{5,4},{6,7},{7,6},{8,9},{9,8},{10,11... | collective-permute-start | bytes 2408456 | tf_op jit(solution)/shard_map/ppermute | solution.py:213
  59.5 0.1 collective-permute-start.12
  59.6 3.9 %collective-permute-start.18 = (f32[96,128]{1,0:T(8,128)S(1)}, f32[96,128]{1,0:T(8,128)S(1)}, u32[]{:S(2)}, u32[]{:S(2)}) collective-permute-start(f32[96,128]{1,0:T(8,128)S(1)} %get-tuple-element.37.refs_0_), channel_id=1, source_target_pairs={{0,6},{1,7},{2,4},{3,5},{4,2},{5,3},{6,0},{7,1},{8,14},{9,15},{10,... | collective-permute-start | bytes 147464 | tf_op jit(solution)/shard_map/ppermute | solution.py:213
  63.5 0.0 collective-permute-start.17
  63.5 0.6 collective-permute-start.16
  64.1 0.0 collective-permute-done.11.refs_1_.refs_16_
  64.1 0.0 collective-permute-done.12.refs_3_.refs_18_
  64.1 1.1 %shard_map.40.refs_1_ = f32[16,128]{1,0:T(8,128)S(1)} custom-call(f32[32,12544]{1,0:T(8,128)S(1)} %copy-done, f32[16,12544]{1,0:T(8,128)S(1)} %collective-permute-done.9.refs_0_.refs_15_, f32[16,12544]{1,0:T(8,128)S(1)} %collective-permute-done.11.refs_1_.refs_16_, f32[16,12544]{1,0:T(8,128)S(1)} %collective-permute-done.10.refs_2_.refs_17_, ...), custom_call_target="tpu_custom_call" | custom-call | flops 1 | bytes 1 | tf_op jit(solution)/shard_map/pallas_call | solution.py:172
  65.3 3.6 %collective-permute-start.15 = (f32[16,128]{1,0:T(8,128)S(1)}, f32[16,128]{1,0:T(8,128)S(1)}, u32[]{:S(2)}, u32[]{:S(2)}) collective-permute-start(f32[16,128]{1,0:T(8,128)S(1)} %shard_map.40.refs_1_), channel_id=1, source_target_pairs={{0,24},{8,16},{16,8},{24,0},{1,25},{9,17},{17,9},{25,1},{2,26},{10... | collective-permute-start | bytes 24584 | tf_op jit(solution)/shard_map/ppermute | solution.py:213
  68.9 0.0 collective-permute-start.14
  68.9 0.0 collective-permute-done.18.refs_3_
  68.9 0.8 %collective-permute-start.13 = (f32[16,128]{1,0:T(8,128)S(1)}, f32[16,128]{1,0:T(8,128)S(1)}, u32[]{:S(2)}, u32[]{:S(2)}) collective-permute-start(f32[16,128]{1,0:T(8,128)S(1)} %shard_map.40.refs_1_), channel_id=1, source_target_pairs={{0,8},{8,0},{16,24},{24,16},{1,9},{9,1},{17,25},{25,17},{2,10},{10... | collective-permute-start | bytes 24584 | tf_op jit(solution)/shard_map/ppermute | solution.py:213
  69.7 0.0 collective-permute-done.17.refs_2_
  69.7 0.0 collective-permute-done.16.refs_1_
  69.7 0.3 shard_map.41
  70.0 0.9 %collective-permute-done.15.refs_4_ = f32[16,128]{1,0:T(8,128)S(1)} collective-permute-done((f32[16,128]{1,0:T(8,128)S(1)}, f32[16,128]{1,0:T(8,128)S(1)}, u32[]{:S(2)}, u32[]{:S(2)}) %collective-permute-start.15) | collective-permute-done | bytes 8224 | tf_op jit(solution)/shard_map/ppermute | solution.py:213
  70.9 2.6 %collective-permute-done.14.refs_3_ = f32[16,128]{1,0:T(8,128)S(1)} collective-permute-done((f32[16,128]{1,0:T(8,128)S(1)}, f32[16,128]{1,0:T(8,128)S(1)}, u32[]{:S(2)}, u32[]{:S(2)}) %collective-permute-start.14) | collective-permute-done | bytes 8224 | tf_op jit(solution)/shard_map/ppermute | solution.py:213
  73.4 0.0 collective-permute-done.13.refs_2_
  73.4 4.3 %shard_map.42 = f32[32,12544]{1,0:T(8,128)} custom-call(f32[64,128]{1,0:T(8,128)S(1)} %get-tuple-element.34.refs_0_, f32[16,128]{1,0:T(8,128)S(1)} %shard_map.40.refs_1_, f32[16,128]{1,0:T(8,128)S(1)} %collective-permute-done.13.refs_2_, f32[16,128]{1,0:T(8,128)S(1)} %collective-permute-done.14.refs_3_, f32[16,128]{1,0:T(8,128)S(1)} %collective-permute-done.15.refs_4_, ...), custom_call_target="tpu_custom_call" | custom-call | flops 1 | bytes 1 | tf_op jit(solution)/shard_map/pallas_call | solution.py:194
  (1 shorter events, 0.0 us)
Async XLA Ops:
  0.0 46.1 %copy-start.1 = (f32[2,16,12544]{2,1,0:T(8,128)S(1)}, f32[2,16,12544]{2,1,0:T(8,128)}, u32[]{:S(2)}) copy-start(f32[2,16,12544]{2,1,0:T(8,128)} %refs_9_) | copy-start | bytes 4816900
  0.0 43.4 %copy-start.2 = (f32[2,16,128]{2,1,0:T(8,128)S(1)}, f32[2,16,128]{2,1,0:T(8,128)}, u32[]{:S(2)}) copy-start(f32[2,16,128]{2,1,0:T(8,128)} %refs_0_.1) | copy-start | bytes 49156
  0.0 46.1 %copy-start = (f32[32,12544]{1,0:T(8,128)S(1)}, f32[32,12544]{1,0:T(8,128)}, u32[]{:S(2)}) copy-start(f32[32,12544]{1,0:T(8,128)} %refs_8_.1) | copy-start | bytes 4816900
  0.0 38.7 %collective-permute-start.1 = (f32[2,16,12544]{2,1,0:T(8,128)}, f32[2,16,12544]{2,1,0:T(8,128)S(1)}, u32[]{:S(2)}, u32[]{:S(2)}) collective-permute-start(f32[2,16,12544]{2,1,0:T(8,128)} %refs_9_), channel_id=1, source_target_pairs={{0,2},{1,5},{2,0},{3,7},{4,6},{5,1},{6,4},{7,3},{8,10},{9,13},{10,... | collective-permute-start | bytes 4816904 | tf_op jit(solution)/shard_map/ppermute | solution.py:213
  3.0 40.6 %collective-permute-start = (f32[2,16,12544]{2,1,0:T(8,128)}, f32[2,16,12544]{2,1,0:T(8,128)S(1)}, u32[]{:S(2)}, u32[]{:S(2)}) collective-permute-start(f32[2,16,12544]{2,1,0:T(8,128)} %refs_9_), channel_id=1, source_target_pairs={{0,1},{1,0},{2,3},{3,2},{4,5},{5,4},{6,7},{7,6},{8,9},{9,8},{10,11... | collective-permute-start | bytes 4816904 | tf_op jit(solution)/shard_map/ppermute | solution.py:213
  3.0 37.4 %collective-permute-start.2 = (f32[2,16,12544]{2,1,0:T(8,128)}, f32[2,16,12544]{2,1,0:T(8,128)S(1)}, u32[]{:S(2)}, u32[]{:S(2)}) collective-permute-start(f32[2,16,12544]{2,1,0:T(8,128)} %refs_9_), channel_id=1, source_target_pairs={{0,4},{1,3},{2,6},{3,1},{4,0},{5,7},{6,2},{7,5},{8,12},{9,11},{10,... | collective-permute-start | bytes 4816904 | tf_op jit(solution)/shard_map/ppermute | solution.py:213
  4.5 36.4 %collective-permute-start.5 = (f32[2,16,128]{2,1,0:T(8,128)}, f32[2,16,128]{2,1,0:T(8,128)S(1)}, u32[]{:S(2)}, u32[]{:S(2)}) collective-permute-start(f32[2,16,128]{2,1,0:T(8,128)} %refs_0_.1), channel_id=1, source_target_pairs={{0,1},{1,0},{2,3},{3,2},{4,5},{5,4},{6,7},{7,6},{8,9},{9,8},{10,11... | collective-permute-start | bytes 49160 | tf_op jit(solution)/shard_map/ppermute | solution.py:213
  38.8 19.7 %collective-permute-start.10 = (f32[16,12544]{1,0:T(8,128)S(1)}, f32[16,12544]{1,0:T(8,128)S(1)}, u32[]{:S(2)}, u32[]{:S(2)}) collective-permute-start(f32[16,12544]{1,0:T(8,128)S(1)} %slice_bitcast_fusion), channel_id=1, source_target_pairs={{0,4},{1,3},{2,6},{3,1},{4,0},{5,7},{6,2},{7,5},{8,12},{9,11},{10,... | collective-permute-start | bytes 2408456 | tf_op jit(solution)/shard_map/ppermute | solution.py:213
  40.4 3.5 %collective-permute-start.4 = (f32[2,16,12544]{2,1,0:T(8,128)S(1)}, f32[2,16,12544]{2,1,0:T(8,128)S(1)}, u32[]{:S(2)}, u32[]{:S(2)}) collective-permute-start(f32[2,16,12544]{2,1,0:T(8,128)S(1)} %collective-permute-done.1.refs_2_.refs_11_), channel_id=1, source_target_pairs={{0,1},{1,0},{2,3},{3,2},{4,5},{5,4},{6,7},{7,6},{8,9},{9,8},{10,11... | collective-permute-start | bytes 4816904 | tf_op jit(solution)/shard_map/ppermute | solution.py:213
  40.4 5.7 %collective-permute-start.3 = (f32[2,16,12544]{2,1,0:T(8,128)S(1)}, f32[2,16,12544]{2,1,0:T(8,128)S(1)}, u32[]{:S(2)}, u32[]{:S(2)}) collective-permute-start(f32[2,16,12544]{2,1,0:T(8,128)S(1)} %collective-permute-done.2.refs_4_.refs_13_), channel_id=1, source_target_pairs={{0,1},{1,0},{2,3},{3,2},{4,5},{5,4},{6,7},{7,6},{8,9},{9,8},{10,11... | collective-permute-start | bytes 4816904 | tf_op jit(solution)/shard_map/ppermute | solution.py:213
  41.0 17.5 %collective-permute-start.9 = (f32[16,12544]{1,0:T(8,128)S(1)}, f32[16,12544]{1,0:T(8,128)S(1)}, u32[]{:S(2)}, u32[]{:S(2)}) collective-permute-start(f32[16,12544]{1,0:T(8,128)S(1)} %slice_bitcast_fusion.1), channel_id=1, source_target_pairs={{0,2},{1,5},{2,0},{3,7},{4,6},{5,1},{6,4},{7,3},{8,10},{9,13},{10,... | collective-permute-start | bytes 2408456 | tf_op jit(solution)/shard_map/ppermute | solution.py:213
  49.7 8.8 %collective-permute-start.8 = (f32[96,128]{1,0:T(8,128)S(1)}, f32[96,128]{1,0:T(8,128)S(1)}, u32[]{:S(2)}, u32[]{:S(2)}) collective-permute-start(f32[96,128]{1,0:T(8,128)S(1)} %shard_map.38.refs_0_), channel_id=1, source_target_pairs={{0,24},{8,16},{16,8},{24,0},{1,25},{9,17},{17,9},{25,1},{2,26},{10... | collective-permute-start | bytes 147464 | tf_op jit(solution)/shard_map/ppermute | solution.py:213
  53.3 5.2 %collective-permute-start.7 = (f32[96,128]{1,0:T(8,128)S(1)}, f32[96,128]{1,0:T(8,128)S(1)}, u32[]{:S(2)}, u32[]{:S(2)}) collective-permute-start(f32[96,128]{1,0:T(8,128)S(1)} %shard_map.38.refs_0_), channel_id=1, source_target_pairs={{0,16},{8,24},{16,0},{24,8},{1,17},{9,25},{17,1},{25,9},{2,18},{10... | collective-permute-start | bytes 147464 | tf_op jit(solution)/shard_map/ppermute | solution.py:213
  53.4 5.2 %collective-permute-start.6 = (f32[96,128]{1,0:T(8,128)S(1)}, f32[96,128]{1,0:T(8,128)S(1)}, u32[]{:S(2)}, u32[]{:S(2)}) collective-permute-start(f32[96,128]{1,0:T(8,128)S(1)} %shard_map.38.refs_0_), channel_id=1, source_target_pairs={{0,8},{8,0},{16,24},{24,16},{1,9},{9,1},{17,25},{25,17},{2,10},{10... | collective-permute-start | bytes 147464 | tf_op jit(solution)/shard_map/ppermute | solution.py:213
  58.5 5.6 %collective-permute-start.11 = (f32[16,12544]{1,0:T(8,128)S(1)}, f32[16,12544]{1,0:T(8,128)S(1)}, u32[]{:S(2)}, u32[]{:S(2)}) collective-permute-start(f32[16,12544]{1,0:T(8,128)S(1)} %collective-permute-done.9.refs_0_.refs_15_), channel_id=1, source_target_pairs={{0,1},{1,0},{2,3},{3,2},{4,5},{5,4},{6,7},{7,6},{8,9},{9,8},{10,11... | collective-permute-start | bytes 2408456 | tf_op jit(solution)/shard_map/ppermute | solution.py:213
  59.5 4.6 %collective-permute-start.12 = (f32[16,12544]{1,0:T(8,128)S(1)}, f32[16,12544]{1,0:T(8,128)S(1)}, u32[]{:S(2)}, u32[]{:S(2)}) collective-permute-start(f32[16,12544]{1,0:T(8,128)S(1)} %collective-permute-done.10.refs_2_.refs_17_), channel_id=1, source_target_pairs={{0,1},{1,0},{2,3},{3,2},{4,5},{5,4},{6,7},{7,6},{8,9},{9,8},{10,11... | collective-permute-start | bytes 2408456 | tf_op jit(solution)/shard_map/ppermute | solution.py:213
  59.6 9.3 %collective-permute-start.18 = (f32[96,128]{1,0:T(8,128)S(1)}, f32[96,128]{1,0:T(8,128)S(1)}, u32[]{:S(2)}, u32[]{:S(2)}) collective-permute-start(f32[96,128]{1,0:T(8,128)S(1)} %get-tuple-element.37.refs_0_), channel_id=1, source_target_pairs={{0,6},{1,7},{2,4},{3,5},{4,2},{5,3},{6,0},{7,1},{8,14},{9,15},{10,... | collective-permute-start | bytes 147464 | tf_op jit(solution)/shard_map/ppermute | solution.py:213
  63.5 6.2 %collective-permute-start.17 = (f32[96,128]{1,0:T(8,128)S(1)}, f32[96,128]{1,0:T(8,128)S(1)}, u32[]{:S(2)}, u32[]{:S(2)}) collective-permute-start(f32[96,128]{1,0:T(8,128)S(1)} %get-tuple-element.37.refs_0_), channel_id=1, source_target_pairs={{0,4},{1,3},{2,6},{3,1},{4,0},{5,7},{6,2},{7,5},{8,12},{9,11},{10,... | collective-permute-start | bytes 147464 | tf_op jit(solution)/shard_map/ppermute | solution.py:213
  63.5 6.2 %collective-permute-start.16 = (f32[96,128]{1,0:T(8,128)S(1)}, f32[96,128]{1,0:T(8,128)S(1)}, u32[]{:S(2)}, u32[]{:S(2)}) collective-permute-start(f32[96,128]{1,0:T(8,128)S(1)} %get-tuple-element.37.refs_0_), channel_id=1, source_target_pairs={{0,2},{1,5},{2,0},{3,7},{4,6},{5,1},{6,4},{7,3},{8,10},{9,13},{10,... | collective-permute-start | bytes 147464 | tf_op jit(solution)/shard_map/ppermute | solution.py:213
  65.3 5.6 %collective-permute-start.15 = (f32[16,128]{1,0:T(8,128)S(1)}, f32[16,128]{1,0:T(8,128)S(1)}, u32[]{:S(2)}, u32[]{:S(2)}) collective-permute-start(f32[16,128]{1,0:T(8,128)S(1)} %shard_map.40.refs_1_), channel_id=1, source_target_pairs={{0,24},{8,16},{16,8},{24,0},{1,25},{9,17},{17,9},{25,1},{2,26},{10... | collective-permute-start | bytes 24584 | tf_op jit(solution)/shard_map/ppermute | solution.py:213
  68.9 4.5 %collective-permute-start.14 = (f32[16,128]{1,0:T(8,128)S(1)}, f32[16,128]{1,0:T(8,128)S(1)}, u32[]{:S(2)}, u32[]{:S(2)}) collective-permute-start(f32[16,128]{1,0:T(8,128)S(1)} %shard_map.40.refs_1_), channel_id=1, source_target_pairs={{0,16},{8,24},{16,0},{24,8},{1,17},{9,25},{17,1},{25,9},{2,18},{10... | collective-permute-start | bytes 24584 | tf_op jit(solution)/shard_map/ppermute | solution.py:213
  68.9 4.5 %collective-permute-start.13 = (f32[16,128]{1,0:T(8,128)S(1)}, f32[16,128]{1,0:T(8,128)S(1)}, u32[]{:S(2)}, u32[]{:S(2)}) collective-permute-start(f32[16,128]{1,0:T(8,128)S(1)} %shard_map.40.refs_1_), channel_id=1, source_target_pairs={{0,8},{8,0},{16,24},{24,16},{1,9},{9,1},{17,25},{25,17},{2,10},{10... | collective-permute-start | bytes 24584 | tf_op jit(solution)/shard_map/ppermute | solution.py:213

commit v3 on v0

--- a/solution.py
+++ b/solution.py
@@ -219,7 +219,8 @@
     while reach < depth:
         value = sum(terms[1:], terms[0])
         span = min(step, depth // reach)
-        terms = [value] + [exchange(value, lambda i, k=k: k * reach, depth, "prow") for k in range(1, span)]
+        steps = sorted(range(1, span), key=lambda k: (k != 1, k != span - 1))
+        terms = [value] + [exchange(value, lambda i, k=k: k * reach, depth, "prow") for k in steps]
         reach *= span
     return terms
 

time: 77.5 us -> 77.4 us (level)
  no operation moved by 1% of the time
where the time goes in v3:
time: 77.4 us; the launch traced here: 77.3 us
  waiting for transfers between devices  44.9 us (58%)
  starting transfers between devices  23 us (30%)
  Pallas kernels  9.17 us (12%)
    ppermute x19, waiting for transfers between devices, exchange(): return lax.ppermute(array, axis, [(i, i ^ partner(i)) for i in range(size)])  44.9 us
    ppermute x19, starting transfers between devices, exchange(): return lax.ppermute(array, axis, [(i, i ^ partner(i)) for i in range(size)])  23 us
    pallas_call x2, Pallas kernels, products(): pl.pallas_call(kernel, in_specs=[pl.BlockSpec(memory_space=pltpu.VMEM)] *...  4.71 us
    pallas_call x1, Pallas kernels, update(): pl.pallas_call(functools.partial(update_kernel, pieces, len(terms)), in_s...  3.94 us
  transfers between devices with their start and end apart: 19, of which 6 were waited for; matrix products, arithmetic and copies ran while one was open for 0% of the time, Pallas kernels for 7%

profile of v3, /device:TPU:0, one launch (start us, length us, event | category | flops | bytes accessed | tf_op | source)
XLA Modules:
  0.0 77.3 jit_solution(11289871474801250592)
XLA Ops:
  0.0 0.0 copy-start.1
  0.0 0.0 copy-start.2
  0.0 0.0 copy-start
  0.0 3.0 %collective-permute-start.1 = (f32[2,16,12544]{2,1,0:T(8,128)}, f32[2,16,12544]{2,1,0:T(8,128)S(1)}, u32[]{:S(2)}, u32[]{:S(2)}) collective-permute-start(f32[2,16,12544]{2,1,0:T(8,128)} %refs_9_), channel_id=1, source_target_pairs={{0,2},{1,5},{2,0},{3,7},{4,6},{5,1},{6,4},{7,3},{8,10},{9,13},{10,... | collective-permute-start | bytes 4816904 | tf_op jit(solution)/shard_map/ppermute | solution.py:214
  3.0 0.0 collective-permute-start
  3.0 1.5 %collective-permute-start.2 = (f32[2,16,12544]{2,1,0:T(8,128)}, f32[2,16,12544]{2,1,0:T(8,128)S(1)}, u32[]{:S(2)}, u32[]{:S(2)}) collective-permute-start(f32[2,16,12544]{2,1,0:T(8,128)} %refs_9_), channel_id=1, source_target_pairs={{0,4},{1,3},{2,6},{3,1},{4,0},{5,7},{6,2},{7,5},{8,12},{9,11},{10,... | collective-permute-start | bytes 4816904 | tf_op jit(solution)/shard_map/ppermute | solution.py:214
  4.5 0.0 collective-permute-start.5
  4.5 34.2 %collective-permute-done.1.refs_2_.refs_11_ = f32[2,16,12544]{2,1,0:T(8,128)S(1)} collective-permute-done((f32[2,16,12544]{2,1,0:T(8,128)}, f32[2,16,12544]{2,1,0:T(8,128)S(1)}, u32[]{:S(2)}, u32[]{:S(2)}) %collective-permute-start.1) | collective-permute-done | bytes 1605664 | tf_op jit(solution)/shard_map/ppermute | solution.py:214
  38.7 0.1 slice_bitcast_fusion
  38.8 1.6 %collective-permute-start.10 = (f32[16,12544]{1,0:T(8,128)S(1)}, f32[16,12544]{1,0:T(8,128)S(1)}, u32[]{:S(2)}, u32[]{:S(2)}) collective-permute-start(f32[16,12544]{1,0:T(8,128)S(1)} %slice_bitcast_fusion), channel_id=1, source_target_pairs={{0,4},{1,3},{2,6},{3,1},{4,0},{5,7},{6,2},{7,5},{8,12},{9,11},{10,... | collective-permute-start | bytes 2408456 | tf_op jit(solution)/shard_map/ppermute | solution.py:214
  40.4 0.0 collective-permute-start.4
  40.4 0.0 collective-permute-done.2.refs_4_.refs_13_
  40.4 0.5 collective-permute-start.3
  40.9 0.1 slice_bitcast_fusion.1
  41.0 0.0 collective-permute-done.5.refs_1_
  41.0 2.4 %collective-permute-start.9 = (f32[16,12544]{1,0:T(8,128)S(1)}, f32[16,12544]{1,0:T(8,128)S(1)}, u32[]{:S(2)}, u32[]{:S(2)}) collective-permute-start(f32[16,12544]{1,0:T(8,128)S(1)} %slice_bitcast_fusion.1), channel_id=1, source_target_pairs={{0,2},{1,5},{2,0},{3,7},{4,6},{5,1},{6,4},{7,3},{8,10},{9,13},{10,... | collective-permute-start | bytes 2408456 | tf_op jit(solution)/shard_map/ppermute | solution.py:214
  43.4 0.0 copy-done.2
  43.4 0.2 shard_map.37.refs_4_
  43.6 0.0 collective-permute-done.refs_1_.refs_10_
  43.6 0.2 collective-permute-done.4.refs_5_.refs_14_
  43.8 2.3 %collective-permute-done.3.refs_3_.refs_12_ = f32[2,16,12544]{2,1,0:T(8,128)S(1)} collective-permute-done((f32[2,16,12544]{2,1,0:T(8,128)S(1)}, f32[2,16,12544]{2,1,0:T(8,128)S(1)}, u32[]{:S(2)}, u32[]{:S(2)}) %collective-permute-start.3) | collective-permute-done | bytes 1605664 | tf_op jit(solution)/shard_map/ppermute | solution.py:214
  46.1 0.0 copy-done.1
  46.1 0.0 copy-done
  46.1 3.6 %shard_map.38.refs_0_ = f32[96,128]{1,0:T(8,128)S(1)} custom-call(f32[32,12544]{1,0:T(8,128)S(1)} %copy-done, f32[2,16,12544]{2,1,0:T(8,128)S(1)} %copy-done.1, f32[2,16,12544]{2,1,0:T(8,128)S(1)} %collective-permute-done.refs_1_.refs_10_, f32[2,16,12544]{2,1,0:T(8,128)S(1)} %collective-permute-done.1.refs_2_.refs_11_, ...), custom_call_target="tpu_custom_call" | custom-call | flops 1 | bytes 1 | tf_op jit(solution)/shard_map/pallas_call | solution.py:173
  49.7 2.6 %collective-permute-start.8 = (f32[96,128]{1,0:T(8,128)S(1)}, f32[96,128]{1,0:T(8,128)S(1)}, u32[]{:S(2)}, u32[]{:S(2)}) collective-permute-start(f32[96,128]{1,0:T(8,128)S(1)} %shard_map.38.refs_0_), channel_id=1, source_target_pairs={{0,16},{8,24},{16,0},{24,8},{1,17},{9,25},{17,1},{25,9},{2,18},{10... | collective-permute-start | bytes 147464 | tf_op jit(solution)/shard_map/ppermute | solution.py:214
  52.3 1.4 %collective-permute-start.7 = (f32[96,128]{1,0:T(8,128)S(1)}, f32[96,128]{1,0:T(8,128)S(1)}, u32[]{:S(2)}, u32[]{:S(2)}) collective-permute-start(f32[96,128]{1,0:T(8,128)S(1)} %shard_map.38.refs_0_), channel_id=1, source_target_pairs={{0,24},{8,16},{16,8},{24,0},{1,25},{9,17},{17,9},{25,1},{2,26},{10... | collective-permute-start | bytes 147464 | tf_op jit(solution)/shard_map/ppermute | solution.py:214
  53.7 0.2 collective-permute-start.6
  53.9 4.6 %collective-permute-done.10.refs_2_.refs_17_ = f32[16,12544]{1,0:T(8,128)S(1)} collective-permute-done((f32[16,12544]{1,0:T(8,128)S(1)}, f32[16,12544]{1,0:T(8,128)S(1)}, u32[]{:S(2)}, u32[]{:S(2)}) %collective-permute-start.10) | collective-permute-done | bytes 802848 | tf_op jit(solution)/shard_map/ppermute | solution.py:214
  58.5 0.0 collective-permute-done.9.refs_0_.refs_15_
  58.5 0.0 collective-permute-done.8.refs_3_
  58.5 0.0 collective-permute-done.7.refs_2_
  58.5 0.0 collective-permute-done.6.refs_1_
  58.5 1.0 %collective-permute-start.11 = (f32[16,12544]{1,0:T(8,128)S(1)}, f32[16,12544]{1,0:T(8,128)S(1)}, u32[]{:S(2)}, u32[]{:S(2)}) collective-permute-start(f32[16,12544]{1,0:T(8,128)S(1)} %collective-permute-done.9.refs_0_.refs_15_), channel_id=1, source_target_pairs={{0,1},{1,0},{2,3},{3,2},{4,5},{5,4},{6,7},{7,6},{8,9},{9,8},{10,11... | collective-permute-start | bytes 2408456 | tf_op jit(solution)/shard_map/ppermute | solution.py:214
  59.5 0.1 collective-permute-start.12
  59.6 3.9 %collective-permute-start.18 = (f32[96,128]{1,0:T(8,128)S(1)}, f32[96,128]{1,0:T(8,128)S(1)}, u32[]{:S(2)}, u32[]{:S(2)}) collective-permute-start(f32[96,128]{1,0:T(8,128)S(1)} %get-tuple-element.37.refs_0_), channel_id=1, source_target_pairs={{0,6},{1,7},{2,4},{3,5},{4,2},{5,3},{6,0},{7,1},{8,14},{9,15},{10,... | collective-permute-start | bytes 147464 | tf_op jit(solution)/shard_map/ppermute | solution.py:214
  63.5 0.0 collective-permute-start.17
  63.5 0.6 collective-permute-start.16
  64.1 0.0 collective-permute-done.11.refs_1_.refs_16_
  64.1 0.0 collective-permute-done.12.refs_3_.refs_18_
  64.1 1.1 %shard_map.40.refs_1_ = f32[16,128]{1,0:T(8,128)S(1)} custom-call(f32[32,12544]{1,0:T(8,128)S(1)} %copy-done, f32[16,12544]{1,0:T(8,128)S(1)} %collective-permute-done.9.refs_0_.refs_15_, f32[16,12544]{1,0:T(8,128)S(1)} %collective-permute-done.11.refs_1_.refs_16_, f32[16,12544]{1,0:T(8,128)S(1)} %collective-permute-done.10.refs_2_.refs_17_, ...), custom_call_target="tpu_custom_call" | custom-call | flops 1 | bytes 1 | tf_op jit(solution)/shard_map/pallas_call | solution.py:173
  65.3 2.6 %collective-permute-start.15 = (f32[16,128]{1,0:T(8,128)S(1)}, f32[16,128]{1,0:T(8,128)S(1)}, u32[]{:S(2)}, u32[]{:S(2)}) collective-permute-start(f32[16,128]{1,0:T(8,128)S(1)} %shard_map.40.refs_1_), channel_id=1, source_target_pairs={{0,16},{8,24},{16,0},{24,8},{1,17},{9,25},{17,1},{25,9},{2,18},{10... | collective-permute-start | bytes 24584 | tf_op jit(solution)/shard_map/ppermute | solution.py:214
  67.9 1.3 %collective-permute-start.14 = (f32[16,128]{1,0:T(8,128)S(1)}, f32[16,128]{1,0:T(8,128)S(1)}, u32[]{:S(2)}, u32[]{:S(2)}) collective-permute-start(f32[16,128]{1,0:T(8,128)S(1)} %shard_map.40.refs_1_), channel_id=1, source_target_pairs={{0,24},{8,16},{16,8},{24,0},{1,25},{9,17},{17,9},{25,1},{2,26},{10... | collective-permute-start | bytes 24584 | tf_op jit(solution)/shard_map/ppermute | solution.py:214
  69.2 0.0 collective-permute-done.18.refs_3_
  69.2 0.2 collective-permute-start.13
  69.4 0.0 collective-permute-done.17.refs_2_
  69.5 0.0 collective-permute-done.16.refs_1_
  69.5 0.3 shard_map.41
  69.8 0.1 collective-permute-done.15.refs_4_
  69.8 3.5 %collective-permute-done.14.refs_3_ = f32[16,128]{1,0:T(8,128)S(1)} collective-permute-done((f32[16,128]{1,0:T(8,128)S(1)}, f32[16,128]{1,0:T(8,128)S(1)}, u32[]{:S(2)}, u32[]{:S(2)}) %collective-permute-start.14) | collective-permute-done | bytes 8224 | tf_op jit(solution)/shard_map/ppermute | solution.py:214
  73.3 0.0 collective-permute-done.13.refs_2_
  73.3 3.9 %shard_map.42 = f32[32,12544]{1,0:T(8,128)} custom-call(f32[64,128]{1,0:T(8,128)S(1)} %get-tuple-element.34.refs_0_, f32[16,128]{1,0:T(8,128)S(1)} %shard_map.40.refs_1_, f32[16,128]{1,0:T(8,128)S(1)} %collective-permute-done.13.refs_2_, f32[16,128]{1,0:T(8,128)S(1)} %collective-permute-done.14.refs_3_, f32[16,128]{1,0:T(8,128)S(1)} %collective-permute-done.15.refs_4_, ...), custom_call_target="tpu_custom_call" | custom-call | flops 1 | bytes 1 | tf_op jit(solution)/shard_map/pallas_call | solution.py:195
  (1 shorter events, 0.0 us)
Async XLA Ops:
  0.0 46.1 %copy-start.1 = (f32[2,16,12544]{2,1,0:T(8,128)S(1)}, f32[2,16,12544]{2,1,0:T(8,128)}, u32[]{:S(2)}) copy-start(f32[2,16,12544]{2,1,0:T(8,128)} %refs_9_) | copy-start | bytes 4816900
  0.0 43.4 %copy-start.2 = (f32[2,16,128]{2,1,0:T(8,128)S(1)}, f32[2,16,128]{2,1,0:T(8,128)}, u32[]{:S(2)}) copy-start(f32[2,16,128]{2,1,0:T(8,128)} %refs_0_.1) | copy-start | bytes 49156
  0.0 46.1 %copy-start = (f32[32,12544]{1,0:T(8,128)S(1)}, f32[32,12544]{1,0:T(8,128)}, u32[]{:S(2)}) copy-start(f32[32,12544]{1,0:T(8,128)} %refs_8_.1) | copy-start | bytes 4816900
  0.0 38.7 %collective-permute-start.1 = (f32[2,16,12544]{2,1,0:T(8,128)}, f32[2,16,12544]{2,1,0:T(8,128)S(1)}, u32[]{:S(2)}, u32[]{:S(2)}) collective-permute-start(f32[2,16,12544]{2,1,0:T(8,128)} %refs_9_), channel_id=1, source_target_pairs={{0,2},{1,5},{2,0},{3,7},{4,6},{5,1},{6,4},{7,3},{8,10},{9,13},{10,... | collective-permute-start | bytes 4816904 | tf_op jit(solution)/shard_map/ppermute | solution.py:214
  3.0 40.6 %collective-permute-start = (f32[2,16,12544]{2,1,0:T(8,128)}, f32[2,16,12544]{2,1,0:T(8,128)S(1)}, u32[]{:S(2)}, u32[]{:S(2)}) collective-permute-start(f32[2,16,12544]{2,1,0:T(8,128)} %refs_9_), channel_id=1, source_target_pairs={{0,1},{1,0},{2,3},{3,2},{4,5},{5,4},{6,7},{7,6},{8,9},{9,8},{10,11... | collective-permute-start | bytes 4816904 | tf_op jit(solution)/shard_map/ppermute | solution.py:214
  3.0 37.4 %collective-permute-start.2 = (f32[2,16,12544]{2,1,0:T(8,128)}, f32[2,16,12544]{2,1,0:T(8,128)S(1)}, u32[]{:S(2)}, u32[]{:S(2)}) collective-permute-start(f32[2,16,12544]{2,1,0:T(8,128)} %refs_9_), channel_id=1, source_target_pairs={{0,4},{1,3},{2,6},{3,1},{4,0},{5,7},{6,2},{7,5},{8,12},{9,11},{10,... | collective-permute-start | bytes 4816904 | tf_op jit(solution)/shard_map/ppermute | solution.py:214
  4.5 36.4 %collective-permute-start.5 = (f32[2,16,128]{2,1,0:T(8,128)}, f32[2,16,128]{2,1,0:T(8,128)S(1)}, u32[]{:S(2)}, u32[]{:S(2)}) collective-permute-start(f32[2,16,128]{2,1,0:T(8,128)} %refs_0_.1), channel_id=1, source_target_pairs={{0,1},{1,0},{2,3},{3,2},{4,5},{5,4},{6,7},{7,6},{8,9},{9,8},{10,11... | collective-permute-start | bytes 49160 | tf_op jit(solution)/shard_map/ppermute | solution.py:214
  38.8 19.7 %collective-permute-start.10 = (f32[16,12544]{1,0:T(8,128)S(1)}, f32[16,12544]{1,0:T(8,128)S(1)}, u32[]{:S(2)}, u32[]{:S(2)}) collective-permute-start(f32[16,12544]{1,0:T(8,128)S(1)} %slice_bitcast_fusion), channel_id=1, source_target_pairs={{0,4},{1,3},{2,6},{3,1},{4,0},{5,7},{6,2},{7,5},{8,12},{9,11},{10,... | collective-permute-start | bytes 2408456 | tf_op jit(solution)/shard_map/ppermute | solution.py:214
  40.4 3.5 %collective-permute-start.4 = (f32[2,16,12544]{2,1,0:T(8,128)S(1)}, f32[2,16,12544]{2,1,0:T(8,128)S(1)}, u32[]{:S(2)}, u32[]{:S(2)}) collective-permute-start(f32[2,16,12544]{2,1,0:T(8,128)S(1)} %collective-permute-done.1.refs_2_.refs_11_), channel_id=1, source_target_pairs={{0,1},{1,0},{2,3},{3,2},{4,5},{5,4},{6,7},{7,6},{8,9},{9,8},{10,11... | collective-permute-start | bytes 4816904 | tf_op jit(solution)/shard_map/ppermute | solution.py:214
  40.4 5.7 %collective-permute-start.3 = (f32[2,16,12544]{2,1,0:T(8,128)S(1)}, f32[2,16,12544]{2,1,0:T(8,128)S(1)}, u32[]{:S(2)}, u32[]{:S(2)}) collective-permute-start(f32[2,16,12544]{2,1,0:T(8,128)S(1)} %collective-permute-done.2.refs_4_.refs_13_), channel_id=1, source_target_pairs={{0,1},{1,0},{2,3},{3,2},{4,5},{5,4},{6,7},{7,6},{8,9},{9,8},{10,11... | collective-permute-start | bytes 4816904 | tf_op jit(solution)/shard_map/ppermute | solution.py:214
  41.0 17.5 %collective-permute-start.9 = (f32[16,12544]{1,0:T(8,128)S(1)}, f32[16,12544]{1,0:T(8,128)S(1)}, u32[]{:S(2)}, u32[]{:S(2)}) collective-permute-start(f32[16,12544]{1,0:T(8,128)S(1)} %slice_bitcast_fusion.1), channel_id=1, source_target_pairs={{0,2},{1,5},{2,0},{3,7},{4,6},{5,1},{6,4},{7,3},{8,10},{9,13},{10,... | collective-permute-start | bytes 2408456 | tf_op jit(solution)/shard_map/ppermute | solution.py:214
  49.7 8.8 %collective-permute-start.8 = (f32[96,128]{1,0:T(8,128)S(1)}, f32[96,128]{1,0:T(8,128)S(1)}, u32[]{:S(2)}, u32[]{:S(2)}) collective-permute-start(f32[96,128]{1,0:T(8,128)S(1)} %shard_map.38.refs_0_), channel_id=1, source_target_pairs={{0,16},{8,24},{16,0},{24,8},{1,17},{9,25},{17,1},{25,9},{2,18},{10... | collective-permute-start | bytes 147464 | tf_op jit(solution)/shard_map/ppermute | solution.py:214
  52.3 6.2 %collective-permute-start.7 = (f32[96,128]{1,0:T(8,128)S(1)}, f32[96,128]{1,0:T(8,128)S(1)}, u32[]{:S(2)}, u32[]{:S(2)}) collective-permute-start(f32[96,128]{1,0:T(8,128)S(1)} %shard_map.38.refs_0_), channel_id=1, source_target_pairs={{0,24},{8,16},{16,8},{24,0},{1,25},{9,17},{17,9},{25,1},{2,26},{10... | collective-permute-start | bytes 147464 | tf_op jit(solution)/shard_map/ppermute | solution.py:214
  53.7 4.8 %collective-permute-start.6 = (f32[96,128]{1,0:T(8,128)S(1)}, f32[96,128]{1,0:T(8,128)S(1)}, u32[]{:S(2)}, u32[]{:S(2)}) collective-permute-start(f32[96,128]{1,0:T(8,128)S(1)} %shard_map.38.refs_0_), channel_id=1, source_target_pairs={{0,8},{8,0},{16,24},{24,16},{1,9},{9,1},{17,25},{25,17},{2,10},{10... | collective-permute-start | bytes 147464 | tf_op jit(solution)/shard_map/ppermute | solution.py:214
  58.5 5.6 %collective-permute-start.11 = (f32[16,12544]{1,0:T(8,128)S(1)}, f32[16,12544]{1,0:T(8,128)S(1)}, u32[]{:S(2)}, u32[]{:S(2)}) collective-permute-start(f32[16,12544]{1,0:T(8,128)S(1)} %collective-permute-done.9.refs_0_.refs_15_), channel_id=1, source_target_pairs={{0,1},{1,0},{2,3},{3,2},{4,5},{5,4},{6,7},{7,6},{8,9},{9,8},{10,11... | collective-permute-start | bytes 2408456 | tf_op jit(solution)/shard_map/ppermute | solution.py:214
  59.5 4.6 %collective-permute-start.12 = (f32[16,12544]{1,0:T(8,128)S(1)}, f32[16,12544]{1,0:T(8,128)S(1)}, u32[]{:S(2)}, u32[]{:S(2)}) collective-permute-start(f32[16,12544]{1,0:T(8,128)S(1)} %collective-permute-done.10.refs_2_.refs_17_), channel_id=1, source_target_pairs={{0,1},{1,0},{2,3},{3,2},{4,5},{5,4},{6,7},{7,6},{8,9},{9,8},{10,11... | collective-permute-start | bytes 2408456 | tf_op jit(solution)/shard_map/ppermute | solution.py:214
  59.6 9.6 %collective-permute-start.18 = (f32[96,128]{1,0:T(8,128)S(1)}, f32[96,128]{1,0:T(8,128)S(1)}, u32[]{:S(2)}, u32[]{:S(2)}) collective-permute-start(f32[96,128]{1,0:T(8,128)S(1)} %get-tuple-element.37.refs_0_), channel_id=1, source_target_pairs={{0,6},{1,7},{2,4},{3,5},{4,2},{5,3},{6,0},{7,1},{8,14},{9,15},{10,... | collective-permute-start | bytes 147464 | tf_op jit(solution)/shard_map/ppermute | solution.py:214
  63.5 6.0 %collective-permute-start.17 = (f32[96,128]{1,0:T(8,128)S(1)}, f32[96,128]{1,0:T(8,128)S(1)}, u32[]{:S(2)}, u32[]{:S(2)}) collective-permute-start(f32[96,128]{1,0:T(8,128)S(1)} %get-tuple-element.37.refs_0_), channel_id=1, source_target_pairs={{0,4},{1,3},{2,6},{3,1},{4,0},{5,7},{6,2},{7,5},{8,12},{9,11},{10,... | collective-permute-start | bytes 147464 | tf_op jit(solution)/shard_map/ppermute | solution.py:214
  63.5 6.0 %collective-permute-start.16 = (f32[96,128]{1,0:T(8,128)S(1)}, f32[96,128]{1,0:T(8,128)S(1)}, u32[]{:S(2)}, u32[]{:S(2)}) collective-permute-start(f32[96,128]{1,0:T(8,128)S(1)} %get-tuple-element.37.refs_0_), channel_id=1, source_target_pairs={{0,2},{1,5},{2,0},{3,7},{4,6},{5,1},{6,4},{7,3},{8,10},{9,13},{10,... | collective-permute-start | bytes 147464 | tf_op jit(solution)/shard_map/ppermute | solution.py:214
  65.3 4.6 %collective-permute-start.15 = (f32[16,128]{1,0:T(8,128)S(1)}, f32[16,128]{1,0:T(8,128)S(1)}, u32[]{:S(2)}, u32[]{:S(2)}) collective-permute-start(f32[16,128]{1,0:T(8,128)S(1)} %shard_map.40.refs_1_), channel_id=1, source_target_pairs={{0,16},{8,24},{16,0},{24,8},{1,17},{9,25},{17,1},{25,9},{2,18},{10... | collective-permute-start | bytes 24584 | tf_op jit(solution)/shard_map/ppermute | solution.py:214
  67.9 5.4 %collective-permute-start.14 = (f32[16,128]{1,0:T(8,128)S(1)}, f32[16,128]{1,0:T(8,128)S(1)}, u32[]{:S(2)}, u32[]{:S(2)}) collective-permute-start(f32[16,128]{1,0:T(8,128)S(1)} %shard_map.40.refs_1_), channel_id=1, source_target_pairs={{0,24},{8,16},{16,8},{24,0},{1,25},{9,17},{17,9},{25,1},{2,26},{10... | collective-permute-start | bytes 24584 | tf_op jit(solution)/shard_map/ppermute | solution.py:214
  69.2 4.1 %collective-permute-start.13 = (f32[16,128]{1,0:T(8,128)S(1)}, f32[16,128]{1,0:T(8,128)S(1)}, u32[]{:S(2)}, u32[]{:S(2)}) collective-permute-start(f32[16,128]{1,0:T(8,128)S(1)} %shard_map.40.refs_1_), channel_id=1, source_target_pairs={{0,8},{8,0},{16,24},{24,16},{1,9},{9,1},{17,25},{25,17},{2,10},{10... | collective-permute-start | bytes 24584 | tf_op jit(solution)/shard_map/ppermute | solution.py:214

commit v4 on v0

--- a/solution.py
+++ b/solution.py
@@ -139,10 +139,9 @@
         triangle_refs[p][...] = jnp.concatenate(triangles[p], axis=0).T
 
 
-def update_kernel(pieces, terms, *refs):
+def update_kernel(terms, *refs):
     near_ref, term_refs, (between_ref, first_ref, second_ref) = refs[0], refs[1 : 1 + terms], refs[1 + terms : 4 + terms]
-    slab_ref, *vector_refs = refs[4 + terms : -3]
-    out_ref, after, sems = refs[-3:]
+    slab_ref, high_ref, low_ref, out_ref, after, sems = refs[4 + terms :]
     (rows, width), nb = slab_ref.shape, near_ref.shape[1]
     group = nb // 4
 
@@ -158,8 +157,7 @@
 
     copies = []
     for at, columns in enumerate(column_tiles(width, UNIT_LIMIT)):
-        blocks = [vector_refs[ref][:, columns] if p is None else vector_refs[ref][p, :, columns] for ref, p in pieces]
-        high, low = split(jnp.concatenate(blocks, axis=0))
+        high, low = high_ref[:, columns], low_ref[:, columns]
         main = dot(both, high, PLAIN)
         rest = dot(both[:rows], low, PLAIN)
         after[:, columns] = slab_ref[:, columns] - (main[:rows] + main[rows:] + rest)
@@ -167,6 +165,13 @@
         copies[-1].start()
     for copy in copies:
         copy.wait()
+
+
+def split_kernel(pieces, *refs):
+    vector_refs, high_ref, low_ref = refs[:-2], *refs[-2:]
+    for columns in column_tiles(high_ref.shape[1], UNIT_LIMIT):
+        blocks = [vector_refs[ref][:, columns] if p is None else vector_refs[ref][p, :, columns] for ref, p in pieces]
+        high_ref[:, columns], low_ref[:, columns] = split(jnp.concatenate(blocks, axis=0))
 
 
 def products(kernel, arrays, *shapes):
@@ -189,11 +194,11 @@
     )(*arrays)
 
 
-def update(near, terms, matrices, slab, arrays, pieces):
+def update(near, terms, matrices, slab, parts):
     width = slab.shape[1]
-    whole = [near, *terms, *matrices, slab, *arrays]
+    whole = [near, *terms, *matrices, slab, *parts]
     return pl.pallas_call(
-        functools.partial(update_kernel, pieces, len(terms)),
+        functools.partial(update_kernel, len(terms)),
         in_specs=[pl.BlockSpec(memory_space=pltpu.VMEM)] * len(whole),
         out_specs=pl.BlockSpec(memory_space=pl.ANY),
         out_shape=jax.ShapeDtypeStruct(slab.shape, jnp.float32),
@@ -264,7 +269,16 @@
     (found,) = products(corner_kernel, [slab, *far], (2 * rows // 4, nb))
     count, part = len(near), len(far) // PANELS
     pieces = [piece for p in range(PANELS) for piece in (*((at, p) for at in range(count)), *((count + p * part + at, None) for at in range(part)))]
-    return update(inner, summed_terms(found, depth, 4), matrices, slab, [*near, *far], pieces)
+    found, far = lax.optimization_barrier((found, far))
+    parts = pl.pallas_call(
+        functools.partial(split_kernel, pieces),
+        in_specs=[pl.BlockSpec(memory_space=pltpu.VMEM)] * len([*near, *far]),
+        out_specs=[pl.BlockSpec(memory_space=pltpu.VMEM)] * 2,
+        out_shape=[jax.ShapeDtypeStruct((PANELS * nb, slab.shape[1]), jnp.bfloat16)] * 2,
+        compiler_params=pltpu.CompilerParams(vmem_limit_bytes=SMALL_LIMIT),
+        cost_estimate=pl.CostEstimate(flops=1, bytes_accessed=16 * PANELS * nb * slab.shape[1], transcendentals=0),
+    )(*near, *far)
+    return update(inner, summed_terms(found, depth, 4), matrices, slab, parts)
 
 
 def solution(mesh):

time: 77.5 us -> 79 us (1.019)
  starting transfers between devices: 23.5 us -> 21.8 us
  waiting for transfers between devices: 44.5 us -> 46.1 us
  Pallas kernels: 9.17 us -> 10.7 us
    ppermute x19, starting transfers between devices: 23.5 us -> 21.8 us  [exchange(): return lax.ppermute(array, axis, [(i, i ^ partner(i)) for i in range(size)])]
    pallas_call x1 -> x2, Pallas kernels: 3.94 us -> 5.54 us  [the longest x1 3.74 us: update(): pl.pallas_call(functools.partial(update_kernel, len(terms)), in_specs=[pl...]
    ppermute x19, waiting for transfers between devices: 44.5 us -> 46.1 us  [exchange(): return lax.ppermute(array, axis, [(i, i ^ partner(i)) for i in range(size)])]
  transfers between devices with their start and end apart: 19 -> 19, of which waited for: 6 -> 5; matrix products, arithmetic and copies ran while one was open for 0% -> 0% of each run, Pallas kernels for 7% -> 9%
where the time goes in v4:
time: 79 us; the launch traced here: 78.8 us
  waiting for transfers between devices  46.1 us (58%)
  starting transfers between devices  21.8 us (28%)
  Pallas kernels  10.7 us (14%)
    ppermute x19, waiting for transfers between devices, exchange(): return lax.ppermute(array, axis, [(i, i ^ partner(i)) for i in range(size)])  46.1 us
    ppermute x19, starting transfers between devices, exchange(): return lax.ppermute(array, axis, [(i, i ^ partner(i)) for i in range(size)])  21.8 us
    pallas_call x2, Pallas kernels, products(): pl.pallas_call(kernel, in_specs=[pl.BlockSpec(memory_space=pltpu.VMEM)] *...  4.69 us
    pallas_call x1, Pallas kernels, update(): pl.pallas_call(functools.partial(update_kernel, len(terms)), in_specs=[pl...  3.74 us
    pallas_call x1, Pallas kernels, body(): pl.pallas_call(functools.partial(split_kernel, pieces), in_specs=[pl.Bloc...  1.8 us
  transfers between devices with their start and end apart: 19, of which 5 were waited for; matrix products, arithmetic and copies ran while one was open for 0% of the time, Pallas kernels for 9%

profile of v4, /device:TPU:0, one launch (start us, length us, event | category | flops | bytes accessed | tf_op | source)
XLA Modules:
  0.0 78.8 jit_solution(903640935173529836)
XLA Ops:
  0.0 0.0 copy-start.1
  0.0 0.0 copy-start.2
  0.0 0.0 copy-start
  0.0 3.0 %collective-permute-start.1 = (f32[2,16,12544]{2,1,0:T(8,128)}, f32[2,16,12544]{2,1,0:T(8,128)S(1)}, u32[]{:S(2)}, u32[]{:S(2)}) collective-permute-start(f32[2,16,12544]{2,1,0:T(8,128)} %refs_0_.3), channel_id=1, source_target_pairs={{0,2},{1,5},{2,0},{3,7},{4,6},{5,1},{6,4},{7,3},{8,10},{9,13},{10,... | collective-permute-start | bytes 4816904 | tf_op jit(solution)/shard_map/ppermute | solution.py:219
  3.0 1.5 %collective-permute-start.2 = (f32[2,16,12544]{2,1,0:T(8,128)}, f32[2,16,12544]{2,1,0:T(8,128)S(1)}, u32[]{:S(2)}, u32[]{:S(2)}) collective-permute-start(f32[2,16,12544]{2,1,0:T(8,128)} %refs_0_.3), channel_id=1, source_target_pairs={{0,4},{1,3},{2,6},{3,1},{4,0},{5,7},{6,2},{7,5},{8,12},{9,11},{10,... | collective-permute-start | bytes 4816904 | tf_op jit(solution)/shard_map/ppermute | solution.py:219
  4.5 0.0 collective-permute-start
  4.5 0.5 collective-permute-start.5
  5.0 33.7 %collective-permute-done.1.refs_2_ = f32[2,16,12544]{2,1,0:T(8,128)S(1)} collective-permute-done((f32[2,16,12544]{2,1,0:T(8,128)}, f32[2,16,12544]{2,1,0:T(8,128)S(1)}, u32[]{:S(2)}, u32[]{:S(2)}) %collective-permute-start.1) | collective-permute-done | bytes 1605664 | tf_op jit(solution)/shard_map/ppermute | solution.py:219
  38.7 0.1 slice_bitcast_fusion
  38.8 1.5 %collective-permute-start.10 = (f32[16,12544]{1,0:T(8,128)S(1)}, f32[16,12544]{1,0:T(8,128)S(1)}, u32[]{:S(2)}, u32[]{:S(2)}) collective-permute-start(f32[16,12544]{1,0:T(8,128)S(1)} %slice_bitcast_fusion), channel_id=1, source_target_pairs={{0,4},{1,3},{2,6},{3,1},{4,0},{5,7},{6,2},{7,5},{8,12},{9,11},{10,... | collective-permute-start | bytes 2408456 | tf_op jit(solution)/shard_map/ppermute | solution.py:219
  40.3 0.0 collective-permute-start.4
  40.3 0.0 collective-permute-done.2.refs_4_
  40.3 0.5 collective-permute-start.3
  40.8 0.1 slice_bitcast_fusion.1
  40.9 0.0 collective-permute-done.5.refs_1_
  40.9 1.7 %collective-permute-start.9 = (f32[16,12544]{1,0:T(8,128)S(1)}, f32[16,12544]{1,0:T(8,128)S(1)}, u32[]{:S(2)}, u32[]{:S(2)}) collective-permute-start(f32[16,12544]{1,0:T(8,128)S(1)} %slice_bitcast_fusion.1), channel_id=1, source_target_pairs={{0,2},{1,5},{2,0},{3,7},{4,6},{5,1},{6,4},{7,3},{8,10},{9,13},{10,... | collective-permute-start | bytes 2408456 | tf_op jit(solution)/shard_map/ppermute | solution.py:219
  42.6 0.0 copy-done.2
  42.6 0.2 shard_map.37.refs_4_
  42.8 0.0 collective-permute-done.refs_1_
  42.8 3.3 %collective-permute-done.3.refs_3_ = f32[2,16,12544]{2,1,0:T(8,128)S(1)} collective-permute-done((f32[2,16,12544]{2,1,0:T(8,128)S(1)}, f32[2,16,12544]{2,1,0:T(8,128)S(1)}, u32[]{:S(2)}, u32[]{:S(2)}) %collective-permute-start.3) | collective-permute-done | bytes 1605664 | tf_op jit(solution)/shard_map/ppermute | solution.py:219
  46.0 0.0 collective-permute-done.4.refs_5_
  46.0 0.0 copy-done.1
  46.0 0.0 copy-done
  46.1 3.6 %shard_map.38.refs_0_ = f32[96,128]{1,0:T(8,128)S(1)} custom-call(f32[32,12544]{1,0:T(8,128)S(1)} %copy-done, f32[2,16,12544]{2,1,0:T(8,128)S(1)} %copy-done.1, f32[2,16,12544]{2,1,0:T(8,128)S(1)} %collective-permute-done.refs_1_, f32[2,16,12544]{2,1,0:T(8,128)S(1)} %collective-permute-done.1.refs_2_, f32[2,16,12544]{2,1,0:T(8,128)S(1)} %collective-permute-done.3.refs_3_, ...), custom_call_target="tpu_custom_call" | custom-call | flops 1 | bytes 1 | tf_op jit(solution)/shard_map/pallas_call | solution.py:178
  49.6 1.8 %collective-permute-start.6 = (f32[96,128]{1,0:T(8,128)S(1)}, f32[96,128]{1,0:T(8,128)S(1)}, u32[]{:S(2)}, u32[]{:S(2)}) collective-permute-start(f32[96,128]{1,0:T(8,128)S(1)} %shard_map.38.refs_0_), channel_id=1, source_target_pairs={{0,8},{8,0},{16,24},{24,16},{1,9},{9,1},{17,25},{25,17},{2,10},{10... | collective-permute-start | bytes 147464 | tf_op jit(solution)/shard_map/ppermute | solution.py:219
  51.4 2.6 %collective-permute-start.7 = (f32[96,128]{1,0:T(8,128)S(1)}, f32[96,128]{1,0:T(8,128)S(1)}, u32[]{:S(2)}, u32[]{:S(2)}) collective-permute-start(f32[96,128]{1,0:T(8,128)S(1)} %shard_map.38.refs_0_), channel_id=1, source_target_pairs={{0,16},{8,24},{16,0},{24,8},{1,17},{9,25},{17,1},{25,9},{2,18},{10... | collective-permute-start | bytes 147464 | tf_op jit(solution)/shard_map/ppermute | solution.py:219
  54.0 0.1 collective-permute-start.8
  54.0 4.4 %collective-permute-done.10.refs_2_.refs_8_ = f32[16,12544]{1,0:T(8,128)S(1)} collective-permute-done((f32[16,12544]{1,0:T(8,128)S(1)}, f32[16,12544]{1,0:T(8,128)S(1)}, u32[]{:S(2)}, u32[]{:S(2)}) %collective-permute-start.10) | collective-permute-done | bytes 802848 | tf_op jit(solution)/shard_map/ppermute | solution.py:219
  58.4 0.0 collective-permute-done.9.refs_0_.refs_6_
  58.4 0.0 collective-permute-done.6.refs_1_
  58.4 0.0 collective-permute-done.7.refs_2_
  58.5 1.4 %collective-permute-done.8.refs_3_ = f32[96,128]{1,0:T(8,128)S(1)} collective-permute-done((f32[96,128]{1,0:T(8,128)S(1)}, f32[96,128]{1,0:T(8,128)S(1)}, u32[]{:S(2)}, u32[]{:S(2)}) %collective-permute-start.8) | collective-permute-done | bytes 49184 | tf_op jit(solution)/shard_map/ppermute | solution.py:219
  59.9 0.0 collective-permute-start.11
  59.9 0.5 collective-permute-start.12
  60.4 1.9 %collective-permute-start.16 = (f32[96,128]{1,0:T(8,128)S(1)}, f32[96,128]{1,0:T(8,128)S(1)}, u32[]{:S(2)}, u32[]{:S(2)}) collective-permute-start(f32[96,128]{1,0:T(8,128)S(1)} %get-tuple-element.45.refs_0_), channel_id=1, source_target_pairs={{0,2},{1,5},{2,0},{3,7},{4,6},{5,1},{6,4},{7,3},{8,10},{9,13},{10,... | collective-permute-start | bytes 147464 | tf_op jit(solution)/shard_map/ppermute | solution.py:219
  62.3 0.9 %collective-permute-start.17 = (f32[96,128]{1,0:T(8,128)S(1)}, f32[96,128]{1,0:T(8,128)S(1)}, u32[]{:S(2)}, u32[]{:S(2)}) collective-permute-start(f32[96,128]{1,0:T(8,128)S(1)} %get-tuple-element.45.refs_0_), channel_id=1, source_target_pairs={{0,4},{1,3},{2,6},{3,1},{4,0},{5,7},{6,2},{7,5},{8,12},{9,11},{10,... | collective-permute-start | bytes 147464 | tf_op jit(solution)/shard_map/ppermute | solution.py:219
  63.3 0.7 collective-permute-start.18
  63.9 0.0 collective-permute-done.11.refs_1_.refs_7_
  64.0 0.0 collective-permute-done.12.refs_3_.refs_9_
  64.0 1.1 %shard_map.40.refs_1_ = f32[16,128]{1,0:T(8,128)S(1)} custom-call(f32[32,12544]{1,0:T(8,128)S(1)} %copy-done, f32[16,12544]{1,0:T(8,128)S(1)} %collective-permute-done.9.refs_0_.refs_6_, f32[16,12544]{1,0:T(8,128)S(1)} %collective-permute-done.11.refs_1_.refs_7_, f32[16,12544]{1,0:T(8,128)S(1)} %collective-permute-done.10.refs_2_.refs_8_, ...), custom_call_target="tpu_custom_call" | custom-call | flops 1 | bytes 1 | tf_op jit(solution)/shard_map/pallas_call | solution.py:178
  65.1 2.0 %collective-permute-start.13 = (f32[16,128]{1,0:T(8,128)S(1)}, f32[16,128]{1,0:T(8,128)S(1)}, u32[]{:S(2)}, u32[]{:S(2)}) collective-permute-start(f32[16,128]{1,0:T(8,128)S(1)} %shard_map.40.refs_1_), channel_id=1, source_target_pairs={{0,8},{8,0},{16,24},{24,16},{1,9},{9,1},{17,25},{25,17},{2,10},{10... | collective-permute-start | bytes 24584 | tf_op jit(solution)/shard_map/ppermute | solution.py:219
  67.0 2.6 %collective-permute-start.14 = (f32[16,128]{1,0:T(8,128)S(1)}, f32[16,128]{1,0:T(8,128)S(1)}, u32[]{:S(2)}, u32[]{:S(2)}) collective-permute-start(f32[16,128]{1,0:T(8,128)S(1)} %shard_map.40.refs_1_), channel_id=1, source_target_pairs={{0,16},{8,24},{16,0},{24,8},{1,17},{9,25},{17,1},{25,9},{2,18},{10... | collective-permute-start | bytes 24584 | tf_op jit(solution)/shard_map/ppermute | solution.py:219
  69.6 0.0 collective-permute-done.16.refs_1_
  69.6 0.0 collective-permute-start.15
  69.6 0.0 collective-permute-done.17.refs_2_
  69.6 0.0 collective-permute-done.18.refs_3_
  69.7 0.3 shard_map.41
  70.0 1.8 %shard_map.42 = (bf16[256,12544]{1,0:T(8,128)(2,1)S(1)}, bf16[256,12544]{1,0:T(8,128)(2,1)S(1)}) custom-call(f32[2,16,12544]{2,1,0:T(8,128)S(1)} %copy-done.1, f32[2,16,12544]{2,1,0:T(8,128)S(1)} %collective-permute-done.refs_1_, f32[2,16,12544]{2,1,0:T(8,128)S(1)} %collective-permute-done.1.refs_2_, f32[2,16,12544]{2,1,0:T(8,128)S(1)} %collective-permute-done.3.refs_3_, ...), custom_call_target="tpu_custom_call" | custom-call | flops 1 | bytes 51380224 | tf_op jit(solution)/shard_map/pallas_call | solution.py:273
  71.8 0.0 collective-permute-done.13.refs_2_
  71.8 0.0 collective-permute-done.14.refs_3_
  71.8 3.3 %collective-permute-done.15.refs_4_ = f32[16,128]{1,0:T(8,128)S(1)} collective-permute-done((f32[16,128]{1,0:T(8,128)S(1)}, f32[16,128]{1,0:T(8,128)S(1)}, u32[]{:S(2)}, u32[]{:S(2)}) %collective-permute-start.15) | collective-permute-done | bytes 8224 | tf_op jit(solution)/shard_map/ppermute | solution.py:219
  75.1 3.7 %shard_map.43 = f32[32,12544]{1,0:T(8,128)} custom-call(f32[64,128]{1,0:T(8,128)S(1)} %get-tuple-element.41.refs_0_, f32[16,128]{1,0:T(8,128)S(1)} %shard_map.40.refs_1_, f32[16,128]{1,0:T(8,128)S(1)} %collective-permute-done.13.refs_2_, f32[16,128]{1,0:T(8,128)S(1)} %collective-permute-done.14.refs_3_, f32[16,128]{1,0:T(8,128)S(1)} %collective-permute-done.15.refs_4_, ...), custom_call_target="tpu_custom_call" | custom-call | flops 1 | bytes 1 | tf_op jit(solution)/shard_map/pallas_call | solution.py:200
  (1 shorter events, 0.0 us)
Async XLA Ops:
  0.0 46.0 %copy-start.1 = (f32[2,16,12544]{2,1,0:T(8,128)S(1)}, f32[2,16,12544]{2,1,0:T(8,128)}, u32[]{:S(2)}) copy-start(f32[2,16,12544]{2,1,0:T(8,128)} %refs_0_.3) | copy-start | bytes 4816900
  0.0 42.6 %copy-start.2 = (f32[2,16,128]{2,1,0:T(8,128)S(1)}, f32[2,16,128]{2,1,0:T(8,128)}, u32[]{:S(2)}) copy-start(f32[2,16,128]{2,1,0:T(8,128)} %refs_0_.1) | copy-start | bytes 49156
  0.0 46.0 %copy-start = (f32[32,12544]{1,0:T(8,128)S(1)}, f32[32,12544]{1,0:T(8,128)}, u32[]{:S(2)}) copy-start(f32[32,12544]{1,0:T(8,128)} %refs_8_.1) | copy-start | bytes 4816900
  0.0 38.7 %collective-permute-start.1 = (f32[2,16,12544]{2,1,0:T(8,128)}, f32[2,16,12544]{2,1,0:T(8,128)S(1)}, u32[]{:S(2)}, u32[]{:S(2)}) collective-permute-start(f32[2,16,12544]{2,1,0:T(8,128)} %refs_0_.3), channel_id=1, source_target_pairs={{0,2},{1,5},{2,0},{3,7},{4,6},{5,1},{6,4},{7,3},{8,10},{9,13},{10,... | collective-permute-start | bytes 4816904 | tf_op jit(solution)/shard_map/ppermute | solution.py:219
  3.0 37.3 %collective-permute-start.2 = (f32[2,16,12544]{2,1,0:T(8,128)}, f32[2,16,12544]{2,1,0:T(8,128)S(1)}, u32[]{:S(2)}, u32[]{:S(2)}) collective-permute-start(f32[2,16,12544]{2,1,0:T(8,128)} %refs_0_.3), channel_id=1, source_target_pairs={{0,4},{1,3},{2,6},{3,1},{4,0},{5,7},{6,2},{7,5},{8,12},{9,11},{10,... | collective-permute-start | bytes 4816904 | tf_op jit(solution)/shard_map/ppermute | solution.py:219
  4.5 38.2 %collective-permute-start = (f32[2,16,12544]{2,1,0:T(8,128)}, f32[2,16,12544]{2,1,0:T(8,128)S(1)}, u32[]{:S(2)}, u32[]{:S(2)}) collective-permute-start(f32[2,16,12544]{2,1,0:T(8,128)} %refs_0_.3), channel_id=1, source_target_pairs={{0,1},{1,0},{2,3},{3,2},{4,5},{5,4},{6,7},{7,6},{8,9},{9,8},{10,11... | collective-permute-start | bytes 4816904 | tf_op jit(solution)/shard_map/ppermute | solution.py:219
  4.5 36.3 %collective-permute-start.5 = (f32[2,16,128]{2,1,0:T(8,128)}, f32[2,16,128]{2,1,0:T(8,128)S(1)}, u32[]{:S(2)}, u32[]{:S(2)}) collective-permute-start(f32[2,16,128]{2,1,0:T(8,128)} %refs_0_.1), channel_id=1, source_target_pairs={{0,1},{1,0},{2,3},{3,2},{4,5},{5,4},{6,7},{7,6},{8,9},{9,8},{10,11... | collective-permute-start | bytes 49160 | tf_op jit(solution)/shard_map/ppermute | solution.py:219
  38.8 19.7 %collective-permute-start.10 = (f32[16,12544]{1,0:T(8,128)S(1)}, f32[16,12544]{1,0:T(8,128)S(1)}, u32[]{:S(2)}, u32[]{:S(2)}) collective-permute-start(f32[16,12544]{1,0:T(8,128)S(1)} %slice_bitcast_fusion), channel_id=1, source_target_pairs={{0,4},{1,3},{2,6},{3,1},{4,0},{5,7},{6,2},{7,5},{8,12},{9,11},{10,... | collective-permute-start | bytes 2408456 | tf_op jit(solution)/shard_map/ppermute | solution.py:219
  40.3 5.8 %collective-permute-start.4 = (f32[2,16,12544]{2,1,0:T(8,128)S(1)}, f32[2,16,12544]{2,1,0:T(8,128)S(1)}, u32[]{:S(2)}, u32[]{:S(2)}) collective-permute-start(f32[2,16,12544]{2,1,0:T(8,128)S(1)} %collective-permute-done.1.refs_2_), channel_id=1, source_target_pairs={{0,1},{1,0},{2,3},{3,2},{4,5},{5,4},{6,7},{7,6},{8,9},{9,8},{10,11... | collective-permute-start | bytes 4816904 | tf_op jit(solution)/shard_map/ppermute | solution.py:219
  40.3 5.7 %collective-permute-start.3 = (f32[2,16,12544]{2,1,0:T(8,128)S(1)}, f32[2,16,12544]{2,1,0:T(8,128)S(1)}, u32[]{:S(2)}, u32[]{:S(2)}) collective-permute-start(f32[2,16,12544]{2,1,0:T(8,128)S(1)} %collective-permute-done.2.refs_4_), channel_id=1, source_target_pairs={{0,1},{1,0},{2,3},{3,2},{4,5},{5,4},{6,7},{7,6},{8,9},{9,8},{10,11... | collective-permute-start | bytes 4816904 | tf_op jit(solution)/shard_map/ppermute | solution.py:219
  40.9 17.6 %collective-permute-start.9 = (f32[16,12544]{1,0:T(8,128)S(1)}, f32[16,12544]{1,0:T(8,128)S(1)}, u32[]{:S(2)}, u32[]{:S(2)}) collective-permute-start(f32[16,12544]{1,0:T(8,128)S(1)} %slice_bitcast_fusion.1), channel_id=1, source_target_pairs={{0,2},{1,5},{2,0},{3,7},{4,6},{5,1},{6,4},{7,3},{8,10},{9,13},{10,... | collective-permute-start | bytes 2408456 | tf_op jit(solution)/shard_map/ppermute | solution.py:219
  49.6 8.8 %collective-permute-start.6 = (f32[96,128]{1,0:T(8,128)S(1)}, f32[96,128]{1,0:T(8,128)S(1)}, u32[]{:S(2)}, u32[]{:S(2)}) collective-permute-start(f32[96,128]{1,0:T(8,128)S(1)} %shard_map.38.refs_0_), channel_id=1, source_target_pairs={{0,8},{8,0},{16,24},{24,16},{1,9},{9,1},{17,25},{25,17},{2,10},{10... | collective-permute-start | bytes 147464 | tf_op jit(solution)/shard_map/ppermute | solution.py:219
  51.4 7.1 %collective-permute-start.7 = (f32[96,128]{1,0:T(8,128)S(1)}, f32[96,128]{1,0:T(8,128)S(1)}, u32[]{:S(2)}, u32[]{:S(2)}) collective-permute-start(f32[96,128]{1,0:T(8,128)S(1)} %shard_map.38.refs_0_), channel_id=1, source_target_pairs={{0,16},{8,24},{16,0},{24,8},{1,17},{9,25},{17,1},{25,9},{2,18},{10... | collective-permute-start | bytes 147464 | tf_op jit(solution)/shard_map/ppermute | solution.py:219
  54.0 5.9 %collective-permute-start.8 = (f32[96,128]{1,0:T(8,128)S(1)}, f32[96,128]{1,0:T(8,128)S(1)}, u32[]{:S(2)}, u32[]{:S(2)}) collective-permute-start(f32[96,128]{1,0:T(8,128)S(1)} %shard_map.38.refs_0_), channel_id=1, source_target_pairs={{0,24},{8,16},{16,8},{24,0},{1,25},{9,17},{17,9},{25,1},{2,26},{10... | collective-permute-start | bytes 147464 | tf_op jit(solution)/shard_map/ppermute | solution.py:219
  59.9 4.1 %collective-permute-start.11 = (f32[16,12544]{1,0:T(8,128)S(1)}, f32[16,12544]{1,0:T(8,128)S(1)}, u32[]{:S(2)}, u32[]{:S(2)}) collective-permute-start(f32[16,12544]{1,0:T(8,128)S(1)} %collective-permute-done.9.refs_0_.refs_6_), channel_id=1, source_target_pairs={{0,1},{1,0},{2,3},{3,2},{4,5},{5,4},{6,7},{7,6},{8,9},{9,8},{10,11... | collective-permute-start | bytes 2408456 | tf_op jit(solution)/shard_map/ppermute | solution.py:219
  59.9 4.1 %collective-permute-start.12 = (f32[16,12544]{1,0:T(8,128)S(1)}, f32[16,12544]{1,0:T(8,128)S(1)}, u32[]{:S(2)}, u32[]{:S(2)}) collective-permute-start(f32[16,12544]{1,0:T(8,128)S(1)} %collective-permute-done.10.refs_2_.refs_8_), channel_id=1, source_target_pairs={{0,1},{1,0},{2,3},{3,2},{4,5},{5,4},{6,7},{7,6},{8,9},{9,8},{10,11... | collective-permute-start | bytes 2408456 | tf_op jit(solution)/shard_map/ppermute | solution.py:219
  60.4 9.2 %collective-permute-start.16 = (f32[96,128]{1,0:T(8,128)S(1)}, f32[96,128]{1,0:T(8,128)S(1)}, u32[]{:S(2)}, u32[]{:S(2)}) collective-permute-start(f32[96,128]{1,0:T(8,128)S(1)} %get-tuple-element.45.refs_0_), channel_id=1, source_target_pairs={{0,2},{1,5},{2,0},{3,7},{4,6},{5,1},{6,4},{7,3},{8,10},{9,13},{10,... | collective-permute-start | bytes 147464 | tf_op jit(solution)/shard_map/ppermute | solution.py:219
  62.3 7.3 %collective-permute-start.17 = (f32[96,128]{1,0:T(8,128)S(1)}, f32[96,128]{1,0:T(8,128)S(1)}, u32[]{:S(2)}, u32[]{:S(2)}) collective-permute-start(f32[96,128]{1,0:T(8,128)S(1)} %get-tuple-element.45.refs_0_), channel_id=1, source_target_pairs={{0,4},{1,3},{2,6},{3,1},{4,0},{5,7},{6,2},{7,5},{8,12},{9,11},{10,... | collective-permute-start | bytes 147464 | tf_op jit(solution)/shard_map/ppermute | solution.py:219
  63.3 6.4 %collective-permute-start.18 = (f32[96,128]{1,0:T(8,128)S(1)}, f32[96,128]{1,0:T(8,128)S(1)}, u32[]{:S(2)}, u32[]{:S(2)}) collective-permute-start(f32[96,128]{1,0:T(8,128)S(1)} %get-tuple-element.45.refs_0_), channel_id=1, source_target_pairs={{0,6},{1,7},{2,4},{3,5},{4,2},{5,3},{6,0},{7,1},{8,14},{9,15},{10,... | collective-permute-start | bytes 147464 | tf_op jit(solution)/shard_map/ppermute | solution.py:219
  65.1 6.7 %collective-permute-start.13 = (f32[16,128]{1,0:T(8,128)S(1)}, f32[16,128]{1,0:T(8,128)S(1)}, u32[]{:S(2)}, u32[]{:S(2)}) collective-permute-start(f32[16,128]{1,0:T(8,128)S(1)} %shard_map.40.refs_1_), channel_id=1, source_target_pairs={{0,8},{8,0},{16,24},{24,16},{1,9},{9,1},{17,25},{25,17},{2,10},{10... | collective-permute-start | bytes 24584 | tf_op jit(solution)/shard_map/ppermute | solution.py:219
  67.0 4.7 %collective-permute-start.14 = (f32[16,128]{1,0:T(8,128)S(1)}, f32[16,128]{1,0:T(8,128)S(1)}, u32[]{:S(2)}, u32[]{:S(2)}) collective-permute-start(f32[16,128]{1,0:T(8,128)S(1)} %shard_map.40.refs_1_), channel_id=1, source_target_pairs={{0,16},{8,24},{16,0},{24,8},{1,17},{9,25},{17,1},{25,9},{2,18},{10... | collective-permute-start | bytes 24584 | tf_op jit(solution)/shard_map/ppermute | solution.py:219
  69.6 5.4 %collective-permute-start.15 = (f32[16,128]{1,0:T(8,128)S(1)}, f32[16,128]{1,0:T(8,128)S(1)}, u32[]{:S(2)}, u32[]{:S(2)}) collective-permute-start(f32[16,128]{1,0:T(8,128)S(1)} %shard_map.40.refs_1_), channel_id=1, source_target_pairs={{0,24},{8,16},{16,8},{24,0},{1,25},{9,17},{17,9},{25,1},{2,26},{10... | collective-permute-start | bytes 24584 | tf_op jit(solution)/shard_map/ppermute | solution.py:219

commit v5 on v4

--- a/solution.py
+++ b/solution.py
@@ -219,12 +219,12 @@
     return lax.ppermute(array, axis, [(i, i ^ partner(i)) for i in range(size)])
 
 
-def summed_terms(value, depth, step):
+def summed_terms(value, depth, step, far_first=False):
     terms, reach = [value], 1
     while reach < depth:
         value = sum(terms[1:], terms[0])
         span = min(step, depth // reach)
-        terms = [value] + [exchange(value, lambda i, k=k: k * reach, depth, "prow") for k in range(1, span)]
+        terms = [value] + [exchange(value, lambda i, k=k: k * reach, depth, "prow") for k in (reversed(range(1, span)) if far_first else range(1, span))]
         reach *= span
     return terms
 
@@ -278,7 +278,7 @@
         compiler_params=pltpu.CompilerParams(vmem_limit_bytes=SMALL_LIMIT),
         cost_estimate=pl.CostEstimate(flops=1, bytes_accessed=16 * PANELS * nb * slab.shape[1], transcendentals=0),
     )(*near, *far)
-    return update(inner, summed_terms(found, depth, 4), matrices, slab, parts)
+    return update(inner, summed_terms(found, depth, 4, far_first=True), matrices, slab, parts)
 
 
 def solution(mesh):

time: 79 us -> 77.5 us (0.981)
  waiting for transfers between devices: 46.1 us -> 44.6 us
    ppermute x19, waiting for transfers between devices: 46.1 us -> 44.6 us  [exchange(): return lax.ppermute(array, axis, [(i, i ^ partner(i)) for i in range(size)])]
where the time goes in v5:
time: 77.5 us; the launch traced here: 77.4 us
  waiting for transfers between devices  44.6 us (58%)
  starting transfers between devices  21.9 us (28%)
  Pallas kernels  10.7 us (14%)
    ppermute x19, waiting for transfers between devices, exchange(): return lax.ppermute(array, axis, [(i, i ^ partner(i)) for i in range(size)])  44.6 us
    ppermute x19, starting transfers between devices, exchange(): return lax.ppermute(array, axis, [(i, i ^ partner(i)) for i in range(size)])  21.9 us
    pallas_call x2, Pallas kernels, products(): pl.pallas_call(kernel, in_specs=[pl.BlockSpec(memory_space=pltpu.VMEM)] *...  4.69 us
    pallas_call x1, Pallas kernels, update(): pl.pallas_call(functools.partial(update_kernel, len(terms)), in_specs=[pl...  3.74 us
    pallas_call x1, Pallas kernels, body(): pl.pallas_call(functools.partial(split_kernel, pieces), in_specs=[pl.Bloc...  1.8 us
  transfers between devices with their start and end apart: 19, of which 5 were waited for; matrix products, arithmetic and copies ran while one was open for 0% of the time, Pallas kernels for 9%

profile of v5, /device:TPU:0, one launch (start us, length us, event | category | flops | bytes accessed | tf_op | source)
XLA Modules:
  0.0 77.4 jit_solution(12459082647598802122)
XLA Ops:
  0.0 0.0 copy-start.1
  0.0 0.0 copy-start.2
  0.0 0.0 copy-start
  0.0 3.0 %collective-permute-start.1 = (f32[2,16,12544]{2,1,0:T(8,128)}, f32[2,16,12544]{2,1,0:T(8,128)S(1)}, u32[]{:S(2)}, u32[]{:S(2)}) collective-permute-start(f32[2,16,12544]{2,1,0:T(8,128)} %refs_0_.3), channel_id=1, source_target_pairs={{0,2},{1,5},{2,0},{3,7},{4,6},{5,1},{6,4},{7,3},{8,10},{9,13},{10,... | collective-permute-start | bytes 4816904 | tf_op jit(solution)/shard_map/ppermute | solution.py:219
  3.0 1.5 %collective-permute-start.2 = (f32[2,16,12544]{2,1,0:T(8,128)}, f32[2,16,12544]{2,1,0:T(8,128)S(1)}, u32[]{:S(2)}, u32[]{:S(2)}) collective-permute-start(f32[2,16,12544]{2,1,0:T(8,128)} %refs_0_.3), channel_id=1, source_target_pairs={{0,4},{1,3},{2,6},{3,1},{4,0},{5,7},{6,2},{7,5},{8,12},{9,11},{10,... | collective-permute-start | bytes 4816904 | tf_op jit(solution)/shard_map/ppermute | solution.py:219
  4.5 0.0 collective-permute-start
  4.5 0.5 collective-permute-start.5
  5.0 33.7 %collective-permute-done.1.refs_2_ = f32[2,16,12544]{2,1,0:T(8,128)S(1)} collective-permute-done((f32[2,16,12544]{2,1,0:T(8,128)}, f32[2,16,12544]{2,1,0:T(8,128)S(1)}, u32[]{:S(2)}, u32[]{:S(2)}) %collective-permute-start.1) | collective-permute-done | bytes 1605664 | tf_op jit(solution)/shard_map/ppermute | solution.py:219
  38.7 0.1 slice_bitcast_fusion
  38.8 1.5 %collective-permute-start.10 = (f32[16,12544]{1,0:T(8,128)S(1)}, f32[16,12544]{1,0:T(8,128)S(1)}, u32[]{:S(2)}, u32[]{:S(2)}) collective-permute-start(f32[16,12544]{1,0:T(8,128)S(1)} %slice_bitcast_fusion), channel_id=1, source_target_pairs={{0,4},{1,3},{2,6},{3,1},{4,0},{5,7},{6,2},{7,5},{8,12},{9,11},{10,... | collective-permute-start | bytes 2408456 | tf_op jit(solution)/shard_map/ppermute | solution.py:219
  40.3 0.0 collective-permute-start.4
  40.3 0.0 collective-permute-done.2.refs_4_
  40.3 0.5 collective-permute-start.3
  40.8 0.1 slice_bitcast_fusion.1
  40.9 0.0 collective-permute-done.5.refs_1_
  40.9 1.7 %collective-permute-start.9 = (f32[16,12544]{1,0:T(8,128)S(1)}, f32[16,12544]{1,0:T(8,128)S(1)}, u32[]{:S(2)}, u32[]{:S(2)}) collective-permute-start(f32[16,12544]{1,0:T(8,128)S(1)} %slice_bitcast_fusion.1), channel_id=1, source_target_pairs={{0,2},{1,5},{2,0},{3,7},{4,6},{5,1},{6,4},{7,3},{8,10},{9,13},{10,... | collective-permute-start | bytes 2408456 | tf_op jit(solution)/shard_map/ppermute | solution.py:219
  42.6 0.0 copy-done.2
  42.6 0.2 shard_map.37.refs_4_
  42.8 0.0 collective-permute-done.refs_1_
  42.8 3.3 %collective-permute-done.3.refs_3_ = f32[2,16,12544]{2,1,0:T(8,128)S(1)} collective-permute-done((f32[2,16,12544]{2,1,0:T(8,128)S(1)}, f32[2,16,12544]{2,1,0:T(8,128)S(1)}, u32[]{:S(2)}, u32[]{:S(2)}) %collective-permute-start.3) | collective-permute-done | bytes 1605664 | tf_op jit(solution)/shard_map/ppermute | solution.py:219
  46.0 0.0 collective-permute-done.4.refs_5_
  46.0 0.0 copy-done.1
  46.0 0.0 copy-done
  46.1 3.6 %shard_map.38.refs_0_ = f32[96,128]{1,0:T(8,128)S(1)} custom-call(f32[32,12544]{1,0:T(8,128)S(1)} %copy-done, f32[2,16,12544]{2,1,0:T(8,128)S(1)} %copy-done.1, f32[2,16,12544]{2,1,0:T(8,128)S(1)} %collective-permute-done.refs_1_, f32[2,16,12544]{2,1,0:T(8,128)S(1)} %collective-permute-done.1.refs_2_, f32[2,16,12544]{2,1,0:T(8,128)S(1)} %collective-permute-done.3.refs_3_, ...), custom_call_target="tpu_custom_call" | custom-call | flops 1 | bytes 1 | tf_op jit(solution)/shard_map/pallas_call | solution.py:178
  49.6 1.8 %collective-permute-start.6 = (f32[96,128]{1,0:T(8,128)S(1)}, f32[96,128]{1,0:T(8,128)S(1)}, u32[]{:S(2)}, u32[]{:S(2)}) collective-permute-start(f32[96,128]{1,0:T(8,128)S(1)} %shard_map.38.refs_0_), channel_id=1, source_target_pairs={{0,8},{8,0},{16,24},{24,16},{1,9},{9,1},{17,25},{25,17},{2,10},{10... | collective-permute-start | bytes 147464 | tf_op jit(solution)/shard_map/ppermute | solution.py:219
  51.4 2.6 %collective-permute-start.7 = (f32[96,128]{1,0:T(8,128)S(1)}, f32[96,128]{1,0:T(8,128)S(1)}, u32[]{:S(2)}, u32[]{:S(2)}) collective-permute-start(f32[96,128]{1,0:T(8,128)S(1)} %shard_map.38.refs_0_), channel_id=1, source_target_pairs={{0,16},{8,24},{16,0},{24,8},{1,17},{9,25},{17,1},{25,9},{2,18},{10... | collective-permute-start | bytes 147464 | tf_op jit(solution)/shard_map/ppermute | solution.py:219
  54.0 0.1 collective-permute-start.8
  54.0 4.4 %collective-permute-done.10.refs_2_.refs_8_ = f32[16,12544]{1,0:T(8,128)S(1)} collective-permute-done((f32[16,12544]{1,0:T(8,128)S(1)}, f32[16,12544]{1,0:T(8,128)S(1)}, u32[]{:S(2)}, u32[]{:S(2)}) %collective-permute-start.10) | collective-permute-done | bytes 802848 | tf_op jit(solution)/shard_map/ppermute | solution.py:219
  58.4 0.0 collective-permute-done.9.refs_0_.refs_6_
  58.4 0.0 collective-permute-done.6.refs_1_
  58.4 0.0 collective-permute-done.7.refs_2_
  58.5 1.4 %collective-permute-done.8.refs_3_ = f32[96,128]{1,0:T(8,128)S(1)} collective-permute-done((f32[96,128]{1,0:T(8,128)S(1)}, f32[96,128]{1,0:T(8,128)S(1)}, u32[]{:S(2)}, u32[]{:S(2)}) %collective-permute-start.8) | collective-permute-done | bytes 49184 | tf_op jit(solution)/shard_map/ppermute | solution.py:219
  59.9 0.0 collective-permute-start.11
  59.9 0.5 collective-permute-start.12
  60.4 1.9 %collective-permute-start.16 = (f32[96,128]{1,0:T(8,128)S(1)}, f32[96,128]{1,0:T(8,128)S(1)}, u32[]{:S(2)}, u32[]{:S(2)}) collective-permute-start(f32[96,128]{1,0:T(8,128)S(1)} %get-tuple-element.45.refs_0_), channel_id=1, source_target_pairs={{0,2},{1,5},{2,0},{3,7},{4,6},{5,1},{6,4},{7,3},{8,10},{9,13},{10,... | collective-permute-start | bytes 147464 | tf_op jit(solution)/shard_map/ppermute | solution.py:219
  62.3 0.9 %collective-permute-start.17 = (f32[96,128]{1,0:T(8,128)S(1)}, f32[96,128]{1,0:T(8,128)S(1)}, u32[]{:S(2)}, u32[]{:S(2)}) collective-permute-start(f32[96,128]{1,0:T(8,128)S(1)} %get-tuple-element.45.refs_0_), channel_id=1, source_target_pairs={{0,4},{1,3},{2,6},{3,1},{4,0},{5,7},{6,2},{7,5},{8,12},{9,11},{10,... | collective-permute-start | bytes 147464 | tf_op jit(solution)/shard_map/ppermute | solution.py:219
  63.3 0.7 collective-permute-start.18
  63.9 0.0 collective-permute-done.11.refs_1_.refs_7_
  64.0 0.0 collective-permute-done.12.refs_3_.refs_9_
  64.0 1.1 %shard_map.40.refs_1_ = f32[16,128]{1,0:T(8,128)S(1)} custom-call(f32[32,12544]{1,0:T(8,128)S(1)} %copy-done, f32[16,12544]{1,0:T(8,128)S(1)} %collective-permute-done.9.refs_0_.refs_6_, f32[16,12544]{1,0:T(8,128)S(1)} %collective-permute-done.11.refs_1_.refs_7_, f32[16,12544]{1,0:T(8,128)S(1)} %collective-permute-done.10.refs_2_.refs_8_, ...), custom_call_target="tpu_custom_call" | custom-call | flops 1 | bytes 1 | tf_op jit(solution)/shard_map/pallas_call | solution.py:178
  65.1 4.0 %collective-permute-start.13 = (f32[16,128]{1,0:T(8,128)S(1)}, f32[16,128]{1,0:T(8,128)S(1)}, u32[]{:S(2)}, u32[]{:S(2)}) collective-permute-start(f32[16,128]{1,0:T(8,128)S(1)} %shard_map.40.refs_1_), channel_id=1, source_target_pairs={{0,24},{8,16},{16,8},{24,0},{1,25},{9,17},{17,9},{25,1},{2,26},{10... | collective-permute-start | bytes 24584 | tf_op jit(solution)/shard_map/ppermute | solution.py:219
  69.1 0.0 collective-permute-start.14
  69.1 0.0 collective-permute-done.16.refs_1_
  69.1 0.6 collective-permute-start.15
  69.7 0.0 collective-permute-done.17.refs_2_
  69.7 0.0 collective-permute-done.18.refs_3_
  69.7 0.3 shard_map.41
  70.0 1.8 %shard_map.42 = (bf16[256,12544]{1,0:T(8,128)(2,1)S(1)}, bf16[256,12544]{1,0:T(8,128)(2,1)S(1)}) custom-call(f32[2,16,12544]{2,1,0:T(8,128)S(1)} %copy-done.1, f32[2,16,12544]{2,1,0:T(8,128)S(1)} %collective-permute-done.refs_1_, f32[2,16,12544]{2,1,0:T(8,128)S(1)} %collective-permute-done.1.refs_2_, f32[2,16,12544]{2,1,0:T(8,128)S(1)} %collective-permute-done.3.refs_3_, ...), custom_call_target="tpu_custom_call" | custom-call | flops 1 | bytes 51380224 | tf_op jit(solution)/shard_map/pallas_call | solution.py:273
  71.8 0.0 collective-permute-done.13.refs_2_
  71.9 1.8 %collective-permute-done.14.refs_3_ = f32[16,128]{1,0:T(8,128)S(1)} collective-permute-done((f32[16,128]{1,0:T(8,128)S(1)}, f32[16,128]{1,0:T(8,128)S(1)}, u32[]{:S(2)}, u32[]{:S(2)}) %collective-permute-start.14) | collective-permute-done | bytes 8224 | tf_op jit(solution)/shard_map/ppermute | solution.py:219
  73.6 0.0 collective-permute-done.15.refs_4_
  73.6 3.7 %shard_map.43 = f32[32,12544]{1,0:T(8,128)} custom-call(f32[64,128]{1,0:T(8,128)S(1)} %get-tuple-element.41.refs_0_, f32[16,128]{1,0:T(8,128)S(1)} %shard_map.40.refs_1_, f32[16,128]{1,0:T(8,128)S(1)} %collective-permute-done.13.refs_2_, f32[16,128]{1,0:T(8,128)S(1)} %collective-permute-done.14.refs_3_, f32[16,128]{1,0:T(8,128)S(1)} %collective-permute-done.15.refs_4_, ...), custom_call_target="tpu_custom_call" | custom-call | flops 1 | bytes 1 | tf_op jit(solution)/shard_map/pallas_call | solution.py:200
  (1 shorter events, 0.0 us)
Async XLA Ops:
  0.0 46.0 %copy-start.1 = (f32[2,16,12544]{2,1,0:T(8,128)S(1)}, f32[2,16,12544]{2,1,0:T(8,128)}, u32[]{:S(2)}) copy-start(f32[2,16,12544]{2,1,0:T(8,128)} %refs_0_.3) | copy-start | bytes 4816900
  0.0 42.6 %copy-start.2 = (f32[2,16,128]{2,1,0:T(8,128)S(1)}, f32[2,16,128]{2,1,0:T(8,128)}, u32[]{:S(2)}) copy-start(f32[2,16,128]{2,1,0:T(8,128)} %refs_0_.1) | copy-start | bytes 49156
  0.0 46.0 %copy-start = (f32[32,12544]{1,0:T(8,128)S(1)}, f32[32,12544]{1,0:T(8,128)}, u32[]{:S(2)}) copy-start(f32[32,12544]{1,0:T(8,128)} %refs_8_.1) | copy-start | bytes 4816900
  0.0 38.7 %collective-permute-start.1 = (f32[2,16,12544]{2,1,0:T(8,128)}, f32[2,16,12544]{2,1,0:T(8,128)S(1)}, u32[]{:S(2)}, u32[]{:S(2)}) collective-permute-start(f32[2,16,12544]{2,1,0:T(8,128)} %refs_0_.3), channel_id=1, source_target_pairs={{0,2},{1,5},{2,0},{3,7},{4,6},{5,1},{6,4},{7,3},{8,10},{9,13},{10,... | collective-permute-start | bytes 4816904 | tf_op jit(solution)/shard_map/ppermute | solution.py:219
  3.0 37.3 %collective-permute-start.2 = (f32[2,16,12544]{2,1,0:T(8,128)}, f32[2,16,12544]{2,1,0:T(8,128)S(1)}, u32[]{:S(2)}, u32[]{:S(2)}) collective-permute-start(f32[2,16,12544]{2,1,0:T(8,128)} %refs_0_.3), channel_id=1, source_target_pairs={{0,4},{1,3},{2,6},{3,1},{4,0},{5,7},{6,2},{7,5},{8,12},{9,11},{10,... | collective-permute-start | bytes 4816904 | tf_op jit(solution)/shard_map/ppermute | solution.py:219
  4.5 38.2 %collective-permute-start = (f32[2,16,12544]{2,1,0:T(8,128)}, f32[2,16,12544]{2,1,0:T(8,128)S(1)}, u32[]{:S(2)}, u32[]{:S(2)}) collective-permute-start(f32[2,16,12544]{2,1,0:T(8,128)} %refs_0_.3), channel_id=1, source_target_pairs={{0,1},{1,0},{2,3},{3,2},{4,5},{5,4},{6,7},{7,6},{8,9},{9,8},{10,11... | collective-permute-start | bytes 4816904 | tf_op jit(solution)/shard_map/ppermute | solution.py:219
  4.5 36.3 %collective-permute-start.5 = (f32[2,16,128]{2,1,0:T(8,128)}, f32[2,16,128]{2,1,0:T(8,128)S(1)}, u32[]{:S(2)}, u32[]{:S(2)}) collective-permute-start(f32[2,16,128]{2,1,0:T(8,128)} %refs_0_.1), channel_id=1, source_target_pairs={{0,1},{1,0},{2,3},{3,2},{4,5},{5,4},{6,7},{7,6},{8,9},{9,8},{10,11... | collective-permute-start | bytes 49160 | tf_op jit(solution)/shard_map/ppermute | solution.py:219
  38.8 19.7 %collective-permute-start.10 = (f32[16,12544]{1,0:T(8,128)S(1)}, f32[16,12544]{1,0:T(8,128)S(1)}, u32[]{:S(2)}, u32[]{:S(2)}) collective-permute-start(f32[16,12544]{1,0:T(8,128)S(1)} %slice_bitcast_fusion), channel_id=1, source_target_pairs={{0,4},{1,3},{2,6},{3,1},{4,0},{5,7},{6,2},{7,5},{8,12},{9,11},{10,... | collective-permute-start | bytes 2408456 | tf_op jit(solution)/shard_map/ppermute | solution.py:219
  40.3 5.8 %collective-permute-start.4 = (f32[2,16,12544]{2,1,0:T(8,128)S(1)}, f32[2,16,12544]{2,1,0:T(8,128)S(1)}, u32[]{:S(2)}, u32[]{:S(2)}) collective-permute-start(f32[2,16,12544]{2,1,0:T(8,128)S(1)} %collective-permute-done.1.refs_2_), channel_id=1, source_target_pairs={{0,1},{1,0},{2,3},{3,2},{4,5},{5,4},{6,7},{7,6},{8,9},{9,8},{10,11... | collective-permute-start | bytes 4816904 | tf_op jit(solution)/shard_map/ppermute | solution.py:219
  40.3 5.7 %collective-permute-start.3 = (f32[2,16,12544]{2,1,0:T(8,128)S(1)}, f32[2,16,12544]{2,1,0:T(8,128)S(1)}, u32[]{:S(2)}, u32[]{:S(2)}) collective-permute-start(f32[2,16,12544]{2,1,0:T(8,128)S(1)} %collective-permute-done.2.refs_4_), channel_id=1, source_target_pairs={{0,1},{1,0},{2,3},{3,2},{4,5},{5,4},{6,7},{7,6},{8,9},{9,8},{10,11... | collective-permute-start | bytes 4816904 | tf_op jit(solution)/shard_map/ppermute | solution.py:219
  40.9 17.6 %collective-permute-start.9 = (f32[16,12544]{1,0:T(8,128)S(1)}, f32[16,12544]{1,0:T(8,128)S(1)}, u32[]{:S(2)}, u32[]{:S(2)}) collective-permute-start(f32[16,12544]{1,0:T(8,128)S(1)} %slice_bitcast_fusion.1), channel_id=1, source_target_pairs={{0,2},{1,5},{2,0},{3,7},{4,6},{5,1},{6,4},{7,3},{8,10},{9,13},{10,... | collective-permute-start | bytes 2408456 | tf_op jit(solution)/shard_map/ppermute | solution.py:219
  49.6 8.8 %collective-permute-start.6 = (f32[96,128]{1,0:T(8,128)S(1)}, f32[96,128]{1,0:T(8,128)S(1)}, u32[]{:S(2)}, u32[]{:S(2)}) collective-permute-start(f32[96,128]{1,0:T(8,128)S(1)} %shard_map.38.refs_0_), channel_id=1, source_target_pairs={{0,8},{8,0},{16,24},{24,16},{1,9},{9,1},{17,25},{25,17},{2,10},{10... | collective-permute-start | bytes 147464 | tf_op jit(solution)/shard_map/ppermute | solution.py:219
  51.4 7.1 %collective-permute-start.7 = (f32[96,128]{1,0:T(8,128)S(1)}, f32[96,128]{1,0:T(8,128)S(1)}, u32[]{:S(2)}, u32[]{:S(2)}) collective-permute-start(f32[96,128]{1,0:T(8,128)S(1)} %shard_map.38.refs_0_), channel_id=1, source_target_pairs={{0,16},{8,24},{16,0},{24,8},{1,17},{9,25},{17,1},{25,9},{2,18},{10... | collective-permute-start | bytes 147464 | tf_op jit(solution)/shard_map/ppermute | solution.py:219
  54.0 5.9 %collective-permute-start.8 = (f32[96,128]{1,0:T(8,128)S(1)}, f32[96,128]{1,0:T(8,128)S(1)}, u32[]{:S(2)}, u32[]{:S(2)}) collective-permute-start(f32[96,128]{1,0:T(8,128)S(1)} %shard_map.38.refs_0_), channel_id=1, source_target_pairs={{0,24},{8,16},{16,8},{24,0},{1,25},{9,17},{17,9},{25,1},{2,26},{10... | collective-permute-start | bytes 147464 | tf_op jit(solution)/shard_map/ppermute | solution.py:219
  59.9 4.1 %collective-permute-start.11 = (f32[16,12544]{1,0:T(8,128)S(1)}, f32[16,12544]{1,0:T(8,128)S(1)}, u32[]{:S(2)}, u32[]{:S(2)}) collective-permute-start(f32[16,12544]{1,0:T(8,128)S(1)} %collective-permute-done.9.refs_0_.refs_6_), channel_id=1, source_target_pairs={{0,1},{1,0},{2,3},{3,2},{4,5},{5,4},{6,7},{7,6},{8,9},{9,8},{10,11... | collective-permute-start | bytes 2408456 | tf_op jit(solution)/shard_map/ppermute | solution.py:219
  59.9 4.1 %collective-permute-start.12 = (f32[16,12544]{1,0:T(8,128)S(1)}, f32[16,12544]{1,0:T(8,128)S(1)}, u32[]{:S(2)}, u32[]{:S(2)}) collective-permute-start(f32[16,12544]{1,0:T(8,128)S(1)} %collective-permute-done.10.refs_2_.refs_8_), channel_id=1, source_target_pairs={{0,1},{1,0},{2,3},{3,2},{4,5},{5,4},{6,7},{7,6},{8,9},{9,8},{10,11... | collective-permute-start | bytes 2408456 | tf_op jit(solution)/shard_map/ppermute | solution.py:219
  60.4 8.7 %collective-permute-start.16 = (f32[96,128]{1,0:T(8,128)S(1)}, f32[96,128]{1,0:T(8,128)S(1)}, u32[]{:S(2)}, u32[]{:S(2)}) collective-permute-start(f32[96,128]{1,0:T(8,128)S(1)} %get-tuple-element.45.refs_0_), channel_id=1, source_target_pairs={{0,2},{1,5},{2,0},{3,7},{4,6},{5,1},{6,4},{7,3},{8,10},{9,13},{10,... | collective-permute-start | bytes 147464 | tf_op jit(solution)/shard_map/ppermute | solution.py:219
  62.3 7.4 %collective-permute-start.17 = (f32[96,128]{1,0:T(8,128)S(1)}, f32[96,128]{1,0:T(8,128)S(1)}, u32[]{:S(2)}, u32[]{:S(2)}) collective-permute-start(f32[96,128]{1,0:T(8,128)S(1)} %get-tuple-element.45.refs_0_), channel_id=1, source_target_pairs={{0,4},{1,3},{2,6},{3,1},{4,0},{5,7},{6,2},{7,5},{8,12},{9,11},{10,... | collective-permute-start | bytes 147464 | tf_op jit(solution)/shard_map/ppermute | solution.py:219
  63.3 6.5 %collective-permute-start.18 = (f32[96,128]{1,0:T(8,128)S(1)}, f32[96,128]{1,0:T(8,128)S(1)}, u32[]{:S(2)}, u32[]{:S(2)}) collective-permute-start(f32[96,128]{1,0:T(8,128)S(1)} %get-tuple-element.45.refs_0_), channel_id=1, source_target_pairs={{0,6},{1,7},{2,4},{3,5},{4,2},{5,3},{6,0},{7,1},{8,14},{9,15},{10,... | collective-permute-start | bytes 147464 | tf_op jit(solution)/shard_map/ppermute | solution.py:219
  65.1 6.8 %collective-permute-start.13 = (f32[16,128]{1,0:T(8,128)S(1)}, f32[16,128]{1,0:T(8,128)S(1)}, u32[]{:S(2)}, u32[]{:S(2)}) collective-permute-start(f32[16,128]{1,0:T(8,128)S(1)} %shard_map.40.refs_1_), channel_id=1, source_target_pairs={{0,24},{8,16},{16,8},{24,0},{1,25},{9,17},{17,9},{25,1},{2,26},{10... | collective-permute-start | bytes 24584 | tf_op jit(solution)/shard_map/ppermute | solution.py:219
  69.1 4.5 %collective-permute-start.14 = (f32[16,128]{1,0:T(8,128)S(1)}, f32[16,128]{1,0:T(8,128)S(1)}, u32[]{:S(2)}, u32[]{:S(2)}) collective-permute-start(f32[16,128]{1,0:T(8,128)S(1)} %shard_map.40.refs_1_), channel_id=1, source_target_pairs={{0,16},{8,24},{16,0},{24,8},{1,17},{9,25},{17,1},{25,9},{2,18},{10... | collective-permute-start | bytes 24584 | tf_op jit(solution)/shard_map/ppermute | solution.py:219
  69.1 4.5 %collective-permute-start.15 = (f32[16,128]{1,0:T(8,128)S(1)}, f32[16,128]{1,0:T(8,128)S(1)}, u32[]{:S(2)}, u32[]{:S(2)}) collective-permute-start(f32[16,128]{1,0:T(8,128)S(1)} %shard_map.40.refs_1_), channel_id=1, source_target_pairs={{0,8},{8,0},{16,24},{24,16},{1,9},{9,1},{17,25},{25,17},{2,10},{10... | collective-permute-start | bytes 24584 | tf_op jit(solution)/shard_map/ppermute | solution.py:219

commit v6 on v1

--- a/solution.py
+++ b/solution.py
@@ -227,7 +227,8 @@
     while reach < depth:
         value = sum(terms[1:], terms[0])
         span = min(step, depth // reach)
-        terms = [value] + [exchange(value, lambda i, k=k: k * reach, depth, "prow") for k in range(1, span)]
+        steps = sorted(range(1, span), key=lambda k: (k != 1, k != span - 1))
+        terms = [value] + [exchange(value, lambda i, k=k: k * reach, depth, "prow") for k in steps]
         reach *= span
     return terms
 

time: 77.5 us -> 77.4 us (level)
  transfers between devices with their start and end apart: 19 -> 19, of which waited for: 6 -> 5; matrix products, arithmetic and copies ran while one was open for 0% -> 0% of each run, Pallas kernels for 7% -> 7%
where the time goes in v6:
time: 77.4 us; the launch traced here: 77.2 us
  waiting for transfers between devices  44.9 us (58%)
  starting transfers between devices  23 us (30%)
  Pallas kernels  9.13 us (12%)
    ppermute x19, waiting for transfers between devices, exchange(): return lax.ppermute(array, axis, [(i, i ^ partner(i)) for i in range(size)])  44.9 us
    ppermute x19, starting transfers between devices, exchange(): return lax.ppermute(array, axis, [(i, i ^ partner(i)) for i in range(size)])  23 us
    pallas_call x2, Pallas kernels, products(): pl.pallas_call(kernel, in_specs=[pl.BlockSpec(memory_space=pltpu.VMEM)] *...  4.69 us
    pallas_call x1, Pallas kernels, update(): pl.pallas_call(functools.partial(update_kernel, pieces, len(terms)), in_s...  3.92 us
  transfers between devices with their start and end apart: 19, of which 5 were waited for; matrix products, arithmetic and copies ran while one was open for 0% of the time, Pallas kernels for 7%

profile of v6, /device:TPU:0, one launch (start us, length us, event | category | flops | bytes accessed | tf_op | source)
XLA Modules:
  0.0 77.2 jit_solution(7646285105777530763)
XLA Ops:
  0.0 0.0 copy-start.1
  0.0 0.0 copy-start.2
  0.0 0.0 copy-start
  0.0 3.0 %collective-permute-start.1 = (f32[2,16,12544]{2,1,0:T(8,128)}, f32[2,16,12544]{2,1,0:T(8,128)S(1)}, u32[]{:S(2)}, u32[]{:S(2)}) collective-permute-start(f32[2,16,12544]{2,1,0:T(8,128)} %refs_9_), channel_id=1, source_target_pairs={{0,2},{1,5},{2,0},{3,7},{4,6},{5,1},{6,4},{7,3},{8,10},{9,13},{10,... | collective-permute-start | bytes 4816904 | tf_op jit(solution)/shard_map/ppermute | solution.py:222
  3.0 0.0 collective-permute-start
  3.0 1.5 %collective-permute-start.2 = (f32[2,16,12544]{2,1,0:T(8,128)}, f32[2,16,12544]{2,1,0:T(8,128)S(1)}, u32[]{:S(2)}, u32[]{:S(2)}) collective-permute-start(f32[2,16,12544]{2,1,0:T(8,128)} %refs_9_), channel_id=1, source_target_pairs={{0,4},{1,3},{2,6},{3,1},{4,0},{5,7},{6,2},{7,5},{8,12},{9,11},{10,... | collective-permute-start | bytes 4816904 | tf_op jit(solution)/shard_map/ppermute | solution.py:222
  4.5 0.0 collective-permute-start.5
  4.5 34.2 %collective-permute-done.1.refs_2_.refs_11_ = f32[2,16,12544]{2,1,0:T(8,128)S(1)} collective-permute-done((f32[2,16,12544]{2,1,0:T(8,128)}, f32[2,16,12544]{2,1,0:T(8,128)S(1)}, u32[]{:S(2)}, u32[]{:S(2)}) %collective-permute-start.1) | collective-permute-done | bytes 1605664 | tf_op jit(solution)/shard_map/ppermute | solution.py:222
  38.7 0.1 slice_bitcast_fusion
  38.8 1.6 %collective-permute-start.10 = (f32[16,12544]{1,0:T(8,128)S(1)}, f32[16,12544]{1,0:T(8,128)S(1)}, u32[]{:S(2)}, u32[]{:S(2)}) collective-permute-start(f32[16,12544]{1,0:T(8,128)S(1)} %slice_bitcast_fusion), channel_id=1, source_target_pairs={{0,4},{1,3},{2,6},{3,1},{4,0},{5,7},{6,2},{7,5},{8,12},{9,11},{10,... | collective-permute-start | bytes 2408456 | tf_op jit(solution)/shard_map/ppermute | solution.py:222
  40.4 0.0 collective-permute-start.4
  40.4 0.0 collective-permute-done.2.refs_4_.refs_13_
  40.4 0.5 collective-permute-start.3
  40.9 0.1 slice_bitcast_fusion.1
  41.0 0.0 collective-permute-done.5.refs_1_
  41.0 2.4 %collective-permute-start.9 = (f32[16,12544]{1,0:T(8,128)S(1)}, f32[16,12544]{1,0:T(8,128)S(1)}, u32[]{:S(2)}, u32[]{:S(2)}) collective-permute-start(f32[16,12544]{1,0:T(8,128)S(1)} %slice_bitcast_fusion.1), channel_id=1, source_target_pairs={{0,2},{1,5},{2,0},{3,7},{4,6},{5,1},{6,4},{7,3},{8,10},{9,13},{10,... | collective-permute-start | bytes 2408456 | tf_op jit(solution)/shard_map/ppermute | solution.py:222
  43.4 0.0 copy-done.2
  43.4 0.2 shard_map.37.refs_4_
  43.6 0.0 collective-permute-done.refs_1_.refs_10_
  43.6 0.2 collective-permute-done.4.refs_5_.refs_14_
  43.8 2.3 %collective-permute-done.3.refs_3_.refs_12_ = f32[2,16,12544]{2,1,0:T(8,128)S(1)} collective-permute-done((f32[2,16,12544]{2,1,0:T(8,128)S(1)}, f32[2,16,12544]{2,1,0:T(8,128)S(1)}, u32[]{:S(2)}, u32[]{:S(2)}) %collective-permute-start.3) | collective-permute-done | bytes 1605664 | tf_op jit(solution)/shard_map/ppermute | solution.py:222
  46.1 0.0 copy-done.1
  46.1 0.0 copy-done
  46.1 3.6 %shard_map.38.refs_0_ = f32[96,128]{1,0:T(8,128)S(1)} custom-call(f32[32,12544]{1,0:T(8,128)S(1)} %copy-done, f32[2,16,12544]{2,1,0:T(8,128)S(1)} %copy-done.1, f32[2,16,12544]{2,1,0:T(8,128)S(1)} %collective-permute-done.refs_1_.refs_10_, f32[2,16,12544]{2,1,0:T(8,128)S(1)} %collective-permute-done.1.refs_2_.refs_11_, ...), custom_call_target="tpu_custom_call" | custom-call | flops 1 | bytes 1 | tf_op jit(solution)/shard_map/pallas_call | solution.py:181
  49.7 2.6 %collective-permute-start.8 = (f32[96,128]{1,0:T(8,128)S(1)}, f32[96,128]{1,0:T(8,128)S(1)}, u32[]{:S(2)}, u32[]{:S(2)}) collective-permute-start(f32[96,128]{1,0:T(8,128)S(1)} %shard_map.38.refs_0_), channel_id=1, source_target_pairs={{0,16},{8,24},{16,0},{24,8},{1,17},{9,25},{17,1},{25,9},{2,18},{10... | collective-permute-start | bytes 147464 | tf_op jit(solution)/shard_map/ppermute | solution.py:222
  52.3 1.4 %collective-permute-start.7 = (f32[96,128]{1,0:T(8,128)S(1)}, f32[96,128]{1,0:T(8,128)S(1)}, u32[]{:S(2)}, u32[]{:S(2)}) collective-permute-start(f32[96,128]{1,0:T(8,128)S(1)} %shard_map.38.refs_0_), channel_id=1, source_target_pairs={{0,24},{8,16},{16,8},{24,0},{1,25},{9,17},{17,9},{25,1},{2,26},{10... | collective-permute-start | bytes 147464 | tf_op jit(solution)/shard_map/ppermute | solution.py:222
  53.7 0.2 collective-permute-start.6
  53.9 4.6 %collective-permute-done.10.refs_2_.refs_17_ = f32[16,12544]{1,0:T(8,128)S(1)} collective-permute-done((f32[16,12544]{1,0:T(8,128)S(1)}, f32[16,12544]{1,0:T(8,128)S(1)}, u32[]{:S(2)}, u32[]{:S(2)}) %collective-permute-start.10) | collective-permute-done | bytes 802848 | tf_op jit(solution)/shard_map/ppermute | solution.py:222
  58.5 0.0 collective-permute-done.9.refs_0_.refs_15_
  58.5 0.0 collective-permute-done.8.refs_3_
  58.5 0.0 collective-permute-done.7.refs_2_
  58.5 0.0 collective-permute-done.6.refs_1_
  58.5 1.0 %collective-permute-start.11 = (f32[16,12544]{1,0:T(8,128)S(1)}, f32[16,12544]{1,0:T(8,128)S(1)}, u32[]{:S(2)}, u32[]{:S(2)}) collective-permute-start(f32[16,12544]{1,0:T(8,128)S(1)} %collective-permute-done.9.refs_0_.refs_15_), channel_id=1, source_target_pairs={{0,1},{1,0},{2,3},{3,2},{4,5},{5,4},{6,7},{7,6},{8,9},{9,8},{10,11... | collective-permute-start | bytes 2408456 | tf_op jit(solution)/shard_map/ppermute | solution.py:222
  59.5 0.1 collective-permute-start.12
  59.6 3.9 %collective-permute-start.18 = (f32[96,128]{1,0:T(8,128)S(1)}, f32[96,128]{1,0:T(8,128)S(1)}, u32[]{:S(2)}, u32[]{:S(2)}) collective-permute-start(f32[96,128]{1,0:T(8,128)S(1)} %get-tuple-element.37.refs_0_), channel_id=1, source_target_pairs={{0,6},{1,7},{2,4},{3,5},{4,2},{5,3},{6,0},{7,1},{8,14},{9,15},{10,... | collective-permute-start | bytes 147464 | tf_op jit(solution)/shard_map/ppermute | solution.py:222
  63.5 0.0 collective-permute-start.17
  63.5 0.6 collective-permute-start.16
  64.1 0.0 collective-permute-done.11.refs_1_.refs_16_
  64.1 0.0 collective-permute-done.12.refs_3_.refs_18_
  64.1 1.1 %shard_map.40.refs_1_ = f32[16,128]{1,0:T(8,128)S(1)} custom-call(f32[32,12544]{1,0:T(8,128)S(1)} %copy-done, f32[16,12544]{1,0:T(8,128)S(1)} %collective-permute-done.9.refs_0_.refs_15_, f32[16,12544]{1,0:T(8,128)S(1)} %collective-permute-done.11.refs_1_.refs_16_, f32[16,12544]{1,0:T(8,128)S(1)} %collective-permute-done.10.refs_2_.refs_17_, ...), custom_call_target="tpu_custom_call" | custom-call | flops 1 | bytes 1 | tf_op jit(solution)/shard_map/pallas_call | solution.py:181
  65.2 2.6 %collective-permute-start.15 = (f32[16,128]{1,0:T(8,128)S(1)}, f32[16,128]{1,0:T(8,128)S(1)}, u32[]{:S(2)}, u32[]{:S(2)}) collective-permute-start(f32[16,128]{1,0:T(8,128)S(1)} %shard_map.40.refs_1_), channel_id=1, source_target_pairs={{0,16},{8,24},{16,0},{24,8},{1,17},{9,25},{17,1},{25,9},{2,18},{10... | collective-permute-start | bytes 24584 | tf_op jit(solution)/shard_map/ppermute | solution.py:222
  67.8 1.3 %collective-permute-start.14 = (f32[16,128]{1,0:T(8,128)S(1)}, f32[16,128]{1,0:T(8,128)S(1)}, u32[]{:S(2)}, u32[]{:S(2)}) collective-permute-start(f32[16,128]{1,0:T(8,128)S(1)} %shard_map.40.refs_1_), channel_id=1, source_target_pairs={{0,24},{8,16},{16,8},{24,0},{1,25},{9,17},{17,9},{25,1},{2,26},{10... | collective-permute-start | bytes 24584 | tf_op jit(solution)/shard_map/ppermute | solution.py:222
  69.2 0.0 collective-permute-done.18.refs_3_
  69.2 0.2 collective-permute-start.13
  69.4 0.0 collective-permute-done.17.refs_2_
  69.4 0.0 collective-permute-done.16.refs_1_
  69.4 0.3 shard_map.41
  69.8 0.0 collective-permute-done.15.refs_4_
  69.8 3.5 %collective-permute-done.14.refs_3_ = f32[16,128]{1,0:T(8,128)S(1)} collective-permute-done((f32[16,128]{1,0:T(8,128)S(1)}, f32[16,128]{1,0:T(8,128)S(1)}, u32[]{:S(2)}, u32[]{:S(2)}) %collective-permute-start.14) | collective-permute-done | bytes 8224 | tf_op jit(solution)/shard_map/ppermute | solution.py:222
  73.3 0.0 collective-permute-done.13.refs_2_
  73.3 3.9 %shard_map.42 = f32[32,12544]{1,0:T(8,128)} custom-call(f32[64,128]{1,0:T(8,128)S(1)} %get-tuple-element.34.refs_0_, f32[16,128]{1,0:T(8,128)S(1)} %shard_map.40.refs_1_, f32[16,128]{1,0:T(8,128)S(1)} %collective-permute-done.13.refs_2_, f32[16,128]{1,0:T(8,128)S(1)} %collective-permute-done.14.refs_3_, f32[16,128]{1,0:T(8,128)S(1)} %collective-permute-done.15.refs_4_, ...), custom_call_target="tpu_custom_call" | custom-call | flops 1 | bytes 1 | tf_op jit(solution)/shard_map/pallas_call | solution.py:203
  (1 shorter events, 0.0 us)
Async XLA Ops:
  0.0 46.1 %copy-start.1 = (f32[2,16,12544]{2,1,0:T(8,128)S(1)}, f32[2,16,12544]{2,1,0:T(8,128)}, u32[]{:S(2)}) copy-start(f32[2,16,12544]{2,1,0:T(8,128)} %refs_9_) | copy-start | bytes 4816900
  0.0 43.4 %copy-start.2 = (f32[2,16,128]{2,1,0:T(8,128)S(1)}, f32[2,16,128]{2,1,0:T(8,128)}, u32[]{:S(2)}) copy-start(f32[2,16,128]{2,1,0:T(8,128)} %refs_0_.1) | copy-start | bytes 49156
  0.0 46.1 %copy-start = (f32[32,12544]{1,0:T(8,128)S(1)}, f32[32,12544]{1,0:T(8,128)}, u32[]{:S(2)}) copy-start(f32[32,12544]{1,0:T(8,128)} %refs_8_.1) | copy-start | bytes 4816900
  0.0 38.7 %collective-permute-start.1 = (f32[2,16,12544]{2,1,0:T(8,128)}, f32[2,16,12544]{2,1,0:T(8,128)S(1)}, u32[]{:S(2)}, u32[]{:S(2)}) collective-permute-start(f32[2,16,12544]{2,1,0:T(8,128)} %refs_9_), channel_id=1, source_target_pairs={{0,2},{1,5},{2,0},{3,7},{4,6},{5,1},{6,4},{7,3},{8,10},{9,13},{10,... | collective-permute-start | bytes 4816904 | tf_op jit(solution)/shard_map/ppermute | solution.py:222
  3.0 40.6 %collective-permute-start = (f32[2,16,12544]{2,1,0:T(8,128)}, f32[2,16,12544]{2,1,0:T(8,128)S(1)}, u32[]{:S(2)}, u32[]{:S(2)}) collective-permute-start(f32[2,16,12544]{2,1,0:T(8,128)} %refs_9_), channel_id=1, source_target_pairs={{0,1},{1,0},{2,3},{3,2},{4,5},{5,4},{6,7},{7,6},{8,9},{9,8},{10,11... | collective-permute-start | bytes 4816904 | tf_op jit(solution)/shard_map/ppermute | solution.py:222
  3.0 37.4 %collective-permute-start.2 = (f32[2,16,12544]{2,1,0:T(8,128)}, f32[2,16,12544]{2,1,0:T(8,128)S(1)}, u32[]{:S(2)}, u32[]{:S(2)}) collective-permute-start(f32[2,16,12544]{2,1,0:T(8,128)} %refs_9_), channel_id=1, source_target_pairs={{0,4},{1,3},{2,6},{3,1},{4,0},{5,7},{6,2},{7,5},{8,12},{9,11},{10,... | collective-permute-start | bytes 4816904 | tf_op jit(solution)/shard_map/ppermute | solution.py:222
  4.5 36.4 %collective-permute-start.5 = (f32[2,16,128]{2,1,0:T(8,128)}, f32[2,16,128]{2,1,0:T(8,128)S(1)}, u32[]{:S(2)}, u32[]{:S(2)}) collective-permute-start(f32[2,16,128]{2,1,0:T(8,128)} %refs_0_.1), channel_id=1, source_target_pairs={{0,1},{1,0},{2,3},{3,2},{4,5},{5,4},{6,7},{7,6},{8,9},{9,8},{10,11... | collective-permute-start | bytes 49160 | tf_op jit(solution)/shard_map/ppermute | solution.py:222
  38.8 19.7 %collective-permute-start.10 = (f32[16,12544]{1,0:T(8,128)S(1)}, f32[16,12544]{1,0:T(8,128)S(1)}, u32[]{:S(2)}, u32[]{:S(2)}) collective-permute-start(f32[16,12544]{1,0:T(8,128)S(1)} %slice_bitcast_fusion), channel_id=1, source_target_pairs={{0,4},{1,3},{2,6},{3,1},{4,0},{5,7},{6,2},{7,5},{8,12},{9,11},{10,... | collective-permute-start | bytes 2408456 | tf_op jit(solution)/shard_map/ppermute | solution.py:222
  40.4 3.5 %collective-permute-start.4 = (f32[2,16,12544]{2,1,0:T(8,128)S(1)}, f32[2,16,12544]{2,1,0:T(8,128)S(1)}, u32[]{:S(2)}, u32[]{:S(2)}) collective-permute-start(f32[2,16,12544]{2,1,0:T(8,128)S(1)} %collective-permute-done.1.refs_2_.refs_11_), channel_id=1, source_target_pairs={{0,1},{1,0},{2,3},{3,2},{4,5},{5,4},{6,7},{7,6},{8,9},{9,8},{10,11... | collective-permute-start | bytes 4816904 | tf_op jit(solution)/shard_map/ppermute | solution.py:222
  40.4 5.7 %collective-permute-start.3 = (f32[2,16,12544]{2,1,0:T(8,128)S(1)}, f32[2,16,12544]{2,1,0:T(8,128)S(1)}, u32[]{:S(2)}, u32[]{:S(2)}) collective-permute-start(f32[2,16,12544]{2,1,0:T(8,128)S(1)} %collective-permute-done.2.refs_4_.refs_13_), channel_id=1, source_target_pairs={{0,1},{1,0},{2,3},{3,2},{4,5},{5,4},{6,7},{7,6},{8,9},{9,8},{10,11... | collective-permute-start | bytes 4816904 | tf_op jit(solution)/shard_map/ppermute | solution.py:222
  41.0 17.5 %collective-permute-start.9 = (f32[16,12544]{1,0:T(8,128)S(1)}, f32[16,12544]{1,0:T(8,128)S(1)}, u32[]{:S(2)}, u32[]{:S(2)}) collective-permute-start(f32[16,12544]{1,0:T(8,128)S(1)} %slice_bitcast_fusion.1), channel_id=1, source_target_pairs={{0,2},{1,5},{2,0},{3,7},{4,6},{5,1},{6,4},{7,3},{8,10},{9,13},{10,... | collective-permute-start | bytes 2408456 | tf_op jit(solution)/shard_map/ppermute | solution.py:222
  49.7 8.8 %collective-permute-start.8 = (f32[96,128]{1,0:T(8,128)S(1)}, f32[96,128]{1,0:T(8,128)S(1)}, u32[]{:S(2)}, u32[]{:S(2)}) collective-permute-start(f32[96,128]{1,0:T(8,128)S(1)} %shard_map.38.refs_0_), channel_id=1, source_target_pairs={{0,16},{8,24},{16,0},{24,8},{1,17},{9,25},{17,1},{25,9},{2,18},{10... | collective-permute-start | bytes 147464 | tf_op jit(solution)/shard_map/ppermute | solution.py:222
  52.3 6.2 %collective-permute-start.7 = (f32[96,128]{1,0:T(8,128)S(1)}, f32[96,128]{1,0:T(8,128)S(1)}, u32[]{:S(2)}, u32[]{:S(2)}) collective-permute-start(f32[96,128]{1,0:T(8,128)S(1)} %shard_map.38.refs_0_), channel_id=1, source_target_pairs={{0,24},{8,16},{16,8},{24,0},{1,25},{9,17},{17,9},{25,1},{2,26},{10... | collective-permute-start | bytes 147464 | tf_op jit(solution)/shard_map/ppermute | solution.py:222
  53.7 4.8 %collective-permute-start.6 = (f32[96,128]{1,0:T(8,128)S(1)}, f32[96,128]{1,0:T(8,128)S(1)}, u32[]{:S(2)}, u32[]{:S(2)}) collective-permute-start(f32[96,128]{1,0:T(8,128)S(1)} %shard_map.38.refs_0_), channel_id=1, source_target_pairs={{0,8},{8,0},{16,24},{24,16},{1,9},{9,1},{17,25},{25,17},{2,10},{10... | collective-permute-start | bytes 147464 | tf_op jit(solution)/shard_map/ppermute | solution.py:222
  58.5 5.6 %collective-permute-start.11 = (f32[16,12544]{1,0:T(8,128)S(1)}, f32[16,12544]{1,0:T(8,128)S(1)}, u32[]{:S(2)}, u32[]{:S(2)}) collective-permute-start(f32[16,12544]{1,0:T(8,128)S(1)} %collective-permute-done.9.refs_0_.refs_15_), channel_id=1, source_target_pairs={{0,1},{1,0},{2,3},{3,2},{4,5},{5,4},{6,7},{7,6},{8,9},{9,8},{10,11... | collective-permute-start | bytes 2408456 | tf_op jit(solution)/shard_map/ppermute | solution.py:222
  59.5 4.6 %collective-permute-start.12 = (f32[16,12544]{1,0:T(8,128)S(1)}, f32[16,12544]{1,0:T(8,128)S(1)}, u32[]{:S(2)}, u32[]{:S(2)}) collective-permute-start(f32[16,12544]{1,0:T(8,128)S(1)} %collective-permute-done.10.refs_2_.refs_17_), channel_id=1, source_target_pairs={{0,1},{1,0},{2,3},{3,2},{4,5},{5,4},{6,7},{7,6},{8,9},{9,8},{10,11... | collective-permute-start | bytes 2408456 | tf_op jit(solution)/shard_map/ppermute | solution.py:222
  59.6 9.6 %collective-permute-start.18 = (f32[96,128]{1,0:T(8,128)S(1)}, f32[96,128]{1,0:T(8,128)S(1)}, u32[]{:S(2)}, u32[]{:S(2)}) collective-permute-start(f32[96,128]{1,0:T(8,128)S(1)} %get-tuple-element.37.refs_0_), channel_id=1, source_target_pairs={{0,6},{1,7},{2,4},{3,5},{4,2},{5,3},{6,0},{7,1},{8,14},{9,15},{10,... | collective-permute-start | bytes 147464 | tf_op jit(solution)/shard_map/ppermute | solution.py:222
  63.5 5.9 %collective-permute-start.17 = (f32[96,128]{1,0:T(8,128)S(1)}, f32[96,128]{1,0:T(8,128)S(1)}, u32[]{:S(2)}, u32[]{:S(2)}) collective-permute-start(f32[96,128]{1,0:T(8,128)S(1)} %get-tuple-element.37.refs_0_), channel_id=1, source_target_pairs={{0,4},{1,3},{2,6},{3,1},{4,0},{5,7},{6,2},{7,5},{8,12},{9,11},{10,... | collective-permute-start | bytes 147464 | tf_op jit(solution)/shard_map/ppermute | solution.py:222
  63.5 5.9 %collective-permute-start.16 = (f32[96,128]{1,0:T(8,128)S(1)}, f32[96,128]{1,0:T(8,128)S(1)}, u32[]{:S(2)}, u32[]{:S(2)}) collective-permute-start(f32[96,128]{1,0:T(8,128)S(1)} %get-tuple-element.37.refs_0_), channel_id=1, source_target_pairs={{0,2},{1,5},{2,0},{3,7},{4,6},{5,1},{6,4},{7,3},{8,10},{9,13},{10,... | collective-permute-start | bytes 147464 | tf_op jit(solution)/shard_map/ppermute | solution.py:222
  65.2 4.6 %collective-permute-start.15 = (f32[16,128]{1,0:T(8,128)S(1)}, f32[16,128]{1,0:T(8,128)S(1)}, u32[]{:S(2)}, u32[]{:S(2)}) collective-permute-start(f32[16,128]{1,0:T(8,128)S(1)} %shard_map.40.refs_1_), channel_id=1, source_target_pairs={{0,16},{8,24},{16,0},{24,8},{1,17},{9,25},{17,1},{25,9},{2,18},{10... | collective-permute-start | bytes 24584 | tf_op jit(solution)/shard_map/ppermute | solution.py:222
  67.8 5.4 %collective-permute-start.14 = (f32[16,128]{1,0:T(8,128)S(1)}, f32[16,128]{1,0:T(8,128)S(1)}, u32[]{:S(2)}, u32[]{:S(2)}) collective-permute-start(f32[16,128]{1,0:T(8,128)S(1)} %shard_map.40.refs_1_), channel_id=1, source_target_pairs={{0,24},{8,16},{16,8},{24,0},{1,25},{9,17},{17,9},{25,1},{2,26},{10... | collective-permute-start | bytes 24584 | tf_op jit(solution)/shard_map/ppermute | solution.py:222
  69.2 4.1 %collective-permute-start.13 = (f32[16,128]{1,0:T(8,128)S(1)}, f32[16,128]{1,0:T(8,128)S(1)}, u32[]{:S(2)}, u32[]{:S(2)}) collective-permute-start(f32[16,128]{1,0:T(8,128)S(1)} %shard_map.40.refs_1_), channel_id=1, source_target_pairs={{0,8},{8,0},{16,24},{24,16},{1,9},{9,1},{17,25},{25,17},{2,10},{10... | collective-permute-start | bytes 24584 | tf_op jit(solution)/shard_map/ppermute | solution.py:222
